TPU v7x, 256 devices: a whole 4x4x8 slice. The times are simulated.
256 devices in a mesh: seq: 32 (over x, y, core), mp: 8 (over z).
Axes of the slice: x: 4, y: 4, z: 8, core: 2. Of those that a mesh axis runs over, the one named last changes fastest.
Arguments:
- tokens: bfloat16 [20480, 1024], P('seq'), may hold values from -6 to 6
- block_modality: int32 [160], P('seq'), may hold values from 0 to 2
- live_blocks: int32 [32], P('seq'), may hold values from 1 to 5, 100 in all
- mode_table: float32 [3, 1024], replicated, may hold values from -5 to 5
- latents: bfloat16 [2048, 4096], P('seq'), may hold values from -6 to 6
- w_query: bfloat16 [4096, 4096], P(None, 'mp'), may hold values from -1 to 1
- w_key: bfloat16 [1024, 4096], P(None, 'mp'), may hold values from -1 to 1
- w_value: bfloat16 [1024, 4096], P(None, 'mp'), may hold values from -0.1875 to 0.1875
- w_out: bfloat16 [4096, 4096], P('mp'), may hold values from -0.375 to 0.375
- cotangent: bfloat16 [2048, 4096], P('seq'), may hold values from -6 to 6
Outputs:
- mixed: bfloat16 [2048, 4096], P('seq')
- grad_key: float32 [1024, 4096], P('seq', 'mp')
- grad_value: float32 [1024, 4096], P('seq', 'mp')
Inputs may be any that keep to these rules, and one draw needn't show every extreme that they name: `live_blocks`: some index of seq has exactly 5 live blocks.
All inputs are finite; a program needn't handle non-finite values.
Results may differ from a plain program's by a relative error of at most 0.04.
The roundings to bfloat16 on the way count: a program that leaves them out, or rounds other values in their place, can miss the bound.
Values may be sent and summed in bfloat16 or wider, within the bound.
No kernel may reach another device: no remote copies, remote signals or barrier semaphores. Data moves between devices by JAX's collectives and lax.ppermute only.
A program may use at most 128 MiB of HBM per device.

v0:
```python
import jax
import jax.numpy as jnp
from jax import lax
from jax.sharding import PartitionSpec as P

HD = 512


masked_floor = -1e30


def normalize(values):
    mean = jnp.mean(values, axis=-1, keepdims=True)
    centred = values - mean
    spread = jnp.mean(centred * centred, axis=-1, keepdims=True)
    return centred * lax.rsqrt(spread + 1e-05)


def on_device(
    tokens,
    block_modality,
    live_blocks,
    mode_table,
    latents,
    w_query,
    w_key,
    w_value,
    w_out,
    cotangent,
):
    tok_count, in_width = tokens.shape
    modes = mode_table.shape[0]
    width = w_key.shape[1]
    heads_here = width // HD
    rows_here = latents.shape[0]
    scale = HD ** (-0.5)
    onehot = (block_modality[:, None] == jnp.arange(modes, dtype=jnp.int32)[None, :]).astype(
        jnp.float32
    )
    block_embed = jnp.dot(onehot, mode_table, precision=lax.Precision.HIGHEST)
    shaped = (
        tokens.astype(jnp.float32).reshape(tok_count // 128, 128, in_width)
        + block_embed[:, None, :]
    )
    normed = normalize(shaped.reshape(tok_count, in_width)).astype(jnp.bfloat16)
    key_rows = jnp.dot(normed, w_key, preferred_element_type=jnp.float32).astype(jnp.bfloat16)
    value_rows = jnp.dot(normed, w_value, preferred_element_type=jnp.float32).astype(jnp.bfloat16)
    lat_norm = normalize(latents.astype(jnp.float32)).astype(jnp.bfloat16)
    query_rows = jnp.dot(lat_norm, w_query, preferred_element_type=jnp.float32).astype(jnp.bfloat16)
    queries = lax.all_gather(query_rows, "seq", axis=0, tiled=True)
    lat_all = queries.shape[0]
    query_heads = queries.reshape(lat_all, heads_here, HD)
    key_heads = key_rows.reshape(tok_count, heads_here, HD)
    value_heads = value_rows.reshape(tok_count, heads_here, HD)
    scores = (
        jnp.einsum("lhd,thd->hlt", query_heads, key_heads, preferred_element_type=jnp.float32)
        * scale
    )
    live = jnp.arange(tok_count, dtype=jnp.int32) < live_blocks[0] * 128
    scores = jnp.where(live[None, None, :], scores, masked_floor)
    top = lax.pmax(jnp.max(scores, axis=2), "seq")
    weights = jnp.exp(scores - top[:, :, None])
    totals = jnp.sum(weights, axis=2).T
    partial_value = jnp.einsum(
        "hlt,thd->lhd",
        weights.astype(jnp.bfloat16),
        value_heads,
        preferred_element_type=jnp.float32,
    ).reshape(lat_all, width)
    totals_all, partial_all = lax.psum((totals, partial_value), "seq")
    first = lax.axis_index("seq") * rows_here
    row_totals = lax.dynamic_slice_in_dim(totals_all, first, rows_here, 0)
    row_sums = lax.dynamic_slice_in_dim(partial_all, first, rows_here, 0)
    attn_rows = (
        (row_sums.reshape(rows_here, heads_here, HD) / row_totals[:, :, None])
        .reshape(rows_here, width)
        .astype(jnp.bfloat16)
    )
    projected = lax.psum(jnp.dot(attn_rows, w_out, preferred_element_type=jnp.float32), "mp")
    mixed = (latents.astype(jnp.float32) + projected).astype(jnp.bfloat16)
    back = lax.dot_general(
        cotangent, w_out, (((1,), (1,)), ((), ())), preferred_element_type=jnp.float32
    ).astype(jnp.bfloat16)
    delta_rows = jnp.sum(
        (back.astype(jnp.float32) * attn_rows.astype(jnp.float32)).reshape(
            rows_here, heads_here, HD
        ),
        axis=2,
    )
    back_all = lax.all_gather(back, "seq", axis=0, tiled=True)
    delta_all, totals_back = (
        lax.all_gather(delta_rows, "seq", axis=0, tiled=True),
        lax.all_gather(row_totals, "seq", axis=0, tiled=True),
    )
    back_heads = back_all.reshape(lat_all, heads_here, HD)
    dprob = jnp.einsum("lhd,thd->hlt", back_heads, value_heads, preferred_element_type=jnp.float32)
    divisor = totals_back.T[:, :, None]
    dscore = (weights * (dprob - delta_all.T[:, :, None]) / divisor * scale).astype(jnp.bfloat16)
    normed_probs = (weights / divisor).astype(jnp.bfloat16)
    dvalue = (
        jnp.einsum("hlt,lhd->thd", normed_probs, back_heads, preferred_element_type=jnp.float32)
        .astype(jnp.bfloat16)
        .reshape(tok_count, width)
    )
    dkey = (
        jnp.einsum("hlt,lhd->thd", dscore, query_heads, preferred_element_type=jnp.float32)
        .astype(jnp.bfloat16)
        .reshape(tok_count, width)
    )
    stacked = jnp.concatenate([dkey, dvalue], axis=1)
    grads = lax.psum_scatter(
        lax.dot_general(
            normed, stacked, (((0,), (0,)), ((), ())), preferred_element_type=jnp.float32
        ),
        "seq",
        scatter_dimension=0,
        tiled=True,
    )
    return (mixed, grads[:, :width], grads[:, width:])


def solution(mesh):
    in_specs = (
        P("seq", None),
        P("seq"),
        P("seq"),
        P(),
        P("seq", None),
        P(None, "mp"),
        P(None, "mp"),
        P(None, "mp"),
        P("mp", None),
        P("seq", None),
    )
    out_specs = (P("seq", None), P("seq", "mp"), P("seq", "mp"))
    return jax.shard_map(
        on_device, mesh=mesh, in_specs=in_specs, out_specs=out_specs, check_vma=False
    )
```

profile of v0, /device:TPU:8, one launch (start us, length us, event | category | flops | bytes accessed | tf_op | source)
XLA Modules:
  0.0 511.0 jit_solution(12584950747241117346)
XLA Ops:
  7.3 1.4 convert_reduce_fusion
  8.6 1.3 fusion.16
  10.0 4.0 convolution_convert_fusion.3
  14.6 0.5 multiply_reduce_fusion
  16.6 0.8 convolution_convert_fusion.1
  17.5 47.9 %all-gather.4.cloned.1.call-done = bf16[2048,512]{1,0:T(8,128)(2,1)} async-done(((bf16[64,512]{1,0:T(8,128)(2,1)}), bf16[2048,512]{1,0:T(8,128)(2,1)}) %all-gather.4.cloned.1.call-update) | async-done | bytes 2097168 | tf_op jit(solution)/shard_map/all_gather | solution.py:50
  65.4 6.5 %fusion = (f32[2048]{0:T(1024)S(1)}, f32[2048,640]{0,1:T(8,128)}) fusion(pred[640]{0:T(1024)(128)(4,1)S(1)} %iota_compare_fusion, bf16[2048,512]{1,0:T(8,128)(2,1)} %all-gather.4.cloned.1.call-done, bf16[640,1024]{1,0:T(8,128)(2,1)} %copy-done.3, bf16[1024,512]{1,0:T(8,128)(2,1)S(1)} %copy-done), kind=kOutput, calls=%fused_computation.4 | convolution fusion | flops 2017523712 | bytes 9708160 | tf_op jit(solution)/shard_map/lhd,thd->hlt/dot_general | solution.py:56
  71.9 61.6 %pmax.7 = f32[2048]{0:T(1024)S(1)} all-reduce(f32[2048]{0:T(1024)S(1)} %get-tuple-element.9), channel_id=1, replica_groups=mesh['seq'=32,'mp'=8] {'seq'}, use_global_device_ids=true, to_apply=%region_5.6 | all-reduce | flops 2048 | bytes 16384 | tf_op jit(solution)/shard_map/pmax | solution.py:61
  133.5 6.6 %convolution_bitcast_fusion = f32[2048,512]{0,1:T(8,128)} fusion(bf16[640,512]{1,0:T(8,128)(2,1)S(1)} %convolution_convert_fusion.1, f32[2048,640]{0,1:T(8,128)} %get-tuple-element.10, f32[2048]{0:T(1024)S(1)} %pmax.7, pred[640]{0:T(1024)(128)(4,1)S(1)} %iota_compare_fusion), kind=kOutput, calls=%fused_computation.5 | convolution fusion | flops 1347420160 | bytes 10101376 | tf_op jit(solution)/shard_map/hlt,thd->lhd/dot_general | solution.py:64
  140.2 0.6 copy-done.10
  140.8 0.6 dynamic-slice
  142.1 3.6 fusion.28
  145.7 64.1 %psum.22 = f32[2048,1]{0,1:T(1,128)S(1)} all-reduce(f32[2048,1]{0,1:T(1,128)S(1)} %bitcast.50), channel_id=1, replica_groups=mesh['seq'=32,'mp'=8] {'seq'}, use_global_device_ids=true, to_apply=%region_8.9 | all-reduce | flops 2048 | bytes 16384 | tf_op jit(solution)/shard_map/psum | solution.py:70
  209.9 53.0 %all-reduce.6.cloned.1.call-done = f32[2048,512]{0,1:T(8,128)} async-done(((f32[2048,512]{0,1:T(8,128)}), f32[2048,512]{0,1:T(8,128)}) %all-reduce.6.cloned.1.call-update) | async-done | bytes 4194320 | tf_op jit(solution)/shard_map/psum | solution.py:70
  263.0 3.5 multiply_reduce_fusion.1
  266.5 0.7 copy.15
  267.3 4.2 fusion.27
  271.8 123.2 %all-reduce.2 = (f32[2048]{0:T(1024)S(1)}, f32[2048]{0:T(1024)S(1)}) all-reduce(f32[2048]{0:T(1024)S(1)} %get-tuple-element.5, f32[2048]{0:T(1024)S(1)} %dynamic-update-slice), channel_id=1, replica_groups=mesh['seq'=32,'mp'=8] {'seq'}, use_global_device_ids=true, to_apply=%add.1 | all-reduce | flops 4096 | bytes 32768
  395.0 7.8 %fusion.13 = bf16[640,512]{0,1:T(8,128)(2,1)} fusion(bf16[2048,512]{1,0:T(8,128)(2,1)S(1)} %copy-done.5, bf16[2048,512]{1,0:T(8,128)(2,1)} %all-gather.6.cloned.1.call-done, bf16[640,512]{1,0:T(8,128)(2,1)} %copy-done.11, f32[2048]{0:T(1024)S(1)} %get-tuple-element.3, f32[2048]{0:T(1024)S(1)} %get-tuple-element.4, f32[2048,640]{0,1:T(8,128)} %get-tuple-element.10, ...), kind=kOutput, calls=%fused_computation.26 | convolution fusion | flops 2695168000 | bytes 10773120 | tf_op jit(solution)/shard_map/hlt,lhd->thd/dot_general | solution.py:106
  402.8 5.4 %fusion.12 = bf16[640,512]{0,1:T(8,128)(2,1)S(1)} fusion(bf16[2048,512]{1,0:T(8,128)(2,1)} %all-gather.6.cloned.1.call-done, f32[2048]{0:T(1024)S(1)} %get-tuple-element.3, f32[2048,640]{0,1:T(8,128)} %get-tuple-element.10, f32[2048]{0:T(1024)S(1)} %pmax.7, pred[640]{0:T(1024)(128)(4,1)S(1)} %iota_compare_fusion), kind=kOutput, calls=%fused_computation.25 | convolution fusion | flops 1349058560 | bytes 8012416 | tf_op jit(solution)/shard_map/hlt,lhd->thd/dot_general | solution.py:101
  408.2 3.8 fusion.8
  412.1 2.1 fusion.18
  414.2 88.7 %reduce-scatter.2.cloned.1.call-done = f32[32,1024]{1,0:T(8,128)} async-done(((f32[1024,1024]{1,0:T(8,128)}), f32[32,1024]{1,0:T(8,128)}) %reduce-scatter.2.cloned.1.call-update) | async-done | bytes 131088 | tf_op jit(solution)/shard_map/reduce_scatter | solution.py:111
  502.9 1.5 fusion.30
  (49 shorter events, 2.2 us)
Async XLA Ops:
  7.2 58.3 %copy-start = (bf16[1024,512]{1,0:T(8,128)(2,1)S(1)}, bf16[1024,512]{1,0:T(8,128)(2,1)}, u32[]{:S(2)}) copy-start(bf16[1024,512]{1,0:T(8,128)(2,1)} %param.16) | copy-start | bytes 3145732
  7.2 6.9 %copy-start.8 = (f32[3,1024]{1,0:T(4,128)S(1)}, f32[3,1024]{1,0:T(4,128)}, u32[]{:S(2)}) copy-start(f32[3,1024]{1,0:T(4,128)} %param.13) | copy-start | bytes 36868
  7.2 6.9 %copy-start.9 = (s32[5]{0:T(128)S(1)}, s32[5]{0:T(128)}, u32[]{:S(2)}) copy-start(s32[5]{0:T(128)} %param.11) | copy-start | bytes 64
  7.2 7.1 %copy-start.1 = (bf16[640,1024]{1,0:T(8,128)(2,1)S(1)}, bf16[640,1024]{1,0:T(8,128)(2,1)}, u32[]{:S(2)}) copy-start(bf16[640,1024]{1,0:T(8,128)(2,1)} %param.10) | copy-start | bytes 3932164
  7.2 58.2 %all-gather.4.cloned.1.call-start = ((), (), s32[]{:S(2)}) async-start(), calls=%async_computation.1 | async-start | bytes 2162688 | tf_op jit(solution)/shard_map/all_gather | solution.py:50
  10.0 6.6 %copy-start.6 = (bf16[1024,512]{1,0:T(8,128)(2,1)S(1)}, bf16[1024,512]{1,0:T(8,128)(2,1)}, u32[]{:S(2)}) copy-start(bf16[1024,512]{1,0:T(8,128)(2,1)} %param.17) | copy-start | bytes 3145732
  14.0 249.0 %all-reduce.6.cloned.1.call-start = ((), (), s32[]{:S(2)}) async-start(), calls=%async_computation.2 | async-start | bytes 8388608 | tf_op jit(solution)/shard_map/psum | solution.py:70
  15.6 1.1 copy-start.3
  17.5 116.0 %copy-start.11 = (bf16[640,512]{1,0:T(8,128)(2,1)}, bf16[640,512]{1,0:T(8,128)(2,1)S(1)}, u32[]{:S(2)}) copy-start(bf16[640,512]{1,0:T(8,128)(2,1)S(1)} %convolution_convert_fusion.1) | copy-start | bytes 1966084
  140.2 0.7 copy-start.10
  140.2 122.8 %copy-start.7 = (bf16[64,4096]{1,0:T(8,128)(2,1)S(1)}, bf16[64,4096]{1,0:T(8,128)(2,1)}, u32[]{:S(2)}) copy-start(bf16[64,4096]{1,0:T(8,128)(2,1)} %param.19) | copy-start | bytes 1572868
  140.2 254.8 %all-gather.6.cloned.1.call-start = ((), (), s32[]{:S(2)}) async-start(), calls=%async_computation.4 | async-start | bytes 2162688 | tf_op jit(solution)/shard_map/all_gather | solution.py:90
  266.4 128.6 %copy-start.5 = (bf16[2048,512]{1,0:T(8,128)(2,1)S(1)}, bf16[2048,512]{1,0:T(8,128)(2,1)}, u32[]{:S(2)}) copy-start(bf16[2048,512]{1,0:T(8,128)(2,1)} %all-gather.4.cloned.1.call-done) | copy-start | bytes 6291460
  267.2 144.8 %all-reduce.8.cloned.1.call-start = ((), (), s32[]{:S(2)}) async-start(), calls=%async_computation.3 | async-start | bytes 2097152 | tf_op jit(solution)/shard_map/psum | solution.py:79
  271.5 231.4 %reduce-scatter.2.cloned.1.call-start = ((), (), s32[]{:S(2)}) async-start(), calls=%async_computation.5 | async-start | bytes 4325376 | tf_op jit(solution)/shard_map/reduce_scatter | solution.py:111
  402.8 5.4 %copy-start.4 = (bf16[640,1024]{1,0:T(8,128)(2,1)S(1)}, bf16[640,1024]{1,0:T(8,128)(2,1)}, u32[]{:S(2)}) copy-start(bf16[640,1024]{1,0:T(8,128)(2,1)} %copy-done.3) | copy-start | bytes 3932164
  402.8 5.4 %copy-start.12 = (bf16[640,512]{0,1:T(8,128)(2,1)S(1)}, bf16[640,512]{0,1:T(8,128)(2,1)}, u32[]{:S(2)}) copy-start(bf16[640,512]{0,1:T(8,128)(2,1)} %fusion.13) | copy-start | bytes 1966084
  408.2 3.8 copy-start.2
Sparse Core Ops, SparseCore 0:
  14.1 51.2 all-gather.3
  140.3 122.6 all-reduce.5
  267.3 48.9 all-gather.5
  318.5 75.8 all-reduce.7
  412.2 90.6 reduce-scatter.1
where the time goes:
time: 511 us
  blocking collectives  249 us (49%)
  waiting for transfers between devices  190 us (37%)
  matrix products  42.8 us (8%)
  between operations  15.3 us (3%)
  other arithmetic  9.72 us (2%)
    unnamed x1, blocking collectives  123 us
    reduce_scatter x1, waiting for transfers between devices, on_device(): lax.psum_scatter(lax.dot_general(normed, stacked, (((0,), (0,)), ((), ())...  88.7 us
    psum x1, blocking collectives, on_device(): totals_all, partial_all = lax.psum((totals, partial_value), 'seq')  64.1 us
    pmax x1, blocking collectives, on_device(): top = lax.pmax(jnp.max(scores, axis=2), 'seq')  61.6 us
    psum x1, waiting for transfers between devices, on_device(): totals_all, partial_all = lax.psum((totals, partial_value), 'seq')  53 us
    all_gather x1, waiting for transfers between devices, on_device(): queries = lax.all_gather(query_rows, 'seq', axis=0, tiled=True)  47.9 us
  transfers between devices with their start and end apart: 5, of which 3 were waited for; matrix products, arithmetic and copies ran while one was open for 6% of the time, Pallas kernels for 0%

commit v1 on v0

v1 whole, which is shorter than its diff:
```python
import jax
import jax.numpy as jnp
from jax import lax
from jax.sharding import Mesh, PartitionSpec as P

HD = 512
SCALE = HD ** (-0.5)
FLOOR = -1e30
XY = ("x", "y")
SEQ = ("x", "y", "core")
f32 = jnp.float32
bf16 = jnp.bfloat16


def normalize(values):
    mean = jnp.mean(values, axis=-1, keepdims=True)
    centred = values - mean
    spread = jnp.mean(centred * centred, axis=-1, keepdims=True)
    return centred * lax.rsqrt(spread + 1e-05)


def spread_out(block, axes, count):
    return lax.all_to_all(
        jnp.broadcast_to(block[None], (count,) + block.shape), axes, 0, 0, tiled=True
    )


def on_device(
    tokens,
    block_modality,
    live_blocks,
    mode_table,
    latents,
    w_query,
    w_key,
    w_value,
    w_out,
    cotangent,
    *,
    chips,
    heads,
):
    tok_count, in_width = tokens.shape
    modes = mode_table.shape[0]
    width = w_key.shape[1]
    rows_here, lat_width = latents.shape
    lat_half = chips * rows_here
    swap = [(0, 1), (1, 0)]

    lat_norm = normalize(latents.astype(f32)).astype(bf16)
    query_rows = jnp.dot(lat_norm, w_query, preferred_element_type=f32).astype(bf16)
    back_rows = lax.dot_general(
        cotangent, w_out, (((1,), (1,)), ((), ())), preferred_element_type=f32
    ).astype(bf16)
    both = spread_out(jnp.concatenate([query_rows, back_rows], axis=1), XY, chips)
    both = both.reshape(lat_half, 2 * width)
    queries, back = both[:, :width], both[:, width:]

    onehot = (block_modality[:, None] == jnp.arange(modes, dtype=jnp.int32)[None, :]).astype(f32)
    block_embed = jnp.dot(onehot, mode_table, precision=lax.Precision.HIGHEST)
    shaped = tokens.astype(f32).reshape(tok_count // 128, 128, in_width) + block_embed[:, None, :]
    normed_own = normalize(shaped.reshape(tok_count, in_width)).astype(bf16)
    normed_other = lax.ppermute(normed_own, "core", swap)
    live_other = lax.ppermute(live_blocks, "core", swap)
    normed = jnp.concatenate([normed_own, normed_other], axis=0)
    place = jnp.arange(tok_count, dtype=jnp.int32)
    live = jnp.concatenate([place < live_blocks[0] * 128, place < live_other[0] * 128])
    keys = jnp.dot(normed, w_key, preferred_element_type=f32).astype(bf16)
    values = jnp.dot(normed, w_value, preferred_element_type=f32).astype(bf16)

    nt = (((1,), (1,)), ((), ()))
    tn = (((0,), (0,)), ((), ()))
    scores = lax.dot_general(queries, keys, nt, preferred_element_type=f32) * SCALE
    scores = jnp.where(live[None, :], scores, FLOOR)
    top = jnp.max(scores, axis=1)
    weights = jnp.exp(scores - top[:, None])
    total = jnp.sum(weights, axis=1)
    dprob = lax.dot_general(back, values, nt, preferred_element_type=f32)
    cross = jnp.sum(weights * dprob, axis=1)

    stats = spread_out(jnp.stack([top, total, cross]), XY, chips)
    tops, totals, crosses = stats[:, 0], stats[:, 1], stats[:, 2]
    top_all = jnp.max(tops, axis=0)
    factor = jnp.exp(tops - top_all)
    total_all = jnp.sum(factor * totals, axis=0)
    delta = jnp.sum(factor * crosses, axis=0) / total_all
    gain = jnp.exp(top - top_all) / total_all

    partial = jnp.dot(weights.astype(bf16), values, preferred_element_type=f32).astype(bf16)
    partials = lax.all_to_all(partial.reshape(chips, rows_here, width), XY, 0, 0, tiled=True)
    chip = lax.axis_index(XY)
    mine = lax.dynamic_slice_in_dim(factor, chip * rows_here, rows_here, 1)
    mine_total = lax.dynamic_slice_in_dim(total_all, chip * rows_here, rows_here, 0)
    attn_rows = (
        jnp.sum(partials.astype(f32) * mine[:, :, None], axis=0) / mine_total[:, None]
    ).astype(bf16)
    projected = jnp.dot(attn_rows, w_out, preferred_element_type=f32).astype(bf16)
    share = rows_here // heads
    pieces = lax.all_to_all(projected.reshape(heads, share, lat_width), "mp", 0, 0, tiled=True)
    head = lax.axis_index("mp")
    lat_share = lax.dynamic_slice_in_dim(latents, head * share, share, 0)
    mixed_share = (lat_share.astype(f32) + jnp.sum(pieces.astype(f32), axis=0)).astype(bf16)
    mixed = spread_out(mixed_share, "mp", heads).reshape(rows_here, lat_width)

    scaled = weights * gain[:, None]
    probs = scaled.astype(bf16)
    dscore = (scaled * (dprob - delta[:, None]) * SCALE).astype(bf16)
    dvalue = lax.dot_general(probs, back, tn, preferred_element_type=f32).astype(bf16)
    dkey = lax.dot_general(dscore, queries, tn, preferred_element_type=f32).astype(bf16)
    stacked = jnp.concatenate([dkey, dvalue], axis=1)
    grads = lax.dot_general(normed, stacked, tn, preferred_element_type=f32).astype(bf16)
    grads = grads.reshape(chips, 2, in_width // (2 * chips), 2 * width)
    core = lax.axis_index("core")
    keep = lax.dynamic_index_in_dim(grads, core, 1, keepdims=False)
    give = lax.dynamic_index_in_dim(grads, 1 - core, 1, keepdims=False)
    took = lax.ppermute(give, "core", swap)
    chip_grads = (keep.astype(f32) + took.astype(f32)).astype(bf16)
    parts = lax.all_to_all(chip_grads, XY, 0, 0, tiled=True)
    out = jnp.sum(parts.astype(f32), axis=0)
    return mixed, out[:, :width], out[:, width:]


def solution(mesh):
    seq, heads = mesh.devices.shape
    side = 4
    fine = Mesh(mesh.devices.reshape(seq // (2 * side), side, 2, heads), SEQ + ("mp",))

    def body(*args):
        return on_device(*args, chips=seq // 2, heads=heads)

    in_specs = (
        P(SEQ, None),
        P(SEQ),
        P(SEQ),
        P(),
        P(SEQ, None),
        P(None, "mp"),
        P(None, "mp"),
        P(None, "mp"),
        P("mp", None),
        P(SEQ, None),
    )
    out_specs = (P(SEQ, None), P(SEQ, "mp"), P(SEQ, "mp"))
    return jax.shard_map(
        body, mesh=fine, in_specs=in_specs, out_specs=out_specs, check_vma=False
    )
```

time: 511 us -> 171 us (0.33)
  blocking collectives: 249 us -> 0 us
  waiting for transfers between devices: 190 us -> 67.2 us
  starting transfers between devices: 0.21 us -> 37.5 us
  between operations: 15.3 us -> 2.2 us
    unnamed x1 -> x0, blocking collectives: 123 us -> none
    reduce_scatter x1 -> x0, waiting for transfers between devices: 88.7 us -> none  [on_device(): lax.psum_scatter(lax.dot_general(normed, stacked, (((0,), (0,)), ((), ())...]
    all_to_all x0 -> x6, waiting for transfers between devices: none -> 65 us  [the longest x3 35.2 us: spread_out(): lax.all_to_all(jnp.broadcast_to(block[None], (count,) + block.shape), axe...]
    psum x1 -> x0, blocking collectives: 64.1 us -> none  [on_device(): totals_all, partial_all = lax.psum((totals, partial_value), 'seq')]
    pmax x1 -> x0, blocking collectives: 61.6 us -> none  [on_device(): top = lax.pmax(jnp.max(scores, axis=2), 'seq')]
    psum x2 -> x0, waiting for transfers between devices: 53.1 us -> none  [the longest x1 53 us: on_device(): totals_all, partial_all = lax.psum((totals, partial_value), 'seq')]
    all_gather x2 -> x0, waiting for transfers between devices: 47.9 us -> none  [the longest x1 47.9 us: on_device(): queries = lax.all_gather(query_rows, 'seq', axis=0, tiled=True)]
    all_to_all x0 -> x6, starting transfers between devices: none -> 37 us  [the longest x3 16 us: spread_out(): lax.all_to_all(jnp.broadcast_to(block[None], (count,) + block.shape), axe...]
  transfers between devices with their start and end apart: 5 -> 9, of which waited for: 3 -> 6; matrix products, arithmetic and copies ran while one was open for 6% -> 22% of each run, Pallas kernels for 0% -> 0%
where the time goes in v1:
time: 171 us; the launch traced here: 170 us
  waiting for transfers between devices  67.2 us (39%)
  matrix products  46.3 us (27%)
  starting transfers between devices  37.5 us (22%)
  other arithmetic  10.6 us (6%)
  local copies, waits for them, and re-layouts  6.52 us (4%)
  between operations  2.2 us (1%)
    all_to_all x3, waiting for transfers between devices, spread_out(): lax.all_to_all(jnp.broadcast_to(block[None], (count,) + block.shape), axe...  35.2 us
    all_to_all x3, starting transfers between devices, spread_out(): lax.all_to_all(jnp.broadcast_to(block[None], (count,) + block.shape), axe...  16 us
    all_to_all x1, waiting for transfers between devices, on_device(): lax.all_to_all(projected.reshape(heads, share, lat_width), 'mp', 0, 0, ti...  15.2 us
    all_to_all x1, waiting for transfers between devices, on_device(): parts = lax.all_to_all(chip_grads, XY, 0, 0, tiled=True)  14.6 us
    all_to_all x1, starting transfers between devices, on_device(): lax.all_to_all(projected.reshape(heads, share, lat_width), 'mp', 0, 0, ti...  8.46 us
    dot_general x1, matrix products, on_device(): lax.dot_general(queries, keys, nt, preferred_element_type=f32) * SCALE  7.46 us
    all_to_all x1, starting transfers between devices, on_device(): parts = lax.all_to_all(chip_grads, XY, 0, 0, tiled=True)  7.22 us
    dot_general x1, matrix products, on_device(): dprob = lax.dot_general(back, values, nt, preferred_element_type=f32)  6.96 us
  transfers between devices with their start and end apart: 9, of which 6 were waited for; matrix products, arithmetic and copies ran while one was open for 22% of the time, Pallas kernels for 0%

profile of v1, /device:TPU:8, one launch (start us, length us, event | category | flops | bytes accessed | tf_op | source)
XLA Modules:
  0.0 170.3 jit_solution(12438706155879316657)
XLA Ops:
  3.5 3.3 %convolution_convert_fusion.6 = bf16[64,512]{1,0:T(8,128)(2,1)S(1)} fusion(bf16[4096,512]{1,0:T(8,128)(2,1)} %param.15, bf16[64,4096]{1,0:T(8,128)(2,1)} %param.14, f32[64]{0:T(128)S(1)} %add_rsqrt_fusion.1, f32[64]{0:T(128)S(1)} %broadcast_multiply_fusion.1), kind=kOutput, calls=%fused_computation.42 | convolution fusion | flops 269516800 | bytes 4784640 | tf_op jit(solution)/shard_map/dot_general | solution.py:51
  8.2 1.6 broadcast_in_dim.15
  9.8 7.5 %all-to-all-start = ((bf16[16,64,1024]{2,1,0:T(8,128)(2,1)}), bf16[16,64,1024]{2,1,0:T(8,128)(2,1)}, u32[]{:S(2)}, u32[]{:S(2)}) async-start(bf16[16,64,1024]{2,1,0:T(8,128)(2,1)} %broadcast_in_dim.15), calls=%async_computation | async-start | bytes 4194304 | tf_op jit(solution)/shard_map/all_to_all | solution.py:23
  18.5 1.6 multiply_convert_fusion.4
  21.2 2.2 %collective-permute-done = s32[1]{0:T(128)} collective-permute-done((s32[1]{0:T(128)}, s32[1]{0:T(128)}, u32[]{:S(2)}, u32[]{:S(2)}) %collective-permute-start) | collective-permute-done | bytes 36 | tf_op jit(solution)/shard_map/ppermute | solution.py:64
  24.1 3.2 %convolution_convert_fusion.3 = bf16[1280,512]{1,0:T(8,128)(2,1)S(1)} fusion(bf16[1024,512]{1,0:T(8,128)(2,1)S(1)} %copy-done.6, bf16[640,1024]{1,0:T(8,128)(2,1)} %collective-permute-done.1, bf16[640,1024]{1,0:T(8,128)(2,1)} %multiply_convert_fusion.4), kind=kOutput, calls=%fused_computation.9 | convolution fusion | flops 1348075520 | bytes 4980736 | tf_op jit(solution)/shard_map/dot_general | solution.py:69
  27.3 19.2 %all-to-all-done = bf16[16,64,1024]{2,1,0:T(8,128)(2,1)} async-done(((bf16[16,64,1024]{2,1,0:T(8,128)(2,1)}), bf16[16,64,1024]{2,1,0:T(8,128)(2,1)}, u32[]{:S(2)}, u32[]{:S(2)}) %all-to-all-start) | async-done | bytes 2097184 | tf_op jit(solution)/shard_map/all_to_all | solution.py:23
  46.5 7.5 %fusion.54 = (f32[1024]{0:T(1024)S(1)}, f32[1024,1280]{1,0:T(8,128)}) fusion(bf16[1024,512]{1,0:T(8,128)(2,1)S(1)} %copy-done, bf16[640,1024]{1,0:T(8,128)(2,1)} %collective-permute-done.1, bf16[640,1024]{1,0:T(8,128)(2,1)} %multiply_convert_fusion.4, bf16[1024,1024]{1,0:T(8,128)(2,1)} %bitcast.2, pred[1280]{0:T(1024)(128)(4,1)S(1)} %pad_add_fusion), kind=kOutput, calls=%fused_computation.87 | convolution fusion | flops 2694183936 | bytes 9966848 | tf_op jit(solution)/shard_map/dot_general | solution.py:73
  53.9 7.0 %fusion.1 = (f32[1024]{0:T(1024)S(1)}, f32[1024]{0:T(1024)S(1)}, f32[1024,1280]{1,0:T(8,128)}) fusion(f32[1024,1280]{1,0:T(8,128)} %get-tuple-element.17, f32[1024]{0:T(1024)S(1)} %get-tuple-element.16, bf16[1280,512]{1,0:T(8,128)(2,1)S(1)} %convolution_convert_fusion.3, bf16[1024,1024]{1,0:T(8,128)(2,1)} %bitcast.2), kind=kOutput, calls=%fused_computation.11 | convolution fusion | flops 1347418112 | bytes 12857344 | tf_op jit(solution)/shard_map/dot_general | solution.py:78
  61.7 5.0 %all-to-all-start.2 = ((f32[16,3,1024]{2,1,0:T(4,128)}), f32[16,3,1024]{2,1,0:T(4,128)S(1)}, u32[]{:S(2)}, u32[]{:S(2)}) async-start(f32[16,3,1024]{2,1,0:T(4,128)} %broadcast_in_dim.21), calls=%async_computation.2 | async-start | bytes 524288 | tf_op jit(solution)/shard_map/all_to_all | solution.py:23
  66.7 5.1 %fusion.22 = bf16[1024,512]{1,0:T(8,128)(2,1)} fusion(bf16[1280,512]{1,0:T(8,128)(2,1)S(1)} %convolution_convert_fusion.3, f32[1024,1280]{1,0:T(8,128)} %get-tuple-element.17, f32[1024]{0:T(1024)S(1)} %get-tuple-element.16), kind=kOutput, calls=%fused_computation.36 | convolution fusion | flops 1345323008 | bytes 7606272 | tf_op jit(solution)/shard_map/dot_general | solution.py:89
  71.7 1.9 %all-to-all-done.2 = f32[16,3,1024]{2,1,0:T(4,128)S(1)} async-done(((f32[16,3,1024]{2,1,0:T(4,128)}), f32[16,3,1024]{2,1,0:T(4,128)S(1)}, u32[]{:S(2)}, u32[]{:S(2)}) %all-to-all-start.2) | async-done | bytes 196640 | tf_op jit(solution)/shard_map/all_to_all | solution.py:23
  73.6 5.3 %all-to-all-start.1 = ((bf16[16,64,512]{2,1,0:T(8,128)(2,1)}), bf16[16,64,512]{2,1,0:T(8,128)(2,1)S(1)}, u32[]{:S(2)}, u32[]{:S(2)}) async-start(bf16[16,64,512]{2,1,0:T(8,128)(2,1)} %bitcast.4), calls=%async_computation.1 | async-start | bytes 2097152 | tf_op jit(solution)/shard_map/all_to_all | solution.py:90
  79.2 6.6 %convolution_convert_fusion.2 = bf16[1280,512]{1,0:T(8,128)(2,1)S(1)} fusion(f32[1024,1280]{1,0:T(8,128)} %get-tuple-element.18, f32[1024,1280]{1,0:T(8,128)} %get-tuple-element.17, f32[1024]{0:T(1024)S(1)} %get-tuple-element.14, f32[1024]{0:T(1024)S(1)} %get-tuple-element.15, f32[1024]{0:T(1024)S(1)} %get-tuple-element.16, bf16[1024,1024]{1,0:T(8,128)(2,1)} %bitcast.2), kind=kOutput, calls=%fused_computation.8 | convolution fusion | flops 1350696960 | bytes 12857344 | tf_op jit(solution)/shard_map/dot_general | solution.py:109
  85.8 3.2 %convolution_convert_fusion.1 = bf16[1280,512]{1,0:T(8,128)(2,1)S(1)} fusion(f32[1024,1280]{1,0:T(8,128)S(1)} %bitcast.53, f32[1024]{0:T(1024)S(1)} %get-tuple-element.15, f32[1024]{0:T(1024)S(1)} %get-tuple-element.16, bf16[1024,1024]{1,0:T(8,128)(2,1)} %bitcast.2), kind=kOutput, calls=%fused_computation.7 | convolution fusion | flops 1346764800 | bytes 7610368 | tf_op jit(solution)/shard_map/dot_general | solution.py:108
  89.1 5.0 %fusion.19 = bf16[1024,1024]{1,0:T(8,128)(2,1)S(1)} fusion(bf16[1280,512]{1,0:T(8,128)(2,1)S(1)} %convolution_convert_fusion.1, bf16[1280,512]{1,0:T(8,128)(2,1)S(1)} %convolution_convert_fusion.2, bf16[640,1024]{1,0:T(8,128)(2,1)} %collective-permute-done.1, bf16[640,1024]{1,0:T(8,128)(2,1)} %multiply_convert_fusion.4), kind=kOutput, calls=%fused_computation.35 | convolution fusion | flops 2695888896 | bytes 7340032 | tf_op jit(solution)/shard_map/dot_general | solution.py:111
  96.1 4.0 %fusion = bf16[8,8,4096]{2,1,0:T(8,128)(2,1)} fusion(bf16[512,4096]{1,0:T(8,128)(2,1)} %param.18, f32[64,512]{1,0:T(8,128)S(1)} %multiply_reduce_fusion.2, f32[64]{0:T(128)S(1)} %dynamic_slice.18), kind=kOutput, calls=%fused_computation.6 | convolution fusion | flops 268763136 | bytes 4849920 | tf_op jit(solution)/shard_map/dot_general | solution.py:97
  100.1 8.5 %all-to-all-start.3 = ((bf16[8,8,4096]{2,1,0:T(8,128)(2,1)}), bf16[8,8,4096]{2,1,0:T(8,128)(2,1)}, u32[]{:S(2)}, u32[]{:S(2)}) async-start(bf16[8,8,4096]{2,1,0:T(8,128)(2,1)} %fusion), calls=%async_computation.3 | async-start | bytes 1048576 | tf_op jit(solution)/shard_map/all_to_all | solution.py:99
  108.6 2.6 %fusion.18 = bf16[16,32,1024]{2,1,0:T(8,128)(2,1)} fusion(bf16[16,32,1024]{2,1,0:T(8,128)(2,1)} %collective-permute-done.2, bf16[16,2,32,1024]{3,2,1,0:T(8,128)(2,1)S(1)} %bitcast.55, s32[]{:T(128)S(6)} %select_n.21), kind=kLoop, calls=%fused_computation.32 | loop fusion | flops 2097152 | bytes 3145732 | tf_op jit(solution)/shard_map/convert_element_type | solution.py:117
  111.2 15.2 %all-to-all-done.3 = bf16[8,8,4096]{2,1,0:T(8,128)(2,1)} async-done(((bf16[8,8,4096]{2,1,0:T(8,128)(2,1)}), bf16[8,8,4096]{2,1,0:T(8,128)(2,1)}, u32[]{:S(2)}, u32[]{:S(2)}) %all-to-all-start.3) | async-done | bytes 524320 | tf_op jit(solution)/shard_map/all_to_all | solution.py:99
  126.4 7.2 %all-to-all-start.5 = ((bf16[16,32,1024]{2,1,0:T(8,128)(2,1)}), bf16[16,32,1024]{2,1,0:T(8,128)(2,1)S(1)}, u32[]{:S(2)}, u32[]{:S(2)}) async-start(bf16[16,32,1024]{2,1,0:T(8,128)(2,1)} %fusion.18), calls=%async_computation.5 | async-start | bytes 2097152 | tf_op jit(solution)/shard_map/all_to_all | solution.py:118
  135.6 14.6 %all-to-all-done.5 = bf16[16,32,1024]{2,1,0:T(8,128)(2,1)S(1)} async-done(((bf16[16,32,1024]{2,1,0:T(8,128)(2,1)}), bf16[16,32,1024]{2,1,0:T(8,128)(2,1)S(1)}, u32[]{:S(2)}, u32[]{:S(2)}) %all-to-all-start.5) | async-done | bytes 1048608 | tf_op jit(solution)/shard_map/all_to_all | solution.py:118
  151.1 3.5 %all-to-all-start.4 = ((bf16[8,8,4096]{2,1,0:T(8,128)(2,1)}), bf16[8,8,4096]{2,1,0:T(8,128)(2,1)S(1)}, u32[]{:S(2)}, u32[]{:S(2)}) async-start(bf16[8,8,4096]{2,1,0:T(8,128)(2,1)} %broadcast_in_dim.22), calls=%async_computation.4 | async-start | bytes 1048576 | tf_op jit(solution)/shard_map/all_to_all | solution.py:23
  155.4 14.1 %all-to-all-done.4 = bf16[8,8,4096]{2,1,0:T(8,128)(2,1)S(1)} async-done(((bf16[8,8,4096]{2,1,0:T(8,128)(2,1)}), bf16[8,8,4096]{2,1,0:T(8,128)(2,1)S(1)}, u32[]{:S(2)}, u32[]{:S(2)}) %all-to-all-start.4) | async-done | bytes 524320 | tf_op jit(solution)/shard_map/all_to_all | solution.py:23
  (57 shorter events, 13.4 us)
Async XLA Ops:
  0.6 45.9 %copy-start = (bf16[1024,512]{1,0:T(8,128)(2,1)S(1)}, bf16[1024,512]{1,0:T(8,128)(2,1)}, u32[]{:S(2)}) copy-start(bf16[1024,512]{1,0:T(8,128)(2,1)} %param.16) | copy-start | bytes 3145732
  2.0 4.8 %copy-start.1 = (bf16[512,4096]{1,0:T(8,128)(2,1)S(1)}, bf16[512,4096]{1,0:T(8,128)(2,1)}, u32[]{:S(2)}) copy-start(bf16[512,4096]{1,0:T(8,128)(2,1)} %param.18) | copy-start | bytes 12582916
  2.0 4.8 %copy-start.5 = (bf16[64,4096]{1,0:T(8,128)(2,1)S(1)}, bf16[64,4096]{1,0:T(8,128)(2,1)}, u32[]{:S(2)}) copy-start(bf16[64,4096]{1,0:T(8,128)(2,1)} %param.19) | copy-start | bytes 1572868
  9.8 7.5 %copy-start.7 = (f32[3,1024]{1,0:T(4,128)S(1)}, f32[3,1024]{1,0:T(4,128)}, u32[]{:S(2)}) copy-start(f32[3,1024]{1,0:T(4,128)} %param.13) | copy-start | bytes 36868
  9.8 7.5 %copy-start.8 = (s32[5]{0:T(128)S(1)}, s32[5]{0:T(128)}, u32[]{:S(2)}) copy-start(s32[5]{0:T(128)} %param.11) | copy-start | bytes 64
  9.8 7.7 %copy-start.2 = (bf16[640,1024]{1,0:T(8,128)(2,1)S(1)}, bf16[640,1024]{1,0:T(8,128)(2,1)}, u32[]{:S(2)}) copy-start(bf16[640,1024]{1,0:T(8,128)(2,1)} %param.10) | copy-start | bytes 3932164
  9.8 36.6 %all-to-all-start = ((bf16[16,64,1024]{2,1,0:T(8,128)(2,1)}), bf16[16,64,1024]{2,1,0:T(8,128)(2,1)}, u32[]{:S(2)}, u32[]{:S(2)}) async-start(bf16[16,64,1024]{2,1,0:T(8,128)(2,1)} %broadcast_in_dim.15), calls=%async_computation | async-start | bytes 4194304 | tf_op jit(solution)/shard_map/all_to_all | solution.py:23
  17.6 6.5 %copy-start.6 = (bf16[1024,512]{1,0:T(8,128)(2,1)S(1)}, bf16[1024,512]{1,0:T(8,128)(2,1)}, u32[]{:S(2)}) copy-start(bf16[1024,512]{1,0:T(8,128)(2,1)} %param.17) | copy-start | bytes 3145732
  20.0 4.0 %collective-permute-start.1 = (bf16[640,1024]{1,0:T(8,128)(2,1)}, bf16[640,1024]{1,0:T(8,128)(2,1)}, u32[]{:S(2)}, u32[]{:S(2)}) collective-permute-start(bf16[640,1024]{1,0:T(8,128)(2,1)} %multiply_convert_fusion.4), channel_id=1, source_target_pairs={{0,8},{8,0},{1,9},{9,1},{2,10},{10,2},{3,11},{11,3},{4,12},{12,4},... | collective-permute-start | bytes 3932168 | tf_op jit(solution)/shard_map/ppermute | solution.py:63
  20.0 3.4 %collective-permute-start = (s32[1]{0:T(128)}, s32[1]{0:T(128)}, u32[]{:S(2)}, u32[]{:S(2)}) collective-permute-start(s32[1]{0:T(128)} %param.12), channel_id=1, source_target_pairs={{0,8},{8,0},{1,9},{9,1},{2,10},{10,2},{3,11},{11,3},{4,12},{12,4},... | collective-permute-start | bytes 20 | tf_op jit(solution)/shard_map/ppermute | solution.py:64
  61.7 12.0 %all-to-all-start.2 = ((f32[16,3,1024]{2,1,0:T(4,128)}), f32[16,3,1024]{2,1,0:T(4,128)S(1)}, u32[]{:S(2)}, u32[]{:S(2)}) async-start(f32[16,3,1024]{2,1,0:T(4,128)} %broadcast_in_dim.21), calls=%async_computation.2 | async-start | bytes 524288 | tf_op jit(solution)/shard_map/all_to_all | solution.py:23
  73.6 22.2 %all-to-all-start.1 = ((bf16[16,64,512]{2,1,0:T(8,128)(2,1)}), bf16[16,64,512]{2,1,0:T(8,128)(2,1)S(1)}, u32[]{:S(2)}, u32[]{:S(2)}) async-start(bf16[16,64,512]{2,1,0:T(8,128)(2,1)} %bitcast.4), calls=%async_computation.1 | async-start | bytes 2097152 | tf_op jit(solution)/shard_map/all_to_all | solution.py:90
  79.0 6.9 %slice-start = ((s8[5242880]{0:T(1024)(128)(4,1)}), s8[4194304]{0:T(1024)(128)(4,1)S(1)}, s32[]{:S(2)}) async-start(s8[5242880]{0:T(1024)(128)(4,1)} %bitcast.52), calls=%async_computation.6 | async-start | bytes 8388608
  79.2 6.6 %slice-start.1 = ((s8[5242880]{0:T(1024)(128)(4,1)}), s8[1048576]{0:T(1024)(128)(4,1)S(1)}, s32[]{:S(2)}) async-start(s8[5242880]{0:T(1024)(128)(4,1)} %bitcast.52), calls=%async_computation.7 | async-start | bytes 2097152
  94.1 1.7 copy-start.3
  95.3 13.3 %collective-permute-start.2 = (bf16[16,32,1024]{2,1,0:T(8,128)(2,1)}, bf16[16,32,1024]{2,1,0:T(8,128)(2,1)}, u32[]{:S(2)}, u32[]{:S(2)}) collective-permute-start(bf16[16,32,1024]{2,1,0:T(8,128)(2,1)} %dynamic-slice_bitcast_fusion), channel_id=1, source_target_pairs={{0,8},{8,0},{1,9},{9,1},{2,10},{10,2},{3,11},{11,3},{4,12},{12,4},... | collective-permute-start | bytes 3145736 | tf_op jit(solution)/shard_map/ppermute | solution.py:116
  96.1 12.5 %copy-start.4 = (bf16[1024,1024]{1,0:T(8,128)(2,1)S(1)}, bf16[1024,1024]{1,0:T(8,128)(2,1)}, u32[]{:S(2)}) copy-start(bf16[1024,1024]{1,0:T(8,128)(2,1)} %copy-done.3) | copy-start | bytes 6291460
  100.1 26.2 %all-to-all-start.3 = ((bf16[8,8,4096]{2,1,0:T(8,128)(2,1)}), bf16[8,8,4096]{2,1,0:T(8,128)(2,1)}, u32[]{:S(2)}, u32[]{:S(2)}) async-start(bf16[8,8,4096]{2,1,0:T(8,128)(2,1)} %fusion), calls=%async_computation.3 | async-start | bytes 1048576 | tf_op jit(solution)/shard_map/all_to_all | solution.py:99
  126.4 23.8 %all-to-all-start.5 = ((bf16[16,32,1024]{2,1,0:T(8,128)(2,1)}), bf16[16,32,1024]{2,1,0:T(8,128)(2,1)S(1)}, u32[]{:S(2)}, u32[]{:S(2)}) async-start(bf16[16,32,1024]{2,1,0:T(8,128)(2,1)} %fusion.18), calls=%async_computation.5 | async-start | bytes 2097152 | tf_op jit(solution)/shard_map/all_to_all | solution.py:118
  151.1 18.5 %all-to-all-start.4 = ((bf16[8,8,4096]{2,1,0:T(8,128)(2,1)}), bf16[8,8,4096]{2,1,0:T(8,128)(2,1)S(1)}, u32[]{:S(2)}, u32[]{:S(2)}) async-start(bf16[8,8,4096]{2,1,0:T(8,128)(2,1)} %broadcast_in_dim.22), calls=%async_computation.4 | async-start | bytes 1048576 | tf_op jit(solution)/shard_map/all_to_all | solution.py:23

commit v2 on v1

--- a/solution.py
+++ b/solution.py
@@ -1,6 +1,10 @@
+import functools
+
 import jax
 import jax.numpy as jnp
 from jax import lax
+from jax.experimental import pallas as pl
+from jax.experimental.pallas import tpu as pltpu
 from jax.sharding import Mesh, PartitionSpec as P
 
 HD = 512
@@ -23,6 +27,141 @@
     return lax.all_to_all(
         jnp.broadcast_to(block[None], (count,) + block.shape), axes, 0, 0, tiled=True
     )
+
+
+def dot_nn(a, b):
+    return jnp.dot(a, b, preferred_element_type=f32)
+
+
+def dot_nt(a, b):
+    return lax.dot_general(a, b, (((1,), (1,)), ((), ())), preferred_element_type=f32)
+
+
+def forward_kernel(live_ref, q_ref, b_ref, k_ref, v_ref, w_ref, d_ref, part_ref, stat_ref):
+    rows = q_ref.shape[0]
+    slots = k_ref.shape[0]
+    half = slots // 2
+    place = lax.broadcasted_iota(jnp.int32, (1, slots), 1)
+    bound = jnp.where(place < half, live_ref[0] * 128, half + live_ref[1] * 128)
+    live = place < bound
+    step = rows // 2
+    for start in range(0, rows, step):
+        here = pl.ds(start, step)
+        scores = dot_nt(q_ref[here, :], k_ref[...]) * SCALE
+        scores = jnp.where(live, scores, FLOOR)
+        top = jnp.max(scores, axis=1, keepdims=True)
+        weights = jnp.exp(scores - top)
+        total = jnp.sum(weights, axis=1, keepdims=True)
+        dprob = dot_nt(b_ref[here, :], v_ref[...])
+        cross = jnp.sum(weights * dprob, axis=1, keepdims=True)
+        rounded = weights.astype(bf16)
+        w_ref[here, :] = rounded
+        d_ref[here, :] = dprob
+        part_ref[here, :] = dot_nn(rounded, v_ref[...]).astype(bf16)
+        lane = lax.broadcasted_iota(jnp.int32, (step, 128), 1)
+        packed = jnp.where(lane == 0, top, jnp.where(lane == 1, total, cross))
+        stat_ref[:, here] = packed.T[:8]
+
+
+def forward(live, both, keys, values):
+    lat, double = both.shape
+    width = double // 2
+    slots = keys.shape[0]
+    rows = 256
+    whole = lambda i: (0, 0)
+    return pl.pallas_call(
+        forward_kernel,
+        grid=(lat // rows,),
+        in_specs=[
+            pl.BlockSpec(memory_space=pltpu.SMEM),
+            pl.BlockSpec((rows, width), lambda i: (i, 0)),
+            pl.BlockSpec((rows, width), lambda i: (i, 1)),
+            pl.BlockSpec((slots, width), whole),
+            pl.BlockSpec((slots, width), whole),
+        ],
+        out_specs=[
+            pl.BlockSpec((rows, slots), lambda i: (i, 0)),
+            pl.BlockSpec((rows, slots), lambda i: (i, 0)),
+            pl.BlockSpec((rows, width), lambda i: (i, 0)),
+            pl.BlockSpec((8, rows), lambda i: (0, i)),
+        ],
+        out_shape=[
+            jax.ShapeDtypeStruct((lat, slots), bf16),
+            jax.ShapeDtypeStruct((lat, slots), f32),
+            jax.ShapeDtypeStruct((lat, width), bf16),
+            jax.ShapeDtypeStruct((8, lat), f32),
+        ],
+        compiler_params=pltpu.CompilerParams(vmem_limit_bytes=40 << 20),
+        cost_estimate=pl.CostEstimate(
+            flops=6 * lat * slots * width,
+            bytes_accessed=6 * lat * slots + 6 * lat * width + 4 * slots * width,
+            transcendentals=lat * slots,
+        ),
+    )(live, both, both, keys, values)
+
+
+def backward_kernel(stat_ref, own_ref, t_ref, w_ref, d_ref, n_ref, out_ref, scaled, delta, grads):
+    step = pl.program_id(0)
+    lat = stat_ref.shape[2]
+    width = t_ref.shape[0] // 2
+    block = w_ref.shape[1]
+
+    @pl.when(step == 0)
+    def _():
+        tops, totals, crosses = stat_ref[:, 0, :], stat_ref[:, 1, :], stat_ref[:, 2, :]
+        top = jnp.max(tops, axis=0, keepdims=True)
+        factor = jnp.exp(tops - top)
+        total = jnp.sum(factor * totals, axis=0, keepdims=True)
+        mean = jnp.sum(factor * crosses, axis=0, keepdims=True) / total
+        delta[...] = jnp.broadcast_to(mean, (128, lat)).T
+        gain = jnp.exp(own_ref[0:1, :] - top) / total
+        scaled[:width] = (t_ref[:width].astype(f32) * (gain * SCALE)).astype(bf16)
+        scaled[width:] = (t_ref[width:].astype(f32) * gain).astype(bf16)
+
+    for part in range(0, block, 128):
+        here = pl.ds(part, 128)
+        dscore = (w_ref[:, here].astype(f32) * (d_ref[:, here] - delta[...])).astype(bf16)
+        there = pl.ds(pl.multiple_of(step * block + part, 128), 128)
+        grads[:width, there] = dot_nn(scaled[:width], dscore).astype(bf16)
+        grads[width:, there] = dot_nn(scaled[width:], w_ref[:, here]).astype(bf16)
+
+    @pl.when(step == pl.num_programs(0) - 1)
+    def _():
+        size = out_ref.shape[0] // 4
+        for row in range(0, out_ref.shape[0], size):
+            out_ref[pl.ds(row, size), :] = dot_nt(n_ref[pl.ds(row, size), :], grads[...]).astype(bf16)
+
+
+def backward(stats, own, turned, weights, dprob, normed_t):
+    lat, slots = weights.shape
+    double = turned.shape[0]
+    in_width = normed_t.shape[0]
+    block = 256
+    return pl.pallas_call(
+        backward_kernel,
+        grid=(slots // block,),
+        in_specs=[
+            pl.BlockSpec(stats.shape, lambda i: (0, 0, 0)),
+            pl.BlockSpec(own.shape, lambda i: (0, 0)),
+            pl.BlockSpec(turned.shape, lambda i: (0, 0)),
+            pl.BlockSpec((lat, block), lambda i: (0, i)),
+            pl.BlockSpec((lat, block), lambda i: (0, i)),
+            pl.BlockSpec(normed_t.shape, lambda i: (0, 0)),
+        ],
+        out_specs=pl.BlockSpec((in_width, double), lambda i: (0, 0)),
+        out_shape=jax.ShapeDtypeStruct((in_width, double), bf16),
+        scratch_shapes=[
+            pltpu.VMEM((double, lat), bf16),
+            pltpu.VMEM((lat, 128), f32),
+            pltpu.VMEM((double, slots), bf16),
+        ],
+        compiler_params=pltpu.CompilerParams(vmem_limit_bytes=40 << 20),
+        cost_estimate=pl.CostEstimate(
+            flops=2 * slots * double * (lat + in_width),
+            bytes_accessed=6 * lat * slots + 2 * in_width * (slots + double) + 2 * double * lat,
+            transcendentals=lat,
+        ),
+    )(stats, own, turned, weights, dprob, normed_t)
 
 
 def on_device(
@@ -54,7 +193,6 @@
     ).astype(bf16)
     both = spread_out(jnp.concatenate([query_rows, back_rows], axis=1), XY, chips)
     both = both.reshape(lat_half, 2 * width)
-    queries, back = both[:, :width], both[:, width:]
 
     onehot = (block_modality[:, None] == jnp.arange(modes, dtype=jnp.int32)[None, :]).astype(f32)
     block_embed = jnp.dot(onehot, mode_table, precision=lax.Precision.HIGHEST)
@@ -63,30 +201,21 @@
     normed_other = lax.ppermute(normed_own, "core", swap)
     live_other = lax.ppermute(live_blocks, "core", swap)
     normed = jnp.concatenate([normed_own, normed_other], axis=0)
-    place = jnp.arange(tok_count, dtype=jnp.int32)
-    live = jnp.concatenate([place < live_blocks[0] * 128, place < live_other[0] * 128])
+    live = jnp.concatenate([live_blocks, live_other])
     keys = jnp.dot(normed, w_key, preferred_element_type=f32).astype(bf16)
     values = jnp.dot(normed, w_value, preferred_element_type=f32).astype(bf16)
 
-    nt = (((1,), (1,)), ((), ()))
-    tn = (((0,), (0,)), ((), ()))
-    scores = lax.dot_general(queries, keys, nt, preferred_element_type=f32) * SCALE
-    scores = jnp.where(live[None, :], scores, FLOOR)
-    top = jnp.max(scores, axis=1)
-    weights = jnp.exp(scores - top[:, None])
-    total = jnp.sum(weights, axis=1)
-    dprob = lax.dot_general(back, values, nt, preferred_element_type=f32)
-    cross = jnp.sum(weights * dprob, axis=1)
-
-    stats = spread_out(jnp.stack([top, total, cross]), XY, chips)
-    tops, totals, crosses = stats[:, 0], stats[:, 1], stats[:, 2]
-    top_all = jnp.max(tops, axis=0)
-    factor = jnp.exp(tops - top_all)
-    total_all = jnp.sum(factor * totals, axis=0)
-    delta = jnp.sum(factor * crosses, axis=0) / total_all
-    gain = jnp.exp(top - top_all) / total_all
-
-    partial = jnp.dot(weights.astype(bf16), values, preferred_element_type=f32).astype(bf16)
+    core = lax.axis_index("core")
+    turned_tokens = normed.T.reshape(chips, 2, in_width // (2 * chips), 2 * tok_count)
+    turned_tokens = jnp.concatenate(
+        [lax.dynamic_index_in_dim(turned_tokens, c, 1, keepdims=False) for c in (core, 1 - core)]
+    ).reshape(in_width, 2 * tok_count)
+
+    weights, dprob, partial, own = forward(live, both, keys, values)
+    stats = spread_out(own, XY, chips)
+    factor = jnp.exp(stats[:, 0] - jnp.max(stats[:, 0], axis=0))
+    total_all = jnp.sum(factor * stats[:, 1], axis=0)
+
     partials = lax.all_to_all(partial.reshape(chips, rows_here, width), XY, 0, 0, tiled=True)
     chip = lax.axis_index(XY)
     mine = lax.dynamic_slice_in_dim(factor, chip * rows_here, rows_here, 1)
@@ -102,17 +231,9 @@
     mixed_share = (lat_share.astype(f32) + jnp.sum(pieces.astype(f32), axis=0)).astype(bf16)
     mixed = spread_out(mixed_share, "mp", heads).reshape(rows_here, lat_width)
 
-    scaled = weights * gain[:, None]
-    probs = scaled.astype(bf16)
-    dscore = (scaled * (dprob - delta[:, None]) * SCALE).astype(bf16)
-    dvalue = lax.dot_general(probs, back, tn, preferred_element_type=f32).astype(bf16)
-    dkey = lax.dot_general(dscore, queries, tn, preferred_element_type=f32).astype(bf16)
-    stacked = jnp.concatenate([dkey, dvalue], axis=1)
-    grads = lax.dot_general(normed, stacked, tn, preferred_element_type=f32).astype(bf16)
-    grads = grads.reshape(chips, 2, in_width // (2 * chips), 2 * width)
-    core = lax.axis_index("core")
-    keep = lax.dynamic_index_in_dim(grads, core, 1, keepdims=False)
-    give = lax.dynamic_index_in_dim(grads, 1 - core, 1, keepdims=False)
+    grads = backward(stats, own, both.T, weights, dprob, turned_tokens)
+    grads = grads.reshape(2, chips, in_width // (2 * chips), 2 * width)
+    keep, give = grads[0], grads[1]
     took = lax.ppermute(give, "core", swap)
     chip_grads = (keep.astype(f32) + took.astype(f32)).astype(bf16)
     parts = lax.all_to_all(chip_grads, XY, 0, 0, tiled=True)

time: 171 us -> 185 us (1.082)
  matrix products: 46.3 us -> 15.9 us
  local copies, waits for them, and re-layouts: 6.52 us -> 28.6 us
  Pallas kernels: 0 us -> 21.8 us
  waiting for transfers between devices: 67.2 us -> 60.3 us
  other arithmetic: 10.6 us -> 17.1 us
    dot_general x6 -> x1, matrix products: 34.2 us -> 4.32 us  [on_device(): keys = jnp.dot(normed, w_key, preferred_element_type=f32).astype(bf16)]
    pallas_call x0 -> x2, Pallas kernels: none -> 21.8 us  [the longest x1 11.9 us: backward(): pl.pallas_call(backward_kernel, grid=(slots // block,), in_specs=[pl.Bloc...]
    unnamed x23 -> x31, local copies, waits for them, and re-layouts: 1.33 us -> 14.5 us
    all_to_all x3, waiting for transfers between devices: 35.2 us -> 28.5 us  [spread_out(): lax.all_to_all(jnp.broadcast_to(block[None], (count,) + block.shape), axe...]
    transpose x0 -> x1, local copies, waits for them, and re-layouts: none -> 4.41 us  [on_device(): normed.T.reshape(chips, 2, in_width // (2 * chips), 2 * tok_count)]
    transpose x0 -> x1, other arithmetic: none -> 3.46 us  [on_device(): normed.T.reshape(chips, 2, in_width // (2 * chips), 2 * tok_count)]
    reshape x0 -> x1, local copies, waits for them, and re-layouts: none -> 2.55 us  [on_device(): both = both.reshape(lat_half, 2 * width)]
    concatenate x1 -> x2, other arithmetic: 0.01 us -> 2.41 us  [the longest x1 1.71 us: on_device(): jnp.concatenate([lax.dynamic_index_in_dim(turned_tokens, c, 1, keepdims=F...]
  transfers between devices with their start and end apart: 9 -> 9, of which waited for: 6 -> 6; matrix products, arithmetic and copies ran while one was open for 22% -> 21% of each run, Pallas kernels for 0% -> 6%
where the time goes in v2:
time: 185 us; the launch traced here: 183 us
  waiting for transfers between devices  60.3 us (33%)
  starting transfers between devices  38.2 us (21%)
  local copies, waits for them, and re-layouts  28.6 us (15%)
  Pallas kernels  21.8 us (12%)
  other arithmetic  17.1 us (9%)
  matrix products  15.9 us (9%)
    all_to_all x3, waiting for transfers between devices, spread_out(): lax.all_to_all(jnp.broadcast_to(block[None], (count,) + block.shape), axe...  28.5 us
    all_to_all x3, starting transfers between devices, spread_out(): lax.all_to_all(jnp.broadcast_to(block[None], (count,) + block.shape), axe...  17.6 us
    all_to_all x1, waiting for transfers between devices, on_device(): parts = lax.all_to_all(chip_grads, XY, 0, 0, tiled=True)  15.7 us
    all_to_all x1, waiting for transfers between devices, on_device(): lax.all_to_all(projected.reshape(heads, share, lat_width), 'mp', 0, 0, ti...  15.6 us
    unnamed x31, local copies, waits for them, and re-layouts  14.5 us
    pallas_call x1, Pallas kernels, backward(): pl.pallas_call(backward_kernel, grid=(slots // block,), in_specs=[pl.Bloc...  11.9 us
    pallas_call x1, Pallas kernels, forward(): pl.pallas_call(forward_kernel, grid=(lat // rows,), in_specs=[pl.BlockSpe...  9.9 us
    all_to_all x1, starting transfers between devices, on_device(): lax.all_to_all(projected.reshape(heads, share, lat_width), 'mp', 0, 0, ti...  8.45 us
  transfers between devices with their start and end apart: 9, of which 6 were waited for; matrix products, arithmetic and copies ran while one was open for 21% of the time, Pallas kernels for 6%

profile of v2, /device:TPU:8, one launch (start us, length us, event | category | flops | bytes accessed | tf_op | source)
XLA Modules:
  0.0 183.3 jit_solution(5260690300013987983)
XLA Ops:
  3.5 2.0 %multiply_reduce_fusion = f32[640]{0:T(1024)S(1)} fusion(bf16[640,1024]{1,0:T(8,128)(2,1)} %param.10, f32[640]{0:T(1024)S(1)} %broadcast_multiply_fusion, f32[5,1024]{1,0:T(8,128)S(1)} %fusion.16), kind=kLoop, calls=%fused_computation.8 | loop fusion | flops 3276160 | bytes 1336320 | tf_op jit(solution)/shard_map/reduce_sum | solution.py:22
  12.5 7.4 %all-to-all-start = ((bf16[16,64,1024]{2,1,0:T(8,128)(2,1)}), bf16[16,64,1024]{2,1,0:T(8,128)(2,1)S(1)}, u32[]{:S(2)}, u32[]{:S(2)}) async-start(bf16[16,64,1024]{2,1,0:T(8,128)(2,1)} %broadcast_in_dim.6), calls=%async_computation | async-start | bytes 4194304 | tf_op jit(solution)/shard_map/all_to_all | solution.py:27
  21.9 3.5 %fusion.8 = bf16[1024,1280]{0,1:T(8,128)(2,1)} fusion(bf16[640,1024]{1,0:T(8,128)(2,1)} %collective-permute-done.1, bf16[640,1024]{1,0:T(8,128)(2,1)} %multiply_convert_fusion), kind=kLoop, calls=%fused_computation.26 | loop fusion | flops 5242880 | bytes 5242880 | tf_op jit(solution)/shard_map/transpose | solution.py:209
  25.3 4.4 %copy.25 = bf16[1024,1280]{1,0:T(8,128)(2,1)} copy(bf16[1024,1280]{0,1:T(8,128)(2,1)} %fusion.8) | data formatting | bytes 5242880 | tf_op jit(solution)/shard_map/transpose | solution.py:209
  29.7 4.4 %convolution_convert_fusion.1.v_ref = bf16[1280,512]{1,0:T(8,128)(2,1)} fusion(bf16[1024,512]{1,0:T(8,128)(2,1)S(1)} %copy-done, bf16[640,1024]{1,0:T(8,128)(2,1)} %collective-permute-done.1, bf16[640,1024]{1,0:T(8,128)(2,1)} %multiply_convert_fusion), kind=kOutput, calls=%fused_computation.2 | convolution fusion | flops 1348075520 | bytes 4980736 | tf_op jit(solution)/shard_map/dot_general | solution.py:206
  34.1 4.3 %convolution_convert_fusion.2.k_ref = bf16[1280,512]{1,0:T(8,128)(2,1)} fusion(bf16[1024,512]{1,0:T(8,128)(2,1)S(1)} %copy-done.14, bf16[640,1024]{1,0:T(8,128)(2,1)} %collective-permute-done.1, bf16[640,1024]{1,0:T(8,128)(2,1)} %multiply_convert_fusion), kind=kOutput, calls=%fused_computation.3 | convolution fusion | flops 1348075520 | bytes 4980736 | tf_op jit(solution)/shard_map/dot_general | solution.py:205
  38.4 10.8 %all-to-all-done = bf16[16,64,1024]{2,1,0:T(8,128)(2,1)S(1)} async-done(((bf16[16,64,1024]{2,1,0:T(8,128)(2,1)}), bf16[16,64,1024]{2,1,0:T(8,128)(2,1)S(1)}, u32[]{:S(2)}, u32[]{:S(2)}) %all-to-all-start) | async-done | bytes 2097184 | tf_op jit(solution)/shard_map/all_to_all | solution.py:27
  51.9 9.9 %shard_map.121 = (bf16[1024,1280]{1,0:T(8,128)(2,1)S(1)}, f32[1024,1280]{1,0:T(8,128)S(1)}, bf16[1024,512]{1,0:T(8,128)(2,1)S(1)}, f32[8,1024]{1,0:T(8,128)S(1)}) custom-call(s32[2]{0:T(128)S(1)} %pad_add_fusion.live_ref, bf16[1024,1024]{1,0:T(8,128)(2,1)S(1)} %bitcast.45, bf16[1024,1024]{1,0:T(8,128)(2,1)S(1)} %bitcast.46, bf16[1280,512]{1,0:T(8,128)(2,1)S(1)} %copy-done.8, ...), custom_call_target="tpu_custom_call" | custom-call | flops 4026531840 | bytes 13631488 | tf_op jit(solution)/shard_map/pallas_call | solution.py:72
  62.8 2.3 %copy-done.4 = f32[1024,1280]{1,0:T(8,128)} copy-done((f32[1024,1280]{1,0:T(8,128)}, f32[1024,1280]{1,0:T(8,128)S(1)}, u32[]{:S(2)}) %copy-start.4) | copy-done | bytes 5242904
  67.5 6.7 %all-to-all-start.2 = ((f32[16,8,1024]{2,1,0:T(8,128)}), f32[16,8,1024]{2,1,0:T(8,128)}, u32[]{:S(2)}, u32[]{:S(2)}) async-start(f32[16,8,1024]{2,1,0:T(8,128)} %broadcast_in_dim.7), calls=%async_computation.2 | async-start | bytes 1048576 | tf_op jit(solution)/shard_map/all_to_all | solution.py:27
  74.2 1.9 %dynamic-slice_bitcast_fusion.1 = (bf16[16,32,1280]{2,1,0:T(8,128)(2,1)S(1)}, bf16[16,32,1280]{2,1,0:T(8,128)(2,1)S(1)}) fusion(bf16[16,2,32,1280]{3,2,1,0:T(8,128)(2,1)} %bitcast.51, s32[]{:T(128)S(6)} %select_n.16, s32[]{:T(128)S(6)} %select_n.17), kind=kLoop, calls=%fused_computation.18 | loop fusion | bytes 5242888 | tf_op jit(solution)/shard_map/jit(dynamic_index_in_dim)/squeeze | solution.py:211
  77.8 2.5 %copy.24 = bf16[1024,1024]{0,1:T(8,128)(2,1)} copy(bf16[1024,1024]{1,0:T(8,128)(2,1)S(1)} %bitcast.47) | data formatting | bytes 4194304 | tf_op jit(solution)/shard_map/reshape | solution.py:195
  80.3 3.6 %all-to-all-done.2.stat_ref = f32[16,8,1024]{2,1,0:T(8,128)} async-done(((f32[16,8,1024]{2,1,0:T(8,128)}), f32[16,8,1024]{2,1,0:T(8,128)}, u32[]{:S(2)}, u32[]{:S(2)}) %all-to-all-start.2) | async-done | bytes 524320 | tf_op jit(solution)/shard_map/all_to_all | solution.py:27
  84.0 4.9 %all-to-all-start.1 = ((bf16[16,64,512]{2,1,0:T(8,128)(2,1)}), bf16[16,64,512]{2,1,0:T(8,128)(2,1)S(1)}, u32[]{:S(2)}, u32[]{:S(2)}) async-start(bf16[16,64,512]{2,1,0:T(8,128)(2,1)} %bitcast.50), calls=%async_computation.1 | async-start | bytes 2097152 | tf_op jit(solution)/shard_map/all_to_all | solution.py:219
  92.2 1.7 copy-done.6
  93.9 11.9 %shard_map.122 = bf16[1024,1024]{1,0:T(8,128)(2,1)S(1)} custom-call(f32[16,8,1024]{2,1,0:T(8,128)} %all-to-all-done.2.stat_ref, f32[8,1024]{1,0:T(8,128)S(1)} %get-tuple-element.8.own_ref, bf16[1024,1024]{1,0:T(8,128)(2,1)S(1)} %bitcast.49, bf16[1024,1280]{1,0:T(8,128)(2,1)S(1)} %copy-done.6, f32[1024,1280]{1,0:T(8,128)} %copy-done.4, ...), custom_call_target="tpu_custom_call" | custom-call | flops 5368709120 | bytes 14680064 | tf_op jit(solution)/shard_map/pallas_call | solution.py:140
  108.8 3.9 %fusion = bf16[8,8,4096]{2,1,0:T(8,128)(2,1)} fusion(bf16[512,4096]{1,0:T(8,128)(2,1)} %param.18, f32[64,512]{1,0:T(8,128)S(1)} %multiply_reduce_fusion.1, f32[64]{0:T(128)S(1)} %dynamic_slice.18), kind=kOutput, calls=%fused_computation.1 | convolution fusion | flops 268763136 | bytes 4849920 | tf_op jit(solution)/shard_map/dot_general | solution.py:226
  112.7 8.5 %all-to-all-start.3 = ((bf16[8,8,4096]{2,1,0:T(8,128)(2,1)}), bf16[8,8,4096]{2,1,0:T(8,128)(2,1)S(1)}, u32[]{:S(2)}, u32[]{:S(2)}) async-start(bf16[8,8,4096]{2,1,0:T(8,128)(2,1)} %fusion), calls=%async_computation.3 | async-start | bytes 1048576 | tf_op jit(solution)/shard_map/all_to_all | solution.py:228
  121.1 2.6 %fusion.3 = bf16[16,32,1024]{2,1,0:T(8,128)(2,1)} fusion(bf16[16,32,1024]{2,1,0:T(8,128)(2,1)S(1)} %bitcast.52, bf16[16,32,1024]{2,1,0:T(8,128)(2,1)} %collective-permute-done.2), kind=kLoop, calls=%fused_computation.12 | loop fusion | flops 2097152 | bytes 3145728 | tf_op jit(solution)/shard_map/convert_element_type | solution.py:238
  123.8 15.6 %all-to-all-done.3 = bf16[8,8,4096]{2,1,0:T(8,128)(2,1)S(1)} async-done(((bf16[8,8,4096]{2,1,0:T(8,128)(2,1)}), bf16[8,8,4096]{2,1,0:T(8,128)(2,1)S(1)}, u32[]{:S(2)}, u32[]{:S(2)}) %all-to-all-start.3) | async-done | bytes 524320 | tf_op jit(solution)/shard_map/all_to_all | solution.py:228
  139.3 7.3 %all-to-all-start.5 = ((bf16[16,32,1024]{2,1,0:T(8,128)(2,1)}), bf16[16,32,1024]{2,1,0:T(8,128)(2,1)S(1)}, u32[]{:S(2)}, u32[]{:S(2)}) async-start(bf16[16,32,1024]{2,1,0:T(8,128)(2,1)} %fusion.3), calls=%async_computation.5 | async-start | bytes 2097152 | tf_op jit(solution)/shard_map/all_to_all | solution.py:239
  147.6 15.7 %all-to-all-done.5 = bf16[16,32,1024]{2,1,0:T(8,128)(2,1)S(1)} async-done(((bf16[16,32,1024]{2,1,0:T(8,128)(2,1)}), bf16[16,32,1024]{2,1,0:T(8,128)(2,1)S(1)}, u32[]{:S(2)}, u32[]{:S(2)}) %all-to-all-start.5) | async-done | bytes 1048608 | tf_op jit(solution)/shard_map/all_to_all | solution.py:239
  164.1 3.5 %all-to-all-start.4 = ((bf16[8,8,4096]{2,1,0:T(8,128)(2,1)}), bf16[8,8,4096]{2,1,0:T(8,128)(2,1)S(1)}, u32[]{:S(2)}, u32[]{:S(2)}) async-start(bf16[8,8,4096]{2,1,0:T(8,128)(2,1)} %broadcast_in_dim.8), calls=%async_computation.4 | async-start | bytes 1048576 | tf_op jit(solution)/shard_map/all_to_all | solution.py:27
  168.5 14.1 %all-to-all-done.4 = bf16[8,8,4096]{2,1,0:T(8,128)(2,1)S(1)} async-done(((bf16[8,8,4096]{2,1,0:T(8,128)(2,1)}), bf16[8,8,4096]{2,1,0:T(8,128)(2,1)S(1)}, u32[]{:S(2)}, u32[]{:S(2)}) %all-to-all-start.4) | async-done | bytes 524320 | tf_op jit(solution)/shard_map/all_to_all | solution.py:27
  (63 shorter events, 28.6 us)
Async XLA Ops:
  0.6 29.1 %copy-start = (bf16[1024,512]{1,0:T(8,128)(2,1)S(1)}, bf16[1024,512]{1,0:T(8,128)(2,1)}, u32[]{:S(2)}) copy-start(bf16[1024,512]{1,0:T(8,128)(2,1)} %param.17) | copy-start | bytes 3145732
  0.6 4.8 %copy-start.10 = (bf16[640,1024]{1,0:T(8,128)(2,1)S(1)}, bf16[640,1024]{1,0:T(8,128)(2,1)}, u32[]{:S(2)}) copy-start(bf16[640,1024]{1,0:T(8,128)(2,1)} %param.10) | copy-start | bytes 3932164
  1.7 5.3 %copy-start.11 = (bf16[64,4096]{1,0:T(8,128)(2,1)S(1)}, bf16[64,4096]{1,0:T(8,128)(2,1)}, u32[]{:S(2)}) copy-start(bf16[64,4096]{1,0:T(8,128)(2,1)} %param.14) | copy-start | bytes 1572868
  3.5 4.1 %copy-start.12 = (bf16[4096,512]{1,0:T(8,128)(2,1)S(1)}, bf16[4096,512]{1,0:T(8,128)(2,1)}, u32[]{:S(2)}) copy-start(bf16[4096,512]{1,0:T(8,128)(2,1)} %param.15) | copy-start | bytes 12582916
  7.0 14.8 %collective-permute-start.1 = (bf16[640,1024]{1,0:T(8,128)(2,1)}, bf16[640,1024]{1,0:T(8,128)(2,1)}, u32[]{:S(2)}, u32[]{:S(2)}) collective-permute-start(bf16[640,1024]{1,0:T(8,128)(2,1)} %multiply_convert_fusion), channel_id=1, source_target_pairs={{0,8},{8,0},{1,9},{9,1},{2,10},{10,2},{3,11},{11,3},{4,12},{12,4},... | collective-permute-start | bytes 3932168 | tf_op jit(solution)/shard_map/ppermute | solution.py:201
  7.2 2.2 %copy-start.9 = (bf16[512,4096]{1,0:T(8,128)(2,1)S(1)}, bf16[512,4096]{1,0:T(8,128)(2,1)}, u32[]{:S(2)}) copy-start(bf16[512,4096]{1,0:T(8,128)(2,1)} %param.18) | copy-start | bytes 12582916
  7.2 2.3 %copy-start.13 = (bf16[64,4096]{1,0:T(8,128)(2,1)S(1)}, bf16[64,4096]{1,0:T(8,128)(2,1)}, u32[]{:S(2)}) copy-start(bf16[64,4096]{1,0:T(8,128)(2,1)} %param.19) | copy-start | bytes 1572868
  12.5 36.7 %all-to-all-start = ((bf16[16,64,1024]{2,1,0:T(8,128)(2,1)}), bf16[16,64,1024]{2,1,0:T(8,128)(2,1)S(1)}, u32[]{:S(2)}, u32[]{:S(2)}) async-start(bf16[16,64,1024]{2,1,0:T(8,128)(2,1)} %broadcast_in_dim.6), calls=%async_computation | async-start | bytes 4194304 | tf_op jit(solution)/shard_map/all_to_all | solution.py:27
  19.9 1.2 collective-permute-start
  29.7 4.4 %copy-start.14 = (bf16[1024,512]{1,0:T(8,128)(2,1)S(1)}, bf16[1024,512]{1,0:T(8,128)(2,1)}, u32[]{:S(2)}) copy-start(bf16[1024,512]{1,0:T(8,128)(2,1)} %param.16) | copy-start | bytes 3145732
  49.2 1.3 copy-start.7
  50.6 1.3 copy-start.8
  61.8 1.0 copy-start.3
  62.8 2.3 %copy-start.4 = (f32[1024,1280]{1,0:T(8,128)}, f32[1024,1280]{1,0:T(8,128)S(1)}, u32[]{:S(2)}) copy-start(f32[1024,1280]{1,0:T(8,128)S(1)} %get-tuple-element.10.d_ref) | copy-start | bytes 15728644
  65.1 1.6 copy-start.5
  67.5 16.4 %all-to-all-start.2 = ((f32[16,8,1024]{2,1,0:T(8,128)}), f32[16,8,1024]{2,1,0:T(8,128)}, u32[]{:S(2)}, u32[]{:S(2)}) async-start(f32[16,8,1024]{2,1,0:T(8,128)} %broadcast_in_dim.7), calls=%async_computation.2 | async-start | bytes 1048576 | tf_op jit(solution)/shard_map/all_to_all | solution.py:27
  84.0 24.6 %all-to-all-start.1 = ((bf16[16,64,512]{2,1,0:T(8,128)(2,1)}), bf16[16,64,512]{2,1,0:T(8,128)(2,1)S(1)}, u32[]{:S(2)}, u32[]{:S(2)}) async-start(bf16[16,64,512]{2,1,0:T(8,128)(2,1)} %bitcast.50), calls=%async_computation.1 | async-start | bytes 2097152 | tf_op jit(solution)/shard_map/all_to_all | solution.py:219
  88.9 1.7 copy-start.1
  90.6 1.6 copy-start.2
  92.2 1.7 copy-start.6
  107.0 14.2 %collective-permute-start.2 = (bf16[16,32,1024]{2,1,0:T(8,128)(2,1)}, bf16[16,32,1024]{2,1,0:T(8,128)(2,1)}, u32[]{:S(2)}, u32[]{:S(2)}) collective-permute-start(bf16[16,32,1024]{2,1,0:T(8,128)(2,1)} %bitcast.13), channel_id=1, source_target_pairs={{0,8},{8,0},{1,9},{9,1},{2,10},{10,2},{3,11},{11,3},{4,12},{12,4},... | collective-permute-start | bytes 3145736 | tf_op jit(solution)/shard_map/ppermute | solution.py:237
  112.7 26.7 %all-to-all-start.3 = ((bf16[8,8,4096]{2,1,0:T(8,128)(2,1)}), bf16[8,8,4096]{2,1,0:T(8,128)(2,1)S(1)}, u32[]{:S(2)}, u32[]{:S(2)}) async-start(bf16[8,8,4096]{2,1,0:T(8,128)(2,1)} %fusion), calls=%async_computation.3 | async-start | bytes 1048576 | tf_op jit(solution)/shard_map/all_to_all | solution.py:228
  139.3 23.9 %all-to-all-start.5 = ((bf16[16,32,1024]{2,1,0:T(8,128)(2,1)}), bf16[16,32,1024]{2,1,0:T(8,128)(2,1)S(1)}, u32[]{:S(2)}, u32[]{:S(2)}) async-start(bf16[16,32,1024]{2,1,0:T(8,128)(2,1)} %fusion.3), calls=%async_computation.5 | async-start | bytes 2097152 | tf_op jit(solution)/shard_map/all_to_all | solution.py:239
  164.1 18.4 %all-to-all-start.4 = ((bf16[8,8,4096]{2,1,0:T(8,128)(2,1)}), bf16[8,8,4096]{2,1,0:T(8,128)(2,1)S(1)}, u32[]{:S(2)}, u32[]{:S(2)}) async-start(bf16[8,8,4096]{2,1,0:T(8,128)(2,1)} %broadcast_in_dim.8), calls=%async_computation.4 | async-start | bytes 1048576 | tf_op jit(solution)/shard_map/all_to_all | solution.py:27

commit v3 on v1

v3 whole, which is shorter than its diff:
```python
import functools

import jax
import jax.numpy as jnp
from jax import lax
from jax.experimental import pallas as pl
from jax.experimental.pallas import tpu as pltpu
from jax.sharding import Mesh, PartitionSpec as P

HD = 512
SCALE = HD ** (-0.5)
FLOOR = -1e30
XY = ("x", "y")
SEQ = ("x", "y", "core")
f32 = jnp.float32
bf16 = jnp.bfloat16


def normalize(values):
    mean = jnp.mean(values, axis=-1, keepdims=True)
    centred = values - mean
    spread = jnp.mean(centred * centred, axis=-1, keepdims=True)
    return centred * lax.rsqrt(spread + 1e-05)


def spread_out(block, axes, count):
    return lax.all_to_all(
        jnp.broadcast_to(block[None], (count,) + block.shape), axes, 0, 0, tiled=True
    )


def ring_gather(block, axis):
    count = lax.axis_size(axis)
    return jnp.stack(
        [block]
        + [
            lax.ppermute(block, axis, [(i, (i + k) % count) for i in range(count)])
            for k in range(1, count)
        ]
    )


def cube_gather(block, axis):
    count = lax.axis_size(axis)
    me = lax.axis_index(axis)
    out = block[None]
    far = count // 2
    while far:
        other = lax.ppermute(out, axis, [(i, i ^ far) for i in range(count)])
        upper = (me & far) != 0
        out = jnp.stack(
            [jnp.where(upper, other, out), jnp.where(upper, out, other)], axis=1
        ).reshape((2 * out.shape[0],) + block.shape)
        far //= 2
    return out


def dot_nn(a, b):
    return jnp.dot(a, b, preferred_element_type=f32)


def dot_nt(a, b):
    return lax.dot_general(a, b, (((1,), (1,)), ((), ())), preferred_element_type=f32)


def dot_tn(a, b):
    return lax.dot_general(a, b, (((0,), (0,)), ((), ())), preferred_element_type=f32)


def far(*arrays):
    return [pltpu.with_memory_space_constraint(a, pltpu.HBM) for a in arrays]


def limits(bytes_wanted):
    return pltpu.CompilerParams(vmem_limit_bytes=bytes_wanted)


def query_kernel(lat_ref, w_ref, out_ref, normed, total):
    step = pl.program_id(0)
    chunk = w_ref.shape[0]

    @pl.when(step == 0)
    def _():
        normed[...] = normalize(lat_ref[...].astype(f32)).astype(bf16)
        total[...] = jnp.zeros_like(total)

    columns = pl.ds(pl.multiple_of(step * chunk, chunk), chunk)
    total[...] += dot_nn(normed[:, columns], w_ref[...])

    @pl.when(step == pl.num_programs(0) - 1)
    def _():
        result = total[...].astype(bf16)
        for copy in range(out_ref.shape[0]):
            out_ref[copy] = result


def make_queries(latents, w_query, copies):
    rows, depth = latents.shape
    width = w_query.shape[1]
    steps = 4
    return pl.pallas_call(
        query_kernel,
        grid=(steps,),
        in_specs=[
            pl.BlockSpec((rows, depth), lambda i: (0, 0)),
            pl.BlockSpec((depth // steps, width), lambda i: (i, 0)),
        ],
        out_specs=pl.BlockSpec((copies, rows, width), lambda i: (0, 0, 0)),
        out_shape=jax.ShapeDtypeStruct((copies, rows, width), bf16),
        scratch_shapes=[pltpu.VMEM((rows, depth), bf16), pltpu.VMEM((rows, width), f32)],
        compiler_params=limits(16 << 20),
        cost_estimate=pl.CostEstimate(
            flops=2 * rows * depth * width,
            bytes_accessed=2 * (rows + width) * depth + 2 * copies * rows * width,
            transcendentals=rows,
        ),
    )(*far(latents, w_query))


def back_kernel(cot_ref, w_ref, after_ref, out_ref, total):
    step = pl.program_id(0)

    @pl.when(step == 0)
    def _():
        total[...] = jnp.zeros_like(total)

    total[...] += dot_nt(cot_ref[...], w_ref[...])

    @pl.when(step == pl.num_programs(0) - 1)
    def _():
        out_ref[...] = total[...].astype(bf16)


def make_back(cotangent, w_out, after):
    rows, depth = cotangent.shape
    width = w_out.shape[0]
    steps = 4
    return pl.pallas_call(
        back_kernel,
        grid=(steps,),
        in_specs=[
            pl.BlockSpec((rows, depth // steps), lambda i: (0, i)),
            pl.BlockSpec((width, depth // steps), lambda i: (0, i)),
            pl.BlockSpec(memory_space=pl.ANY),
        ],
        out_specs=pl.BlockSpec((rows, width), lambda i: (0, 0)),
        out_shape=jax.ShapeDtypeStruct((rows, width), bf16),
        scratch_shapes=[pltpu.VMEM((rows, width), f32)],
        compiler_params=limits(16 << 20),
        cost_estimate=pl.CostEstimate(
            flops=2 * rows * depth * width,
            bytes_accessed=2 * (rows + width) * depth,
            transcendentals=0,
        ),
    )(*far(cotangent, w_out), after)


def token_kernel(
    facts_ref, table_ref, own_ref, other_ref, wk_ref, wv_ref, after_ref, k_ref, v_ref, n_ref
):
    def work(side, ref):
        for block in range(ref.shape[0] // 128):
            mode = facts_ref[side, block]
            place = pl.ds(block * 128, 128)
            raw = ref[place, :].astype(f32) + table_ref[pl.ds(mode, 1), :]
            n_ref[place, :] = normalize(raw).astype(bf16)

    @pl.when(pl.program_id(0) == 0)
    def _():
        work(0, own_ref)

    @pl.when(pl.program_id(0) == 1)
    def _():
        work(1, other_ref)

    k_ref[...] = dot_nn(n_ref[...], wk_ref[...]).astype(bf16)
    v_ref[...] = dot_nn(n_ref[...], wv_ref[...]).astype(bf16)


def make_tokens(facts, table, own, other, w_key, w_value, after):
    slots, in_width = own.shape
    width = w_key.shape[1]
    whole = lambda i: (0, 0)
    side = lambda i: (i, 0)
    return pl.pallas_call(
        token_kernel,
        grid=(2,),
        in_specs=[pl.BlockSpec(memory_space=pltpu.SMEM)]
        + [pl.BlockSpec(a.shape, whole) for a in (table, own, other, w_key, w_value)]
        + [pl.BlockSpec(memory_space=pl.ANY)],
        out_specs=[
            pl.BlockSpec((slots, width), side),
            pl.BlockSpec((slots, width), side),
            pl.BlockSpec((slots, in_width), side),
        ],
        out_shape=[
            pltpu.HBM((2 * slots, width), bf16),
            pltpu.HBM((2 * slots, width), bf16),
            pltpu.HBM((2 * slots, in_width), bf16),
        ],
        compiler_params=limits(40 << 20),
        cost_estimate=pl.CostEstimate(
            flops=8 * slots * in_width * width,
            bytes_accessed=4 * in_width * (2 * slots + width) + 8 * slots * width,
            transcendentals=2 * slots,
        ),
    )(facts, table, *far(own), other, *far(w_key, w_value), after)


def in_three(value):
    high = value.astype(bf16).astype(f32)
    middle = (value - high).astype(bf16).astype(f32)
    return high, middle, value - high - middle


def scores_kernel(facts_ref, q_ref, k_ref, v_ref, w_ref, part_ref, top_ref):
    rows, width = q_ref.shape
    slots = k_ref.shape[0]
    half = slots // 2
    last = facts_ref.shape[1] - 1
    place = lax.broadcasted_iota(jnp.int32, (1, slots), 1)
    bound = jnp.where(place < half, facts_ref[0, last] * 128, half + facts_ref[1, last] * 128)
    scores = dot_nt(q_ref[...], k_ref[...]) * SCALE
    scores = jnp.where(place < bound, scores, FLOOR)
    top = jnp.max(scores, axis=1, keepdims=True)
    weights = jnp.exp(scores - top)
    total = jnp.sum(weights, axis=1, keepdims=True)
    rounded = weights.astype(bf16)
    w_ref[...] = rounded
    part_ref[:, :width] = dot_nn(rounded, v_ref[...]).astype(bf16)
    lane = lax.broadcasted_iota(jnp.int32, (rows, 128), 1)
    packed = jnp.zeros((rows, 128), f32)
    for index, term in enumerate(in_three(top) + in_three(total)):
        packed = jnp.where(lane == index, term, packed)
    part_ref[:, width:] = packed.astype(bf16)
    top_ref[...] = jnp.broadcast_to(top, (rows, 128))


def attend(facts, queries, keys, values):
    lat, width = queries.shape
    slots = keys.shape[0]
    rows = 256
    whole = lambda i: (0, 0)
    return pl.pallas_call(
        scores_kernel,
        grid=(lat // rows,),
        in_specs=[
            pl.BlockSpec(memory_space=pltpu.SMEM),
            pl.BlockSpec((rows, width), lambda i: (i, 0)),
            pl.BlockSpec((slots, width), whole),
            pl.BlockSpec((slots, width), whole),
        ],
        out_specs=[
            pl.BlockSpec((rows, slots), lambda i: (i, 0)),
            pl.BlockSpec((rows, width + 128), lambda i: (i, 0)),
            pl.BlockSpec((rows, 128), lambda i: (i, 0)),
        ],
        out_shape=[
            pltpu.HBM((lat, slots), bf16),
            pltpu.HBM((lat, width + 128), bf16),
            pltpu.HBM((lat, 128), f32),
        ],
        compiler_params=limits(32 << 20),
        cost_estimate=pl.CostEstimate(
            flops=4 * lat * slots * width,
            bytes_accessed=2 * lat * slots + 6 * lat * width + 4 * slots * width,
            transcendentals=lat * slots,
        ),
    )(facts, queries, *far(keys, values))


def combine_kernel(part_ref, back_ref, near_ref, attn_ref, stat_ref, passed_ref):
    passed_ref[...] = near_ref[...]
    rows, width = back_ref.shape
    terms = part_ref[:, :, width:].astype(f32)
    tops = terms[:, :, 0:1] + terms[:, :, 1:2] + terms[:, :, 2:3]
    totals = terms[:, :, 3:4] + terms[:, :, 4:5] + terms[:, :, 5:6]
    top = jnp.max(tops, axis=0)
    factors = jnp.exp(tops - top[None])
    total = jnp.sum(factors * totals, axis=0)
    summed = jnp.sum(part_ref[:, :, :width].astype(f32) * factors, axis=0)
    attn = (summed / total).astype(bf16)
    attn_ref[...] = attn
    delta = jnp.sum(back_ref[...].astype(f32) * attn.astype(f32), axis=1, keepdims=True)
    lane = lax.broadcasted_iota(jnp.int32, (rows, 128), 1)
    packed = jnp.where(lane == 0, top, jnp.where(lane == 1, total, delta))
    stat_ref[...] = jnp.concatenate([packed, packed], axis=0).T[:8]


def combine(partials, back, near):
    rows, width = back.shape
    vmem = pl.BlockSpec(memory_space=pltpu.VMEM)
    return pl.pallas_call(
        combine_kernel,
        in_specs=[vmem] * 3,
        out_specs=[vmem] * 3,
        out_shape=[
            jax.ShapeDtypeStruct((rows, width), bf16),
            jax.ShapeDtypeStruct((8, 2 * rows), f32),
            jax.ShapeDtypeStruct(near.shape, bf16),
        ],
        compiler_params=limits(24 << 20),
        cost_estimate=pl.CostEstimate(
            flops=2 * partials.size, bytes_accessed=2 * partials.size, transcendentals=rows
        ),
    )(partials, back, near)


def chip_entry(place_ref, chip, side_x, side_y):
    back_x = lax.rem(place_ref[0] - chip // side_y + side_x, side_x)
    back_y = lax.rem(place_ref[1] - chip % side_y + side_y, side_y)
    return back_x, back_y


def product_kernel(place_ref, b_ref, v_ref, d_ref, rows_ref):
    side_x, side_y, rows = b_ref.shape[:3]
    step = pl.program_id(0)
    for row in range(side_y):
        entry = chip_entry(place_ref, step * side_y + row, side_x, side_y)
        rows_ref[pl.ds(row * rows, rows), :] = b_ref[entry]
    d_ref[...] = dot_nt(rows_ref[...], v_ref[...])


def products(place, back_rings, values):
    side_x, side_y, rows, width = back_rings.shape
    lat = side_x * side_y * rows
    slots = values.shape[0]
    block = side_y * rows
    return pl.pallas_call(
        product_kernel,
        grid=(side_x,),
        in_specs=[
            pl.BlockSpec(memory_space=pltpu.SMEM),
            pl.BlockSpec(back_rings.shape, lambda i: (0, 0, 0, 0)),
            pl.BlockSpec((slots, width), lambda i: (0, 0)),
        ],
        out_specs=[
            pl.BlockSpec((block, slots), lambda i: (i, 0)),
            pl.BlockSpec((block, width), lambda i: (i, 0)),
        ],
        out_shape=[pltpu.HBM((lat, slots), f32), pltpu.HBM((lat, width), bf16)],
        compiler_params=limits(24 << 20),
        cost_estimate=pl.CostEstimate(
            flops=2 * lat * slots * width,
            bytes_accessed=4 * lat * slots + 2 * width * (2 * lat + slots),
            transcendentals=0,
        ),
    )(place, back_rings, *far(values))


def backward_kernel(
    place_ref, stat_ref, top_ref, q_ref, b_ref, w_ref, d_ref, out_ref, scaled, delta
):
    width = q_ref.shape[1]
    block = w_ref.shape[1]
    side_x, side_y = stat_ref.shape[0], stat_ref.shape[1]
    rows = stat_ref.shape[3] // 2

    @pl.when(pl.program_id(0) == 0)
    def _():
        for chip in range(side_x * side_y):
            piece = stat_ref[chip_entry(place_ref, chip, side_x, side_y)]
            turned = jnp.concatenate([piece] * 16, axis=0).T[:rows]
            here = pl.ds(chip * rows, rows)
            gain = jnp.exp(top_ref[here, :] - turned[:, 0:1]) / turned[:, 1:2]
            delta[here, :] = jnp.broadcast_to(turned[:, 2:3], (rows, 128))
            gain = jnp.concatenate([gain] * (width // 128), axis=1)
            scaled[here, :width] = (q_ref[here, :].astype(f32) * (gain * SCALE)).astype(bf16)
            scaled[here, width:] = (b_ref[here, :].astype(f32) * gain).astype(bf16)

    mean = jnp.concatenate([delta[...]] * (block // 128), axis=1)
    dscore = (w_ref[...].astype(f32) * (d_ref[...] - mean)).astype(bf16)
    out_ref[:, :width] = dot_tn(dscore, scaled[:, :width]).astype(bf16)
    out_ref[:, width:] = dot_tn(w_ref[...], scaled[:, width:]).astype(bf16)


def backward(place, stats, tops, queries, back, weights, dprob):
    lat, slots = weights.shape
    width = queries.shape[1]
    block = 256
    whole = lambda i: (0, 0)
    return pl.pallas_call(
        backward_kernel,
        grid=(slots // block,),
        in_specs=[
            pl.BlockSpec(memory_space=pltpu.SMEM),
            pl.BlockSpec(stats.shape, lambda i: (0, 0, 0, 0)),
            pl.BlockSpec(tops.shape, whole),
            pl.BlockSpec(queries.shape, whole),
            pl.BlockSpec(back.shape, whole),
            pl.BlockSpec((lat, block), lambda i: (0, i)),
            pl.BlockSpec((lat, block), lambda i: (0, i)),
        ],
        out_specs=pl.BlockSpec((block, 2 * width), lambda i: (i, 0)),
        out_shape=pltpu.HBM((slots, 2 * width), bf16),
        scratch_shapes=[pltpu.VMEM((lat, 2 * width), bf16), pltpu.VMEM((lat, 128), f32)],
        compiler_params=limits(32 << 20),
        cost_estimate=pl.CostEstimate(
            flops=4 * slots * width * lat,
            bytes_accessed=6 * lat * slots + 4 * slots * width + 4 * width * lat,
            transcendentals=lat,
        ),
    )(place, stats, tops, queries, *far(back, weights, dprob))


def weight_kernel(place_ref, n_ref, g_ref, after_ref, keep_ref, give_ref):
    result = dot_tn(n_ref[...], g_ref[...]).astype(bf16)
    chips, share = keep_ref.shape[0], keep_ref.shape[1]
    for core, refs in ((0, (keep_ref, give_ref)), (1, (give_ref, keep_ref))):

        @pl.when(place_ref[2] == core)
        def _():
            for chip in range(chips):
                for part in range(2):
                    first = (2 * chip + part) * share
                    refs[part][chip] = result[first : first + share, :]


def weight_grads(place, normed, grads, after, chips):
    slots, in_width = normed.shape
    double = grads.shape[1]
    share = in_width // (2 * chips)
    steps = 4
    piece = jax.ShapeDtypeStruct((chips, share, double), bf16)
    piece_spec = pl.BlockSpec((chips // steps, share, double), lambda i: (i, 0, 0))
    return pl.pallas_call(
        weight_kernel,
        grid=(steps,),
        in_specs=[
            pl.BlockSpec(memory_space=pltpu.SMEM),
            pl.BlockSpec((slots, in_width // steps), lambda i: (0, i)),
            pl.BlockSpec((slots, double), lambda i: (0, 0)),
            pl.BlockSpec(memory_space=pl.ANY),
        ],
        out_specs=[piece_spec] * 2,
        out_shape=[piece] * 2,
        compiler_params=limits(32 << 20),
        cost_estimate=pl.CostEstimate(
            flops=2 * slots * double * in_width,
            bytes_accessed=2 * (slots * (in_width + double) + in_width * double),
            transcendentals=0,
        ),
    )(place, *far(normed, grads), after)


def add_kernel(pieces_ref, lat_ref, out_ref):
    total = lat_ref[...].astype(f32) + jnp.sum(pieces_ref[...].astype(f32), axis=0)
    out_ref[...] = total.astype(bf16)


def add_pieces(pieces, latents):
    vmem = pl.BlockSpec(memory_space=pltpu.VMEM)
    return pl.pallas_call(
        add_kernel,
        in_specs=[vmem, vmem],
        out_specs=vmem,
        out_shape=jax.ShapeDtypeStruct(latents.shape, bf16),
        cost_estimate=pl.CostEstimate(
            flops=pieces.size, bytes_accessed=2 * pieces.size, transcendentals=0
        ),
    )(pieces, latents)


def on_device(
    tokens,
    block_modality,
    live_blocks,
    mode_table,
    latents,
    w_query,
    w_key,
    w_value,
    w_out,
    cotangent,
    *,
    chips,
    heads,
):
    tok_count, in_width = tokens.shape
    width = w_key.shape[1]
    rows_here, lat_width = latents.shape
    lat_half = chips * rows_here
    swap = [(0, 1), (1, 0)]

    tokens_other = lax.ppermute(tokens, "core", swap)
    facts_own = jnp.concatenate([block_modality, live_blocks])
    facts = jnp.stack([facts_own, lax.ppermute(facts_own, "core", swap)])

    query_copies = make_queries(latents, w_query, chips)
    queries = lax.all_to_all(query_copies, XY, 0, 0, tiled=True).reshape(lat_half, width)
    keys, values, normed = make_tokens(
        facts, mode_table, tokens, tokens_other, w_key, w_value, query_copies
    )

    weights, partial, tops = attend(facts, queries, keys, values)
    partials = lax.all_to_all(
        partial.reshape(chips, rows_here, width + 128), XY, 0, 0, tiled=True
    )
    back_rows = make_back(cotangent, w_out, tops)
    attn_rows, stat_rows, back_near = combine(partials, back_rows, ring_gather(back_rows, "y"))
    stats = ring_gather(ring_gather(stat_rows, "y"), "x")
    back_rings = ring_gather(back_near, "x")
    projected = jnp.dot(attn_rows, w_out, preferred_element_type=f32).astype(bf16)
    share = rows_here // heads
    pieces = lax.all_to_all(projected.reshape(heads, share, lat_width), "mp", 0, 0, tiled=True)

    place = jnp.stack([lax.axis_index(axis) for axis in ("x", "y", "core")]).astype(jnp.int32)
    dprob, back = products(place, back_rings, values)
    grads = backward(place, stats, tops, queries, back, weights, dprob)

    head = lax.axis_index("mp")
    lat_share = lax.dynamic_slice_in_dim(latents, head * share, share, 0)
    mixed_share = add_pieces(pieces, lat_share)
    mixed = cube_gather(mixed_share, "mp").reshape(rows_here, lat_width)
    keep, give = weight_grads(place, normed, grads, mixed_share, chips)
    took = lax.ppermute(give, "core", swap)
    chip_grads = (keep.astype(f32) + took.astype(f32)).astype(bf16)
    parts = lax.all_to_all(chip_grads, XY, 0, 0, tiled=True)
    out = jnp.sum(parts.astype(f32), axis=0)
    return mixed, out[:, :width], out[:, width:]


def solution(mesh):
    seq, heads = mesh.devices.shape
    side = 4
    fine = Mesh(mesh.devices.reshape(seq // (2 * side), side, 2, heads), SEQ + ("mp",))

    def body(*args):
        return on_device(*args, chips=seq // 2, heads=heads)

    in_specs = (
        P(SEQ, None),
        P(SEQ),
        P(SEQ),
        P(),
        P(SEQ, None),
        P(None, "mp"),
        P(None, "mp"),
        P(None, "mp"),
        P("mp", None),
        P(SEQ, None),
    )
    out_specs = (P(SEQ, None), P(SEQ, "mp"), P(SEQ, "mp"))
    return jax.shard_map(
        body, mesh=fine, in_specs=in_specs, out_specs=out_specs, check_vma=False
    )
```

time: 171 us -> 151 us (0.88)
  Pallas kernels: 0 us -> 47.3 us
  matrix products: 46.3 us -> 3.83 us
  waiting for transfers between devices: 67.2 us -> 41.1 us
  starting transfers between devices: 37.5 us -> 50.5 us
  other arithmetic: 10.6 us -> 2.17 us
  local copies, waits for them, and re-layouts: 6.52 us -> 3.78 us
    pallas_call x0 -> x9, Pallas kernels: none -> 47.3 us  [the longest x1 8.98 us: backward(): pl.pallas_call(backward_kernel, grid=(slots // block,), in_specs=[pl.Bloc...]
    dot_general x10 -> x0, matrix products: 42.3 us -> none  [the longest x1 7.46 us: on_device(): lax.dot_general(queries, keys, nt, preferred_element_type=f32) * SCALE]
    all_to_all x4 -> x2, waiting for transfers between devices: 35.2 us -> 6.89 us  [the longest x1 6.88 us: on_device(): lax.all_to_all(query_copies, XY, 0, 0, tiled=True).reshape(lat_half, width)]
    ppermute x2 -> x17, starting transfers between devices: 0.51 us -> 23.5 us  [the longest x12 16.7 us: ring_gather(): lax.ppermute(block, axis, [(i, (i + k) % count) for i in range(count)])]
    all_to_all x1, waiting for transfers between devices: 15.2 us -> 0.01 us  [on_device(): lax.all_to_all(projected.reshape(heads, share, lat_width), 'mp', 0, 0, ti...]
    ppermute x2 -> x17, waiting for transfers between devices: 2.21 us -> 16.6 us  [the longest x12 14.9 us: ring_gather(): lax.ppermute(block, axis, [(i, (i + k) % count) for i in range(count)])]
    all_to_all x4 -> x2, starting transfers between devices: 21.3 us -> 12.6 us  [the longest x1 7.53 us: on_device(): lax.all_to_all(query_copies, XY, 0, 0, tiled=True).reshape(lat_half, width)]
    reduce_sum x7 -> x0, other arithmetic: 5.1 us -> none  [the longest x2 2.03 us: normalize(): spread = jnp.mean(centred * centred, axis=-1, keepdims=True)]
  transfers between devices with their start and end apart: 9 -> 22, of which waited for: 6 -> 10; matrix products, arithmetic and copies ran while one was open for 22% -> 5% of each run, Pallas kernels for 0% -> 25%
where the time goes in v3:
time: 151 us; the launch traced here: 150 us
  starting transfers between devices  50.5 us (33%)
  Pallas kernels  47.3 us (31%)
  waiting for transfers between devices  41.1 us (27%)
  matrix products  3.83 us (3%)
  local copies, waits for them, and re-layouts  3.78 us (3%)
  other arithmetic  2.17 us (1%)
    ppermute x12, starting transfers between devices, ring_gather(): lax.ppermute(block, axis, [(i, (i + k) % count) for i in range(count)])  16.7 us
    all_to_all x1, waiting for transfers between devices, on_device(): parts = lax.all_to_all(chip_grads, XY, 0, 0, tiled=True)  15.8 us
    ppermute x12, waiting for transfers between devices, ring_gather(): lax.ppermute(block, axis, [(i, (i + k) % count) for i in range(count)])  14.9 us
    pallas_call x1, Pallas kernels, backward(): pl.pallas_call(backward_kernel, grid=(slots // block,), in_specs=[pl.Bloc...  8.98 us
    all_to_all x1, starting transfers between devices, on_device(): lax.all_to_all(projected.reshape(heads, share, lat_width), 'mp', 0, 0, ti...  8.46 us
    pallas_call x1, Pallas kernels, make_tokens(): pl.pallas_call(token_kernel, grid=(2,), in_specs=[pl.BlockSpec(memory_spa...  8.29 us
    all_to_all x1, starting transfers between devices, on_device(): lax.all_to_all(query_copies, XY, 0, 0, tiled=True).reshape(lat_half, width)  7.53 us
    pallas_call x1, Pallas kernels, attend(): pl.pallas_call(scores_kernel, grid=(lat // rows,), in_specs=[pl.BlockSpec...  7.36 us
  transfers between devices with their start and end apart: 22, of which 10 were waited for; matrix products, arithmetic and copies ran while one was open for 5% of the time, Pallas kernels for 25%

profile of v3, /device:TPU:8, one launch (start us, length us, event | category | flops | bytes accessed | tf_op | source)
XLA Modules:
  0.0 150.2 jit_solution(2307510669229908731)
XLA Ops:
  0.7 5.1 %shard_map.121.after_ref = bf16[16,64,512]{2,1,0:T(8,128)(2,1)} custom-call(bf16[64,4096]{1,0:T(8,128)(2,1)} %lat_ref.1, bf16[4096,512]{1,0:T(8,128)(2,1)} %w_ref.2), custom_call_target="tpu_custom_call" | custom-call | flops 268435456 | bytes 5767168 | tf_op jit(solution)/shard_map/pallas_call | solution.py:101
  5.8 7.5 %all-to-all-start = ((bf16[16,64,512]{2,1,0:T(8,128)(2,1)}), bf16[16,64,512]{2,1,0:T(8,128)(2,1)S(1)}, u32[]{:S(2)}, u32[]{:S(2)}) async-start(bf16[16,64,512]{2,1,0:T(8,128)(2,1)} %shard_map.121.after_ref), calls=%async_computation | async-start | bytes 2097152 | tf_op jit(solution)/shard_map/all_to_all | solution.py:490
  15.2 8.3 %shard_map.122 = (bf16[1280,512]{1,0:T(8,128)(2,1)}, bf16[1280,512]{1,0:T(8,128)(2,1)}, bf16[1280,1024]{1,0:T(8,128)(2,1)}) custom-call(s32[2,6]{1,0:T(2,128)S(1)} %pad_add_fusion.facts_ref, f32[3,1024]{1,0:T(4,128)S(1)} %copy-done.2, bf16[640,1024]{1,0:T(8,128)(2,1)} %own_ref.1, bf16[640,1024]{1,0:T(8,128)(2,1)} %collective-permute-done.1.other_ref, ...), custom_call_target="tpu_custom_call" | custom-call | flops 2684354560 | bytes 9961472 | tf_op jit(solution)/shard_map/pallas_call | solution.py:185
  23.5 6.9 %all-to-all-done = bf16[16,64,512]{2,1,0:T(8,128)(2,1)S(1)} async-done(((bf16[16,64,512]{2,1,0:T(8,128)(2,1)}), bf16[16,64,512]{2,1,0:T(8,128)(2,1)S(1)}, u32[]{:S(2)}, u32[]{:S(2)}) %all-to-all-start) | async-done | bytes 1048608 | tf_op jit(solution)/shard_map/all_to_all | solution.py:490
  30.4 7.4 %shard_map.123 = (bf16[1024,1280]{1,0:T(8,128)(2,1)}, bf16[1024,640]{1,0:T(8,128)(2,1)}, f32[1024,128]{1,0:T(8,128)}) custom-call(s32[2,6]{1,0:T(2,128)S(1)} %pad_add_fusion.facts_ref, bf16[1024,512]{1,0:T(8,128)(2,1)S(1)} %bitcast.54, bf16[1280,512]{1,0:T(8,128)(2,1)} %get-tuple-element.16.k_ref, bf16[1280,512]{1,0:T(8,128)(2,1)} %get-tuple-element.17.v_ref), custom_call_target="tpu_custom_call" | custom-call | flops 2684354560 | bytes 8388608 | tf_op jit(solution)/shard_map/pallas_call | solution.py:244
  37.8 5.1 %all-to-all-start.1 = ((bf16[16,64,640]{2,1,0:T(8,128)(2,1)}), bf16[16,64,640]{2,1,0:T(8,128)(2,1)S(1)}, u32[]{:S(2)}, u32[]{:S(2)}) async-start(bf16[16,64,640]{2,1,0:T(8,128)(2,1)} %bitcast.60), calls=%async_computation.1 | async-start | bytes 2621440 | tf_op jit(solution)/shard_map/all_to_all | solution.py:496
  42.9 4.0 %shard_map.124.back_ref = bf16[64,512]{1,0:T(8,128)(2,1)S(1)} custom-call(bf16[64,4096]{1,0:T(8,128)(2,1)} %cot_ref.1, bf16[512,4096]{1,0:T(8,128)(2,1)} %w_ref.3, f32[1024,128]{1,0:T(8,128)S(1)} %copy-done), custom_call_target="tpu_custom_call" | custom-call | flops 268435456 | bytes 4718592 | tf_op jit(solution)/shard_map/pallas_call | solution.py:138
  49.3 2.4 %collective-permute-start.4 = (bf16[64,512]{1,0:T(8,128)(2,1)S(1)}, bf16[64,512]{1,0:T(8,128)(2,1)S(1)}, u32[]{:S(2)}, u32[]{:S(2)}) collective-permute-start(bf16[64,512]{1,0:T(8,128)(2,1)S(1)} %shard_map.124.back_ref), channel_id=1, source_target_pairs={{0,48},{16,0},{32,16},{48,32},{1,49},{17,1},{33,17},{49,33},{2,50}... | collective-permute-start | bytes 196616 | tf_op jit(solution)/shard_map/ppermute | solution.py:37
  51.7 7.3 %collective-permute-done.2 = bf16[64,512]{1,0:T(8,128)(2,1)S(1)} collective-permute-done((bf16[64,512]{1,0:T(8,128)(2,1)S(1)}, bf16[64,512]{1,0:T(8,128)(2,1)S(1)}, u32[]{:S(2)}, u32[]{:S(2)}) %collective-permute-start.2) | collective-permute-done | bytes 65568 | tf_op jit(solution)/shard_map/ppermute | solution.py:37
  59.1 2.5 %collective-permute-done.3 = bf16[64,512]{1,0:T(8,128)(2,1)S(1)} collective-permute-done((bf16[64,512]{1,0:T(8,128)(2,1)S(1)}, bf16[64,512]{1,0:T(8,128)(2,1)S(1)}, u32[]{:S(2)}, u32[]{:S(2)}) %collective-permute-start.3) | collective-permute-done | bytes 65568 | tf_op jit(solution)/shard_map/ppermute | solution.py:37
  63.0 2.9 %collective-permute-start.15 = (bf16[4,64,512]{2,1,0:T(8,128)(2,1)S(1)}, bf16[4,64,512]{2,1,0:T(8,128)(2,1)S(1)}, u32[]{:S(2)}, u32[]{:S(2)}) collective-permute-start(bf16[4,64,512]{2,1,0:T(8,128)(2,1)S(1)} %get-tuple-element.23), channel_id=1, source_target_pairs={{0,128},{64,192},{128,0},{192,64},{1,129},{65,193},{129,1},{193,65... | collective-permute-start | bytes 786440 | tf_op jit(solution)/shard_map/ppermute | solution.py:37
  67.2 2.8 %collective-permute-start.9 = (f32[8,128]{1,0:T(8,128)S(1)}, f32[8,128]{1,0:T(8,128)S(1)}, u32[]{:S(2)}, u32[]{:S(2)}) collective-permute-start(f32[8,128]{1,0:T(8,128)S(1)} %get-tuple-element.22), channel_id=1, source_target_pairs={{0,32},{16,48},{32,0},{48,16},{1,33},{17,49},{33,1},{49,17},{2,34}... | collective-permute-start | bytes 12296 | tf_op jit(solution)/shard_map/ppermute | solution.py:37
  70.4 3.8 %fusion = bf16[8,8,4096]{2,1,0:T(8,128)(2,1)} fusion(bf16[64,512]{1,0:T(8,128)(2,1)S(1)} %get-tuple-element.20, bf16[512,4096]{1,0:T(8,128)(2,1)} %w_ref.3), kind=kOutput, calls=%fused_computation.1 | convolution fusion | flops 268697600 | bytes 4784128 | tf_op jit(solution)/shard_map/dot_general | solution.py:503
  74.2 8.5 %all-to-all-start.2 = ((bf16[8,8,4096]{2,1,0:T(8,128)(2,1)}), bf16[8,8,4096]{2,1,0:T(8,128)(2,1)S(1)}, u32[]{:S(2)}, u32[]{:S(2)}) async-start(bf16[8,8,4096]{2,1,0:T(8,128)(2,1)} %fusion), calls=%async_computation.2 | async-start | bytes 1048576 | tf_op jit(solution)/shard_map/all_to_all | solution.py:505
  82.7 1.8 %collective-permute-start.16 = (bf16[4,64,512]{2,1,0:T(8,128)(2,1)S(1)}, bf16[4,64,512]{2,1,0:T(8,128)(2,1)S(1)}, u32[]{:S(2)}, u32[]{:S(2)}) collective-permute-start(bf16[4,64,512]{2,1,0:T(8,128)(2,1)S(1)} %get-tuple-element.23), channel_id=1, source_target_pairs={{0,192},{64,0},{128,64},{192,128},{1,193},{65,1},{129,65},{193,129... | collective-permute-start | bytes 786440 | tf_op jit(solution)/shard_map/ppermute | solution.py:37
  87.5 2.0 %collective-permute-done.11 = f32[4,8,128]{2,1,0:T(8,128)S(1)} collective-permute-done((f32[4,8,128]{2,1,0:T(8,128)S(1)}, f32[4,8,128]{2,1,0:T(8,128)S(1)}, u32[]{:S(2)}, u32[]{:S(2)}) %collective-permute-start.11) | collective-permute-done | bytes 16416 | tf_op jit(solution)/shard_map/ppermute | solution.py:37
  93.4 5.2 %shard_map.127 = (f32[1024,1280]{1,0:T(8,128)}, bf16[1024,512]{1,0:T(8,128)(2,1)}) custom-call(s32[3]{0:T(128)S(1)} %pad_add_fusion.2.place_ref, bf16[4,4,64,512]{3,2,1,0:T(8,128)(2,1)S(1)} %pad_maximum_fusion.b_ref, bf16[1280,512]{1,0:T(8,128)(2,1)} %get-tuple-element.17.v_ref), custom_call_target="tpu_custom_call" | custom-call | flops 1342177280 | bytes 8650752 | tf_op jit(solution)/shard_map/pallas_call | solution.py:329
  99.3 1.8 %shard_map.126.after_ref = bf16[8,4096]{1,0:T(8,128)(2,1)} custom-call(bf16[8,8,4096]{2,1,0:T(8,128)(2,1)} %copy-done.3, bf16[8,4096]{1,0:T(8,128)(2,1)} %constant_dynamic-slice_fusion.lat_ref), custom_call_target="tpu_custom_call" | custom-call | flops 262144 | bytes 524288 | tf_op jit(solution)/shard_map/pallas_call | solution.py:453
  101.1 5.9 %collective-permute-start.5 = (bf16[1,8,4096]{2,1,0:T(8,128)(2,1)}, bf16[1,8,4096]{2,1,0:T(8,128)(2,1)S(1)}, u32[]{:S(2)}, u32[]{:S(2)}) collective-permute-start(bf16[1,8,4096]{2,1,0:T(8,128)(2,1)} %bitcast.57), channel_id=1, source_target_pairs={{0,4},{1,5},{2,6},{3,7},{4,0},{5,1},{6,2},{7,3},{8,12},{9,13},{10,... | collective-permute-start | bytes 196616 | tf_op jit(solution)/shard_map/ppermute | solution.py:49
  107.0 9.0 %shard_map.128.g_ref = bf16[1280,1024]{1,0:T(8,128)(2,1)} custom-call(s32[3]{0:T(128)S(1)} %pad_add_fusion.2.place_ref, f32[4,4,8,128]{3,2,1,0:T(8,128)S(1)} %pad_maximum_fusion.4.stat_ref, f32[1024,128]{1,0:T(8,128)S(1)} %copy-done, bf16[1024,512]{1,0:T(8,128)(2,1)S(1)} %bitcast.55, bf16[1024,512]{1,0:T(8,128)(2,1)} %get-tuple-element.24.b_ref, ...), custom_call_target="tpu_custom_call" | custom-call | flops 2684354560 | bytes 12582912 | tf_op jit(solution)/shard_map/pallas_call | solution.py:382
  116.6 5.9 %shard_map.129 = (bf16[16,32,1024]{2,1,0:T(8,128)(2,1)S(1)}, bf16[16,32,1024]{2,1,0:T(8,128)(2,1)S(1)}) custom-call(s32[3]{0:T(128)S(1)} %pad_add_fusion.2.place_ref, bf16[1280,1024]{1,0:T(8,128)(2,1)} %get-tuple-element.21.n_ref, bf16[1280,1024]{1,0:T(8,128)(2,1)} %shard_map.128.g_ref, bf16[8,4096]{1,0:T(8,128)(2,1)S(1)} %copy-done.1), custom_call_target="tpu_custom_call" | custom-call | flops 2684354560 | bytes 7340032 | tf_op jit(solution)/shard_map/pallas_call | solution.py:426
  123.5 1.8 %collective-permute-done.17 = bf16[16,32,1024]{2,1,0:T(8,128)(2,1)S(1)} collective-permute-done((bf16[16,32,1024]{2,1,0:T(8,128)(2,1)S(1)}, bf16[16,32,1024]{2,1,0:T(8,128)(2,1)S(1)}, u32[]{:S(2)}, u32[]{:S(2)}) %collective-permute-start.17) | collective-permute-done | bytes 1048608 | tf_op jit(solution)/shard_map/ppermute | solution.py:516
  126.7 5.9 %all-to-all-start.3 = ((bf16[16,32,1024]{2,1,0:T(8,128)(2,1)}), bf16[16,32,1024]{2,1,0:T(8,128)(2,1)S(1)}, u32[]{:S(2)}, u32[]{:S(2)}) async-start(bf16[16,32,1024]{2,1,0:T(8,128)(2,1)} %add_convert_fusion), calls=%async_computation.3 | async-start | bytes 2097152 | tf_op jit(solution)/shard_map/all_to_all | solution.py:518
  133.5 15.8 %all-to-all-done.3 = bf16[16,32,1024]{2,1,0:T(8,128)(2,1)S(1)} async-done(((bf16[16,32,1024]{2,1,0:T(8,128)(2,1)}), bf16[16,32,1024]{2,1,0:T(8,128)(2,1)S(1)}, u32[]{:S(2)}, u32[]{:S(2)}) %all-to-all-start.3) | async-done | bytes 1048608 | tf_op jit(solution)/shard_map/all_to_all | solution.py:518
  (60 shorter events, 19.3 us)
Async XLA Ops:
  0.6 14.6 %collective-permute-start.1 = (bf16[640,1024]{1,0:T(8,128)(2,1)}, bf16[640,1024]{1,0:T(8,128)(2,1)}, u32[]{:S(2)}, u32[]{:S(2)}) collective-permute-start(bf16[640,1024]{1,0:T(8,128)(2,1)} %own_ref.1), channel_id=1, source_target_pairs={{0,8},{8,0},{1,9},{9,1},{2,10},{10,2},{3,11},{11,3},{4,12},{12,4},... | collective-permute-start | bytes 3932168 | tf_op jit(solution)/shard_map/ppermute | solution.py:485
  5.8 9.4 %copy-start.2 = (f32[3,1024]{1,0:T(4,128)S(1)}, f32[3,1024]{1,0:T(4,128)}, u32[]{:S(2)}) copy-start(f32[3,1024]{1,0:T(4,128)} %table_ref.1) | copy-start | bytes 36868
  5.8 24.6 %all-to-all-start = ((bf16[16,64,512]{2,1,0:T(8,128)(2,1)}), bf16[16,64,512]{2,1,0:T(8,128)(2,1)S(1)}, u32[]{:S(2)}, u32[]{:S(2)}) async-start(bf16[16,64,512]{2,1,0:T(8,128)(2,1)} %shard_map.121.after_ref), calls=%async_computation | async-start | bytes 2097152 | tf_op jit(solution)/shard_map/all_to_all | solution.py:490
  14.1 1.1 collective-permute-start
  37.8 23.9 %all-to-all-start.1 = ((bf16[16,64,640]{2,1,0:T(8,128)(2,1)}), bf16[16,64,640]{2,1,0:T(8,128)(2,1)S(1)}, u32[]{:S(2)}, u32[]{:S(2)}) async-start(bf16[16,64,640]{2,1,0:T(8,128)(2,1)} %bitcast.60), calls=%async_computation.1 | async-start | bytes 2621440 | tf_op jit(solution)/shard_map/all_to_all | solution.py:496
  46.9 12.1 %collective-permute-start.2 = (bf16[64,512]{1,0:T(8,128)(2,1)S(1)}, bf16[64,512]{1,0:T(8,128)(2,1)S(1)}, u32[]{:S(2)}, u32[]{:S(2)}) collective-permute-start(bf16[64,512]{1,0:T(8,128)(2,1)S(1)} %shard_map.124.back_ref), channel_id=1, source_target_pairs={{0,16},{16,32},{32,48},{48,0},{1,17},{17,33},{33,49},{49,1},{2,18}... | collective-permute-start | bytes 196616 | tf_op jit(solution)/shard_map/ppermute | solution.py:37
  48.5 13.1 %collective-permute-start.3 = (bf16[64,512]{1,0:T(8,128)(2,1)S(1)}, bf16[64,512]{1,0:T(8,128)(2,1)S(1)}, u32[]{:S(2)}, u32[]{:S(2)}) collective-permute-start(bf16[64,512]{1,0:T(8,128)(2,1)S(1)} %shard_map.124.back_ref), channel_id=1, source_target_pairs={{0,32},{16,48},{32,0},{48,16},{1,33},{17,49},{33,1},{49,17},{2,34}... | collective-permute-start | bytes 196616 | tf_op jit(solution)/shard_map/ppermute | solution.py:37
  49.3 12.3 %collective-permute-start.4 = (bf16[64,512]{1,0:T(8,128)(2,1)S(1)}, bf16[64,512]{1,0:T(8,128)(2,1)S(1)}, u32[]{:S(2)}, u32[]{:S(2)}) collective-permute-start(bf16[64,512]{1,0:T(8,128)(2,1)S(1)} %shard_map.124.back_ref), channel_id=1, source_target_pairs={{0,48},{16,0},{32,16},{48,32},{1,49},{17,1},{33,17},{49,33},{2,50}... | collective-permute-start | bytes 196616 | tf_op jit(solution)/shard_map/ppermute | solution.py:37
  62.4 30.9 %collective-permute-start.14 = (bf16[4,64,512]{2,1,0:T(8,128)(2,1)S(1)}, bf16[4,64,512]{2,1,0:T(8,128)(2,1)S(1)}, u32[]{:S(2)}, u32[]{:S(2)}) collective-permute-start(bf16[4,64,512]{2,1,0:T(8,128)(2,1)S(1)} %get-tuple-element.23), channel_id=1, source_target_pairs={{0,64},{64,128},{128,192},{192,0},{1,65},{65,129},{129,193},{193,1... | collective-permute-start | bytes 786440 | tf_op jit(solution)/shard_map/ppermute | solution.py:37
  63.0 30.2 %collective-permute-start.15 = (bf16[4,64,512]{2,1,0:T(8,128)(2,1)S(1)}, bf16[4,64,512]{2,1,0:T(8,128)(2,1)S(1)}, u32[]{:S(2)}, u32[]{:S(2)}) collective-permute-start(bf16[4,64,512]{2,1,0:T(8,128)(2,1)S(1)} %get-tuple-element.23), channel_id=1, source_target_pairs={{0,128},{64,192},{128,0},{192,64},{1,129},{65,193},{129,1},{193,65... | collective-permute-start | bytes 786440 | tf_op jit(solution)/shard_map/ppermute | solution.py:37
  65.8 16.8 %collective-permute-start.8 = (f32[8,128]{1,0:T(8,128)S(1)}, f32[8,128]{1,0:T(8,128)S(1)}, u32[]{:S(2)}, u32[]{:S(2)}) collective-permute-start(f32[8,128]{1,0:T(8,128)S(1)} %get-tuple-element.22), channel_id=1, source_target_pairs={{0,16},{16,32},{32,48},{48,0},{1,17},{17,33},{33,49},{49,1},{2,18}... | collective-permute-start | bytes 12296 | tf_op jit(solution)/shard_map/ppermute | solution.py:37
  67.2 17.2 %collective-permute-start.9 = (f32[8,128]{1,0:T(8,128)S(1)}, f32[8,128]{1,0:T(8,128)S(1)}, u32[]{:S(2)}, u32[]{:S(2)}) collective-permute-start(f32[8,128]{1,0:T(8,128)S(1)} %get-tuple-element.22), channel_id=1, source_target_pairs={{0,32},{16,48},{32,0},{48,16},{1,33},{17,49},{33,1},{49,17},{2,34}... | collective-permute-start | bytes 12296 | tf_op jit(solution)/shard_map/ppermute | solution.py:37
  70.1 14.4 %collective-permute-start.10 = (f32[8,128]{1,0:T(8,128)S(1)}, f32[8,128]{1,0:T(8,128)S(1)}, u32[]{:S(2)}, u32[]{:S(2)}) collective-permute-start(f32[8,128]{1,0:T(8,128)S(1)} %get-tuple-element.22), channel_id=1, source_target_pairs={{0,48},{16,0},{32,16},{48,32},{1,49},{17,1},{33,17},{49,33},{2,50}... | collective-permute-start | bytes 12296 | tf_op jit(solution)/shard_map/ppermute | solution.py:37
  74.2 24.4 %all-to-all-start.2 = ((bf16[8,8,4096]{2,1,0:T(8,128)(2,1)}), bf16[8,8,4096]{2,1,0:T(8,128)(2,1)S(1)}, u32[]{:S(2)}, u32[]{:S(2)}) async-start(bf16[8,8,4096]{2,1,0:T(8,128)(2,1)} %fusion), calls=%async_computation.2 | async-start | bytes 1048576 | tf_op jit(solution)/shard_map/all_to_all | solution.py:505
  82.7 10.6 %collective-permute-start.16 = (bf16[4,64,512]{2,1,0:T(8,128)(2,1)S(1)}, bf16[4,64,512]{2,1,0:T(8,128)(2,1)S(1)}, u32[]{:S(2)}, u32[]{:S(2)}) collective-permute-start(bf16[4,64,512]{2,1,0:T(8,128)(2,1)S(1)} %get-tuple-element.23), channel_id=1, source_target_pairs={{0,192},{64,0},{128,64},{192,128},{1,193},{65,1},{129,65},{193,129... | collective-permute-start | bytes 786440 | tf_op jit(solution)/shard_map/ppermute | solution.py:37
  84.4 5.0 %collective-permute-start.11 = (f32[4,8,128]{2,1,0:T(8,128)S(1)}, f32[4,8,128]{2,1,0:T(8,128)S(1)}, u32[]{:S(2)}, u32[]{:S(2)}) collective-permute-start(f32[4,8,128]{2,1,0:T(8,128)S(1)} %get-tuple-element.38), channel_id=1, source_target_pairs={{0,64},{64,128},{128,192},{192,0},{1,65},{65,129},{129,193},{193,1... | collective-permute-start | bytes 49160 | tf_op jit(solution)/shard_map/ppermute | solution.py:37
  86.3 5.2 %collective-permute-start.12 = (f32[4,8,128]{2,1,0:T(8,128)S(1)}, f32[4,8,128]{2,1,0:T(8,128)S(1)}, u32[]{:S(2)}, u32[]{:S(2)}) collective-permute-start(f32[4,8,128]{2,1,0:T(8,128)S(1)} %get-tuple-element.38), channel_id=1, source_target_pairs={{0,128},{64,192},{128,0},{192,64},{1,129},{65,193},{129,1},{193,65... | collective-permute-start | bytes 49160 | tf_op jit(solution)/shard_map/ppermute | solution.py:37
  89.5 3.7 %collective-permute-start.13 = (f32[4,8,128]{2,1,0:T(8,128)S(1)}, f32[4,8,128]{2,1,0:T(8,128)S(1)}, u32[]{:S(2)}, u32[]{:S(2)}) collective-permute-start(f32[4,8,128]{2,1,0:T(8,128)S(1)} %get-tuple-element.38), channel_id=1, source_target_pairs={{0,192},{64,0},{128,64},{192,128},{1,193},{65,1},{129,65},{193,129... | collective-permute-start | bytes 49160 | tf_op jit(solution)/shard_map/ppermute | solution.py:37
  101.1 14.8 %collective-permute-start.5 = (bf16[1,8,4096]{2,1,0:T(8,128)(2,1)}, bf16[1,8,4096]{2,1,0:T(8,128)(2,1)S(1)}, u32[]{:S(2)}, u32[]{:S(2)}) collective-permute-start(bf16[1,8,4096]{2,1,0:T(8,128)(2,1)} %bitcast.57), channel_id=1, source_target_pairs={{0,4},{1,5},{2,6},{3,7},{4,0},{5,1},{6,2},{7,3},{8,12},{9,13},{10,... | collective-permute-start | bytes 196616 | tf_op jit(solution)/shard_map/ppermute | solution.py:49
  107.0 9.0 %copy-start.1 = (bf16[8,4096]{1,0:T(8,128)(2,1)S(1)}, bf16[8,4096]{1,0:T(8,128)(2,1)}, u32[]{:S(2)}) copy-start(bf16[8,4096]{1,0:T(8,128)(2,1)} %shard_map.126.after_ref) | copy-start | bytes 196612
  116.0 7.4 %collective-permute-start.6 = (bf16[2,8,4096]{2,1,0:T(8,128)(2,1)S(1)}, bf16[2,8,4096]{2,1,0:T(8,128)(2,1)S(1)}, u32[]{:S(2)}, u32[]{:S(2)}) collective-permute-start(bf16[2,8,4096]{2,1,0:T(8,128)(2,1)S(1)} %maximum_bitcast_fusion), channel_id=1, source_target_pairs={{0,2},{1,3},{2,0},{3,1},{4,6},{5,7},{6,4},{7,5},{8,10},{9,11},{10,... | collective-permute-start | bytes 393224 | tf_op jit(solution)/shard_map/ppermute | solution.py:49
  122.6 2.7 %collective-permute-start.17 = (bf16[16,32,1024]{2,1,0:T(8,128)(2,1)S(1)}, bf16[16,32,1024]{2,1,0:T(8,128)(2,1)S(1)}, u32[]{:S(2)}, u32[]{:S(2)}) collective-permute-start(bf16[16,32,1024]{2,1,0:T(8,128)(2,1)S(1)} %get-tuple-element.28), channel_id=1, source_target_pairs={{0,8},{8,0},{1,9},{9,1},{2,10},{10,2},{3,11},{11,3},{4,12},{12,4},... | collective-permute-start | bytes 3145736 | tf_op jit(solution)/shard_map/ppermute | solution.py:516
  123.4 9.1 %collective-permute-start.7 = (bf16[4,8,4096]{2,1,0:T(8,128)(2,1)S(1)}, bf16[4,8,4096]{2,1,0:T(8,128)(2,1)S(1)}, u32[]{:S(2)}, u32[]{:S(2)}) collective-permute-start(bf16[4,8,4096]{2,1,0:T(8,128)(2,1)S(1)} %bitcast.61), channel_id=1, source_target_pairs={{0,1},{1,0},{2,3},{3,2},{4,5},{5,4},{6,7},{7,6},{8,9},{9,8},{10,11... | collective-permute-start | bytes 786440 | tf_op jit(solution)/shard_map/ppermute | solution.py:49
  126.7 22.6 %all-to-all-start.3 = ((bf16[16,32,1024]{2,1,0:T(8,128)(2,1)}), bf16[16,32,1024]{2,1,0:T(8,128)(2,1)S(1)}, u32[]{:S(2)}, u32[]{:S(2)}) async-start(bf16[16,32,1024]{2,1,0:T(8,128)(2,1)} %add_convert_fusion), calls=%async_computation.3 | async-start | bytes 2097152 | tf_op jit(solution)/shard_map/all_to_all | solution.py:518
  (3 other events, 14.1 us)

commit v4 on v3

v4 whole, which is shorter than its diff:
```python
import functools

import jax
import jax.numpy as jnp
from jax import lax
from jax.experimental import pallas as pl
from jax.experimental.pallas import tpu as pltpu
from jax.sharding import Mesh, PartitionSpec as P

HD = 512
SCALE = HD ** (-0.5)
FLOOR = -1e30
XY = ("x", "y")
SEQ = ("x", "y", "core")
f32 = jnp.float32
bf16 = jnp.bfloat16


def normalize(values):
    mean = jnp.mean(values, axis=-1, keepdims=True)
    centred = values - mean
    spread = jnp.mean(centred * centred, axis=-1, keepdims=True)
    return centred * lax.rsqrt(spread + 1e-05)


def spread_out(block, axes, count):
    return lax.all_to_all(
        jnp.broadcast_to(block[None], (count,) + block.shape), axes, 0, 0, tiled=True
    )


def ring_blocks(block, axis):
    count = lax.axis_size(axis)
    return [block] + [
        lax.ppermute(block, axis, [(i, (i + k) % count) for i in range(count)])
        for k in range(1, count)
    ]


def ring_gather(block, axis):
    return jnp.stack(ring_blocks(block, axis))


def dot_nn(a, b):
    return jnp.dot(a, b, preferred_element_type=f32)


def dot_nt(a, b):
    return lax.dot_general(a, b, (((1,), (1,)), ((), ())), preferred_element_type=f32)


def dot_tn(a, b):
    return lax.dot_general(a, b, (((0,), (0,)), ((), ())), preferred_element_type=f32)


def far(*arrays):
    return [pltpu.with_memory_space_constraint(a, pltpu.HBM) for a in arrays]


def limits(bytes_wanted):
    return pltpu.CompilerParams(vmem_limit_bytes=bytes_wanted)


def latent_kernel(lat_ref, wq_ref, cot_ref, wo_ref, q_ref, b_ref, normed, total_q, total_b):
    step = pl.program_id(0)
    chunk = wq_ref.shape[0]

    @pl.when(step == 0)
    def _():
        normed[...] = normalize(lat_ref[...].astype(f32)).astype(bf16)
        total_q[...] = jnp.zeros_like(total_q)
        total_b[...] = jnp.zeros_like(total_b)

    columns = pl.ds(pl.multiple_of(step * chunk, chunk), chunk)
    total_q[...] += dot_nn(normed[:, columns], wq_ref[...])
    total_b[...] += dot_nt(cot_ref[...], wo_ref[...])

    @pl.when(step == pl.num_programs(0) - 1)
    def _():
        q_ref[...] = total_q[...].astype(bf16)
        b_ref[...] = total_b[...].astype(bf16)


def make_latents(latents, w_query, cotangent, w_out):
    rows, depth = latents.shape
    width = w_query.shape[1]
    steps = 4
    out = jax.ShapeDtypeStruct((rows, width), bf16)
    return pl.pallas_call(
        latent_kernel,
        grid=(steps,),
        in_specs=[
            pl.BlockSpec((rows, depth), lambda i: (0, 0)),
            pl.BlockSpec((depth // steps, width), lambda i: (i, 0)),
            pl.BlockSpec((rows, depth // steps), lambda i: (0, i)),
            pl.BlockSpec((width, depth // steps), lambda i: (0, i)),
        ],
        out_specs=[pl.BlockSpec((rows, width), lambda i: (0, 0))] * 2,
        out_shape=[out, out],
        scratch_shapes=[
            pltpu.VMEM((rows, depth), bf16),
            pltpu.VMEM((rows, width), f32),
            pltpu.VMEM((rows, width), f32),
        ],
        compiler_params=limits(24 << 20),
        cost_estimate=pl.CostEstimate(
            flops=4 * rows * depth * width,
            bytes_accessed=4 * (rows + width) * depth,
            transcendentals=rows,
        ),
    )(*far(latents, w_query, cotangent, w_out))


def token_kernel(
    facts_ref, table_ref, own_ref, other_ref, wk_ref, wv_ref, after_ref, k_ref, v_ref, n_ref
):
    def work(side, ref):
        for block in range(ref.shape[0] // 128):
            mode = facts_ref[side, block]
            place = pl.ds(block * 128, 128)
            raw = ref[place, :].astype(f32) + table_ref[pl.ds(mode, 1), :]
            n_ref[place, :] = normalize(raw).astype(bf16)

    @pl.when(pl.program_id(0) == 0)
    def _():
        work(0, own_ref)

    @pl.when(pl.program_id(0) == 1)
    def _():
        work(1, other_ref)

    k_ref[...] = dot_nn(n_ref[...], wk_ref[...]).astype(bf16)
    v_ref[...] = dot_nn(n_ref[...], wv_ref[...]).astype(bf16)


def make_tokens(facts, table, own, other, w_key, w_value, after):
    slots, in_width = own.shape
    width = w_key.shape[1]
    whole = lambda i: (0, 0)
    side = lambda i: (i, 0)
    return pl.pallas_call(
        token_kernel,
        grid=(2,),
        in_specs=[pl.BlockSpec(memory_space=pltpu.SMEM)]
        + [pl.BlockSpec(a.shape, whole) for a in (table, own, other, w_key, w_value)]
        + [pl.BlockSpec(memory_space=pl.ANY)],
        out_specs=[
            pl.BlockSpec((slots, width), side),
            pl.BlockSpec((slots, width), side),
            pl.BlockSpec((slots, in_width), side),
        ],
        out_shape=[
            pltpu.HBM((2 * slots, width), bf16),
            pltpu.HBM((2 * slots, width), bf16),
            pltpu.HBM((2 * slots, in_width), bf16),
        ],
        compiler_params=limits(40 << 20),
        cost_estimate=pl.CostEstimate(
            flops=8 * slots * in_width * width,
            bytes_accessed=4 * in_width * (2 * slots + width) + 8 * slots * width,
            transcendentals=2 * slots,
        ),
    )(facts, table, *far(own), other, *far(w_key, w_value), after)


def pass_kernel(array_ref, after_ref, out_ref):
    del array_ref, after_ref, out_ref


def pass_on(array, after):
    hbm = pl.BlockSpec(memory_space=pl.ANY)
    return pl.pallas_call(
        pass_kernel,
        in_specs=[hbm, hbm],
        out_specs=hbm,
        out_shape=jax.ShapeDtypeStruct(array.shape, array.dtype),
        input_output_aliases={0: 0},
    )(array, after)


def in_three(value):
    high = value.astype(bf16).astype(f32)
    middle = (value - high).astype(bf16).astype(f32)
    return high, middle, value - high - middle


def gathered(refs, here, rows):
    side_far, side_near = len(refs), refs[0].shape[0]
    for back_far, ref in enumerate(refs):
        for back_near in range(side_near):
            at_far = lax.rem(here[0] - back_far + side_far, side_far)
            at_near = lax.rem(here[1] - back_near + side_near, side_near)
            yield at_far, at_near, ref[back_near]


def scores_kernel(
    facts_ref, place_ref, q0_ref, q1_ref, q2_ref, q3_ref, b0_ref, b1_ref, b2_ref, b3_ref, k_ref,
    v_ref, w_ref, d_ref, part_ref, stat_ref, both_ref, ordered
):
    rows = w_ref.shape[0]
    slots, width = k_ref.shape
    share = q0_ref.shape[1]
    half = slots // 2
    last = facts_ref.shape[1] - 1
    step = pl.program_id(0)

    @pl.when(step == 0)
    def _():
        at_x, at_y = place_ref[0], place_ref[1]
        side = q0_ref.shape[0]
        for x, y, block in gathered((q0_ref, q1_ref, q2_ref, q3_ref), (at_x, at_y), share):
            first = pl.multiple_of((x * side + y) * share, share)
            ordered[pl.ds(first, share), :width] = block
        for y, x, block in gathered((b0_ref, b1_ref, b2_ref, b3_ref), (at_y, at_x), share):
            first = pl.multiple_of((x * side + y) * share, share)
            ordered[pl.ds(first, share), width:] = block

    taken = ordered[pl.ds(pl.multiple_of(step * rows, rows), rows), :]
    both_ref[...] = taken
    place = lax.broadcasted_iota(jnp.int32, (1, slots), 1)
    bound = jnp.where(place < half, facts_ref[0, last] * 128, half + facts_ref[1, last] * 128)
    scores = dot_nt(taken[:, :width], k_ref[...]) * SCALE
    scores = jnp.where(place < bound, scores, FLOOR)
    top = jnp.max(scores, axis=1, keepdims=True)
    weights = jnp.exp(scores - top)
    total = jnp.sum(weights, axis=1, keepdims=True)
    rounded = weights.astype(bf16)
    w_ref[...] = rounded
    dprob = dot_nt(taken[:, width:], v_ref[...])
    d_ref[...] = dprob
    cross = jnp.sum(weights * dprob, axis=1, keepdims=True)
    part_ref[:, :width] = dot_nn(rounded, v_ref[...]).astype(bf16)
    lane = lax.broadcasted_iota(jnp.int32, (rows, 128), 1)
    packed = jnp.zeros((rows, 128), f32)
    for index, term in enumerate(in_three(top) + in_three(total)):
        packed = jnp.where(lane == index, term, packed)
    part_ref[:, width:] = packed.astype(bf16)
    stat_ref[...] = jnp.where(lane == 0, top, jnp.where(lane == 1, total, cross)).T[:8]


def attend(facts, place, query_rings, back_rings, keys, values):
    side, share, width = query_rings[0].shape
    lat = len(query_rings) * side * share
    slots = keys.shape[0]
    rows = 256
    whole = lambda i: (0, 0)
    chunk = lambda i: (i, 0)
    smem = pl.BlockSpec(memory_space=pltpu.SMEM)
    ring = pl.BlockSpec((side, share, width), lambda i: (0, 0, 0))
    return pl.pallas_call(
        scores_kernel,
        grid=(lat // rows,),
        in_specs=[smem, smem] + [ring] * 8 + [pl.BlockSpec((slots, width), whole)] * 2,
        out_specs=[
            pl.BlockSpec((rows, slots), chunk),
            pl.BlockSpec((rows, slots), chunk),
            pl.BlockSpec((rows, width + 128), chunk),
            pl.BlockSpec((8, rows), lambda i: (0, i)),
            pl.BlockSpec((rows, 2 * width), chunk),
        ],
        out_shape=[
            pltpu.HBM((lat, slots), bf16),
            pltpu.HBM((lat, slots), f32),
            pltpu.HBM((lat, width + 128), bf16),
            jax.ShapeDtypeStruct((8, lat), f32),
            pltpu.HBM((lat, 2 * width), bf16),
        ],
        scratch_shapes=[pltpu.VMEM((lat, 2 * width), bf16)],
        compiler_params=limits(40 << 20),
        cost_estimate=pl.CostEstimate(
            flops=6 * lat * slots * width,
            bytes_accessed=6 * lat * slots + 10 * lat * width + 4 * slots * width,
            transcendentals=lat * slots,
        ),
    )(facts, place, *query_rings, *back_rings, *far(keys, values))


def combine_kernel(part_ref, after_ref, attn_ref):
    width = attn_ref.shape[1]
    terms = part_ref[:, :, width:].astype(f32)
    tops = terms[:, :, 0:1] + terms[:, :, 1:2] + terms[:, :, 2:3]
    totals = terms[:, :, 3:4] + terms[:, :, 4:5] + terms[:, :, 5:6]
    top = jnp.max(tops, axis=0)
    factors = jnp.exp(tops - top[None])
    total = jnp.sum(factors * totals, axis=0)
    summed = jnp.sum(part_ref[:, :, :width].astype(f32) * factors, axis=0)
    attn_ref[...] = (summed / total).astype(bf16)


def combine(partials, after):
    _, rows, wide = partials.shape
    vmem = pl.BlockSpec(memory_space=pltpu.VMEM)
    return pl.pallas_call(
        combine_kernel,
        in_specs=[vmem, pl.BlockSpec(memory_space=pl.ANY)],
        out_specs=vmem,
        out_shape=jax.ShapeDtypeStruct((rows, wide - 128), bf16),
        compiler_params=limits(24 << 20),
        cost_estimate=pl.CostEstimate(
            flops=2 * partials.size, bytes_accessed=2 * partials.size, transcendentals=rows
        ),
    )(partials, after)


def backward_kernel(
    core_ref, stat_ref, own_ref, both_ref, w_ref, d_ref, n_ref, after_ref, keep_ref,
    give_ref,    scaled, delta, grads, normed, result, arrived
):
    step = pl.program_id(0)
    width = both_ref.shape[1] // 2
    block = w_ref.shape[1]
    lat = both_ref.shape[0]
    fetch = pltpu.make_async_copy(n_ref, normed, arrived)

    @pl.when(step == 0)
    def _():
        fetch.start()
        every = stat_ref[...]
        count = every.shape[1] - 2
        tops = jnp.max(every[:, :count], axis=1)
        totals, crosses = every[:, count], every[:, count + 1]
        top = jnp.max(tops, axis=0, keepdims=True)
        factor = jnp.exp(tops - top)
        total = jnp.sum(factor * totals, axis=0, keepdims=True)
        mean = jnp.sum(factor * crosses, axis=0, keepdims=True) / total
        delta[...] = jnp.broadcast_to(mean, (128, lat)).T
        gain = jnp.exp(own_ref[0:1, :] - top) / total
        gain = jnp.broadcast_to(gain, (128, lat)).T
        gain = jnp.concatenate([gain] * (width // 128), axis=1)
        scaled[:, :width] = (both_ref[:, :width].astype(f32) * (gain * SCALE)).astype(bf16)
        scaled[:, width:] = (both_ref[:, width:].astype(f32) * gain).astype(bf16)

    mean = jnp.concatenate([delta[...]] * (block // 128), axis=1)
    dscore = (w_ref[...].astype(f32) * (d_ref[...] - mean)).astype(bf16)
    there = pl.ds(pl.multiple_of(step * block, block), block)
    grads[there, :width] = dot_tn(dscore, scaled[:, :width]).astype(bf16)
    grads[there, width:] = dot_tn(w_ref[...], scaled[:, width:]).astype(bf16)

    @pl.when(step == pl.num_programs(0) - 1)
    def _():
        fetch.wait()
        result[...] = dot_tn(normed[...], grads[...]).astype(bf16)
        chips, share = keep_ref.shape[0], keep_ref.shape[1]
        for core, refs in ((0, (keep_ref, give_ref)), (1, (give_ref, keep_ref))):

            @pl.when(core_ref[0] == core)
            def _():
                for chip in range(chips):
                    for part in range(2):
                        rows = pl.ds((2 * chip + part) * share, share)
                        refs[part][chip] = result[rows, :]


def backward(core, stats, own, both, weights, dprob, normed, after, chips):
    lat, slots = weights.shape
    width = both.shape[1] // 2
    in_width = normed.shape[1]
    share = in_width // (2 * chips)
    block = 256
    whole = lambda i: (0, 0)
    piece = pltpu.HBM((chips, share, 2 * width), bf16)
    piece_spec = pl.BlockSpec((chips, share, 2 * width), lambda i: (0, 0, 0))
    return pl.pallas_call(
        backward_kernel,
        grid=(slots // block,),
        in_specs=[
            pl.BlockSpec(memory_space=pltpu.SMEM),
            pl.BlockSpec(stats.shape, lambda i: (0, 0, 0)),
            pl.BlockSpec(own.shape, whole),
            pl.BlockSpec(both.shape, whole),
            pl.BlockSpec((lat, block), lambda i: (0, i)),
            pl.BlockSpec((lat, block), lambda i: (0, i)),
            pl.BlockSpec(memory_space=pl.ANY),
            pl.BlockSpec(memory_space=pl.ANY),
        ],
        out_specs=[piece_spec] * 2,
        out_shape=[piece] * 2,
        scratch_shapes=[
            pltpu.VMEM((lat, 2 * width), bf16),
            pltpu.VMEM((lat, 128), f32),
            pltpu.VMEM((slots, 2 * width), bf16),
            pltpu.VMEM(normed.shape, bf16),
            pltpu.VMEM((in_width, 2 * width), bf16),
            pltpu.SemaphoreType.DMA,
        ],
        compiler_params=limits(40 << 20),
        cost_estimate=pl.CostEstimate(
            flops=4 * slots * width * (lat + in_width),
            bytes_accessed=6 * lat * slots + 2 * in_width * (slots + 2 * width) + 4 * width * lat,
            transcendentals=lat,
        ),
    )(core, stats, own, *far(both, weights, dprob, normed), after)


def add_kernel(pieces_ref, lat_ref, after_ref, out_ref):
    total = lat_ref[...].astype(f32) + jnp.sum(pieces_ref[...].astype(f32), axis=0)
    out_ref[...] = total.astype(bf16)


def add_pieces(pieces, latents, after):
    vmem = pl.BlockSpec(memory_space=pltpu.VMEM)
    return pl.pallas_call(
        add_kernel,
        in_specs=[vmem, vmem, pl.BlockSpec(memory_space=pl.ANY)],
        out_specs=vmem,
        out_shape=jax.ShapeDtypeStruct(latents.shape, bf16),
        cost_estimate=pl.CostEstimate(
            flops=pieces.size, bytes_accessed=2 * pieces.size, transcendentals=0
        ),
    )(pieces, latents, after)


def place_kernel(low_ref, v0_ref, v1_ref, v2_ref, v3_ref, out_ref):
    refs = (v0_ref, v1_ref, v2_ref, v3_ref)
    low = low_ref[0]
    for move, ref in enumerate(refs):
        at = jnp.where(move & 1, 1 - low % 2, low % 2) + 2 * jnp.where(
            move & 2, 1 - low // 2, low // 2
        )
        for high in range(ref.shape[0]):
            out_ref[high * len(refs) + at] = ref[high]


def place_pieces(low, pieces):
    pair, rows, width = pieces[0].shape
    vmem = pl.BlockSpec(memory_space=pltpu.VMEM)
    shape = (pair * len(pieces), rows, width)
    return pl.pallas_call(
        place_kernel,
        in_specs=[pl.BlockSpec(memory_space=pltpu.SMEM)] + [vmem] * len(pieces),
        out_specs=vmem,
        out_shape=jax.ShapeDtypeStruct(shape, bf16),
        compiler_params=limits(16 << 20),
        cost_estimate=pl.CostEstimate(
            flops=0, bytes_accessed=4 * pair * len(pieces) * rows * width, transcendentals=0
        ),
    )(low, *pieces)


def on_device(
    tokens,
    block_modality,
    live_blocks,
    mode_table,
    latents,
    w_query,
    w_key,
    w_value,
    w_out,
    cotangent,
    *,
    chips,
    heads,
):
    tok_count, in_width = tokens.shape
    width = w_key.shape[1]
    rows_here, lat_width = latents.shape
    lat_half = chips * rows_here
    swap = [(0, 1), (1, 0)]

    tokens_other = lax.ppermute(tokens, "core", swap)
    facts_own = jnp.concatenate([block_modality, live_blocks])
    facts = jnp.stack([facts_own, lax.ppermute(facts_own, "core", swap)])

    query_rows, back_rows = make_latents(latents, w_query, cotangent, w_out)
    query_rings = ring_blocks(ring_gather(query_rows, "y"), "x")
    back_rings = ring_blocks(ring_gather(back_rows, "x"), "y")
    keys, values, normed = make_tokens(
        facts, mode_table, tokens, tokens_other, w_key, w_value, query_rows
    )

    place = jnp.stack([lax.axis_index(axis) for axis in ("x", "y", "core")]).astype(jnp.int32)
    weights, dprob, partial, own, both = attend(
        facts, place, query_rings, back_rings, keys, values
    )

    near = ring_gather(own[:3], "y")
    near_tops = near[:, 0]
    scale = jnp.exp(near_tops - jnp.max(near_tops, axis=0))
    near_sums = jnp.sum(near[:, 1:] * scale[:, None], axis=0)
    stats = ring_gather(jnp.concatenate([near_tops, near_sums]), "x")

    partials = lax.all_to_all(
        partial.reshape(chips, rows_here, width + 128), XY, 0, 0, tiled=True
    )
    share = rows_here // heads
    lat_share = lax.dynamic_slice_in_dim(latents, lax.axis_index("mp") * share, share, 0)
    attn_rows = combine(partials, lat_share)
    projected = jnp.dot(attn_rows, w_out, preferred_element_type=f32).astype(bf16)
    pieces = lax.all_to_all(projected.reshape(heads, share, lat_width), "mp", 0, 0, tiled=True)
    core = lax.axis_index("core")[None].astype(jnp.int32)
    keep, give = backward(core, stats, own, both, weights, dprob, normed, projected, chips)

    took = lax.ppermute(pass_on(give, pieces), "core", swap)
    mixed_share = add_pieces(pieces, lat_share, give)
    chip_grads = (keep.astype(f32) + took.astype(f32)).astype(bf16)
    head = lax.axis_index("mp")
    across = lax.ppermute(mixed_share, "mp", [(i, i ^ 4) for i in range(heads)])
    upper = head >= 4
    pair = jnp.stack(
        [jnp.where(upper, across, mixed_share), jnp.where(upper, mixed_share, across)]
    )
    quads = [pair] + [
        lax.ppermute(pair, "mp", [(i, i ^ move) for i in range(heads)]) for move in (1, 2, 3)
    ]
    mixed = place_pieces((head % 4)[None].astype(jnp.int32), quads).reshape(rows_here, lat_width)
    parts = lax.all_to_all(chip_grads, XY, 0, 0, tiled=True)
    out = jnp.sum(parts.astype(f32), axis=0)
    return mixed, out[:, :width], out[:, width:]


def solution(mesh):
    seq, heads = mesh.devices.shape
    side = 4
    fine = Mesh(mesh.devices.reshape(seq // (2 * side), side, 2, heads), SEQ + ("mp",))

    def body(*args):
        return on_device(*args, chips=seq // 2, heads=heads)

    in_specs = (
        P(SEQ, None),
        P(SEQ),
        P(SEQ),
        P(),
        P(SEQ, None),
        P(None, "mp"),
        P(None, "mp"),
        P(None, "mp"),
        P("mp", None),
        P(SEQ, None),
    )
    out_specs = (P(SEQ, None), P(SEQ, "mp"), P(SEQ, "mp"))
    return jax.shard_map(
        body, mesh=fine, in_specs=in_specs, out_specs=out_specs, check_vma=False
    )
```

time: 151 us -> 139 us (0.921)
  waiting for transfers between devices: 41.1 us -> 32.1 us
  Pallas kernels: 47.3 us -> 38.8 us
  starting transfers between devices: 50.5 us -> 57.1 us
    all_to_all x1, waiting for transfers between devices: 15.8 us -> 2.24 us  [on_device(): parts = lax.all_to_all(chip_grads, XY, 0, 0, tiled=True)]
    ppermute x16 -> x23, starting transfers between devices: 23.4 us -> 35.9 us  [the longest x18 25.5 us: ring_blocks(): lax.ppermute(block, axis, [(i, (i + k) % count) for i in range(count)])]
    pallas_call x7 -> x6, Pallas kernels: 30 us -> 18.6 us  [the longest x1 9.5 us: attend(): pl.pallas_call(scores_kernel, grid=(lat // rows,), in_specs=[smem, smem]...]
    ppermute x16 -> x23, waiting for transfers between devices: 17.4 us -> 28 us  [the longest x18 19.9 us: ring_blocks(): lax.ppermute(block, axis, [(i, (i + k) % count) for i in range(count)])]
    all_to_all x1 -> x0, starting transfers between devices: 7.53 us -> none  [on_device(): lax.all_to_all(query_copies, XY, 0, 0, tiled=True).reshape(lat_half, width)]
    all_to_all x1 -> x0, waiting for transfers between devices: 6.88 us -> none  [on_device(): lax.all_to_all(query_copies, XY, 0, 0, tiled=True).reshape(lat_half, width)]
    pallas_call x1, Pallas kernels: 8.98 us -> 12.3 us  [backward(): pl.pallas_call(backward_kernel, grid=(slots // block,), in_specs=[pl.Bloc...]
    all_to_all x1, waiting for transfers between devices: 0.01 us -> 1.92 us  [on_device(): lax.all_to_all(partial.reshape(chips, rows_here, width + 128), XY, 0, 0,...]
  transfers between devices with their start and end apart: 22 -> 28, of which waited for: 10 -> 11; matrix products, arithmetic and copies ran while one was open for 5% -> 2% of each run, Pallas kernels for 25% -> 19%
where the time goes in v4:
time: 139 us
  starting transfers between devices  57.1 us (41%)
  Pallas kernels  38.8 us (28%)
  waiting for transfers between devices  32.1 us (23%)
  matrix products  3.83 us (3%)
  local copies, waits for them, and re-layouts  3.2 us (2%)
  other arithmetic  2.09 us (2%)
  between operations  1.53 us (1%)
    ppermute x18, starting transfers between devices, ring_blocks(): lax.ppermute(block, axis, [(i, (i + k) % count) for i in range(count)])  25.5 us
    ppermute x18, waiting for transfers between devices, ring_blocks(): lax.ppermute(block, axis, [(i, (i + k) % count) for i in range(count)])  19.9 us
    pallas_call x1, Pallas kernels, backward(): pl.pallas_call(backward_kernel, grid=(slots // block,), in_specs=[pl.Bloc...  12.3 us
    pallas_call x1, Pallas kernels, attend(): pl.pallas_call(scores_kernel, grid=(lat // rows,), in_specs=[smem, smem]...  9.5 us
    all_to_all x1, starting transfers between devices, on_device(): lax.all_to_all(projected.reshape(heads, share, lat_width), 'mp', 0, 0, ti...  8.7 us
    ppermute x3, waiting for transfers between devices, on_device(): lax.ppermute(pair, 'mp', [(i, i ^ move) for i in range(heads)])  8.06 us
    pallas_call x1, Pallas kernels, make_tokens(): pl.pallas_call(token_kernel, grid=(2,), in_specs=[pl.BlockSpec(memory_spa...  7.9 us
    all_to_all x1, starting transfers between devices, on_device(): parts = lax.all_to_all(chip_grads, XY, 0, 0, tiled=True)  6.26 us
  transfers between devices with their start and end apart: 28, of which 11 were waited for; matrix products, arithmetic and copies ran while one was open for 2% of the time, Pallas kernels for 19%

profile of v4, /device:TPU:8, one launch (start us, length us, event | category | flops | bytes accessed | tf_op | source)
XLA Modules:
  0.0 138.6 jit_solution(16039580311049156246)
XLA Ops:
  0.8 5.9 %shard_map.121 = (bf16[64,512]{1,0:T(8,128)(2,1)S(1)}, bf16[64,512]{1,0:T(8,128)(2,1)S(1)}) custom-call(bf16[64,4096]{1,0:T(8,128)(2,1)} %lat_ref.1, bf16[4096,512]{1,0:T(8,128)(2,1)} %wq_ref.1, bf16[64,4096]{1,0:T(8,128)(2,1)} %cot_ref.1, bf16[512,4096]{1,0:T(8,128)(2,1)} %wo_ref.1), custom_call_target="tpu_custom_call" | custom-call | flops 536870912 | bytes 9437184 | tf_op jit(solution)/shard_map/pallas_call | solution.py:89
  6.7 1.6 %collective-permute-start.1 = (bf16[64,512]{1,0:T(8,128)(2,1)S(1)}, bf16[64,512]{1,0:T(8,128)(2,1)S(1)}, u32[]{:S(2)}, u32[]{:S(2)}) collective-permute-start(bf16[64,512]{1,0:T(8,128)(2,1)S(1)} %get-tuple-element.15.after_ref), channel_id=1, source_target_pairs={{0,16},{16,32},{32,48},{48,0},{1,17},{17,33},{33,49},{49,1},{2,18}... | collective-permute-start | bytes 196616 | tf_op jit(solution)/shard_map/ppermute | solution.py:35
  8.3 2.7 %collective-permute-start.2 = (bf16[64,512]{1,0:T(8,128)(2,1)S(1)}, bf16[64,512]{1,0:T(8,128)(2,1)S(1)}, u32[]{:S(2)}, u32[]{:S(2)}) collective-permute-start(bf16[64,512]{1,0:T(8,128)(2,1)S(1)} %get-tuple-element.15.after_ref), channel_id=1, source_target_pairs={{0,32},{16,48},{32,0},{48,16},{1,33},{17,49},{33,1},{49,17},{2,34}... | collective-permute-start | bytes 196616 | tf_op jit(solution)/shard_map/ppermute | solution.py:35
  13.9 2.8 %collective-permute-start.8 = (bf16[64,512]{1,0:T(8,128)(2,1)S(1)}, bf16[64,512]{1,0:T(8,128)(2,1)S(1)}, u32[]{:S(2)}, u32[]{:S(2)}) collective-permute-start(bf16[64,512]{1,0:T(8,128)(2,1)S(1)} %get-tuple-element.16), channel_id=1, source_target_pairs={{0,128},{64,192},{128,0},{192,64},{1,129},{65,193},{129,1},{193,65... | collective-permute-start | bytes 196616 | tf_op jit(solution)/shard_map/ppermute | solution.py:35
  20.1 3.1 %collective-permute-start.5 = (bf16[4,64,512]{2,1,0:T(8,128)(2,1)S(1)}, bf16[4,64,512]{2,1,0:T(8,128)(2,1)S(1)}, u32[]{:S(2)}, u32[]{:S(2)}) collective-permute-start(bf16[4,64,512]{2,1,0:T(8,128)(2,1)S(1)} %pad_maximum_fusion.q0_ref), channel_id=1, source_target_pairs={{0,128},{64,192},{128,0},{192,64},{1,129},{65,193},{129,1},{193,65... | collective-permute-start | bytes 786440 | tf_op jit(solution)/shard_map/ppermute | solution.py:35
  24.1 7.9 %collective-permute-done.4.q1_ref = bf16[4,64,512]{2,1,0:T(8,128)(2,1)S(1)} collective-permute-done((bf16[4,64,512]{2,1,0:T(8,128)(2,1)S(1)}, bf16[4,64,512]{2,1,0:T(8,128)(2,1)S(1)}, u32[]{:S(2)}, u32[]{:S(2)}) %collective-permute-start.4) | collective-permute-done | bytes 262176 | tf_op jit(solution)/shard_map/ppermute | solution.py:35
  34.1 7.9 %shard_map.122 = (bf16[1280,512]{1,0:T(8,128)(2,1)}, bf16[1280,512]{1,0:T(8,128)(2,1)}, bf16[1280,1024]{1,0:T(8,128)(2,1)}) custom-call(s32[2,6]{1,0:T(2,128)S(1)} %pad_add_fusion.facts_ref, f32[3,1024]{1,0:T(4,128)S(1)} %copy-done.1, bf16[640,1024]{1,0:T(8,128)(2,1)} %own_ref.1, bf16[640,1024]{1,0:T(8,128)(2,1)S(1)} %collective-permute-done.13.other_ref, ...), custom_call_target="tpu_custom_call" | custom-call | flops 2684354560 | bytes 9961472 | tf_op jit(solution)/shard_map/pallas_call | solution.py:141
  42.2 9.5 %shard_map.123 = (bf16[1024,1280]{1,0:T(8,128)(2,1)}, f32[1024,1280]{1,0:T(8,128)}, bf16[1024,640]{1,0:T(8,128)(2,1)}, f32[8,1024]{1,0:T(8,128)S(1)}, bf16[1024,1024]{1,0:T(8,128)(2,1)}) custom-call(s32[2,6]{1,0:T(2,128)S(1)} %pad_add_fusion.facts_ref, s32[3]{0:T(128)S(1)} %pad_add_fusion.2.place_ref, bf16[4,64,512]{2,1,0:T(8,128)(2,1)S(1)} %pad_maximum_fusion.q0_ref, ...), custom_call_target="tpu_custom_call" | custom-call | flops 4026531840 | bytes 15728640 | tf_op jit(solution)/shard_map/pallas_call | solution.py:250
  51.7 6.0 %all-to-all-start = ((bf16[16,64,640]{2,1,0:T(8,128)(2,1)}), bf16[16,64,640]{2,1,0:T(8,128)(2,1)S(1)}, u32[]{:S(2)}, u32[]{:S(2)}) async-start(bf16[16,64,640]{2,1,0:T(8,128)(2,1)} %bitcast.38), calls=%async_computation | async-start | bytes 2621440 | tf_op jit(solution)/shard_map/all_to_all | solution.py:483
  57.8 1.5 %collective-permute-start.14 = (f32[3,1024]{1,0:T(4,128)S(1)}, f32[3,1024]{1,0:T(4,128)S(1)}, u32[]{:S(2)}, u32[]{:S(2)}) collective-permute-start(f32[3,1024]{1,0:T(4,128)S(1)} %get-tuple-element.34), channel_id=1, source_target_pairs={{0,16},{16,32},{32,48},{48,0},{1,17},{17,33},{33,49},{49,1},{2,18}... | collective-permute-start | bytes 36872 | tf_op jit(solution)/shard_map/ppermute | solution.py:35
  60.1 2.4 %collective-permute-start.16 = (f32[3,1024]{1,0:T(4,128)S(1)}, f32[3,1024]{1,0:T(4,128)S(1)}, u32[]{:S(2)}, u32[]{:S(2)}) collective-permute-start(f32[3,1024]{1,0:T(4,128)S(1)} %get-tuple-element.34), channel_id=1, source_target_pairs={{0,48},{16,0},{32,16},{48,32},{1,49},{17,1},{33,17},{49,33},{2,50}... | collective-permute-start | bytes 36872 | tf_op jit(solution)/shard_map/ppermute | solution.py:35
  63.4 7.6 %collective-permute-done.14 = f32[3,1024]{1,0:T(4,128)S(1)} collective-permute-done((f32[3,1024]{1,0:T(4,128)S(1)}, f32[3,1024]{1,0:T(4,128)S(1)}, u32[]{:S(2)}, u32[]{:S(2)}) %collective-permute-start.14) | collective-permute-done | bytes 12320 | tf_op jit(solution)/shard_map/ppermute | solution.py:35
  71.2 1.9 %all-to-all-done.part_ref = bf16[16,64,640]{2,1,0:T(8,128)(2,1)S(1)} async-done(((bf16[16,64,640]{2,1,0:T(8,128)(2,1)}), bf16[16,64,640]{2,1,0:T(8,128)(2,1)S(1)}, u32[]{:S(2)}, u32[]{:S(2)}) %all-to-all-start) | async-done | bytes 1310752 | tf_op jit(solution)/shard_map/all_to_all | solution.py:483
  73.7 3.8 %convolution_convert_fusion.after_ref = bf16[64,4096]{1,0:T(8,128)(2,1)} fusion(bf16[64,512]{1,0:T(8,128)(2,1)S(1)} %shard_map.124, bf16[512,4096]{1,0:T(8,128)(2,1)} %wo_ref.1), kind=kOutput, calls=%fused_computation | convolution fusion | flops 268697600 | bytes 4784128 | tf_op jit(solution)/shard_map/dot_general | solution.py:489
  77.5 8.7 %all-to-all-start.1 = ((bf16[8,8,4096]{2,1,0:T(8,128)(2,1)}), bf16[8,8,4096]{2,1,0:T(8,128)(2,1)S(1)}, u32[]{:S(2)}, u32[]{:S(2)}) async-start(bf16[8,8,4096]{2,1,0:T(8,128)(2,1)} %bitcast.15), calls=%async_computation.1 | async-start | bytes 1048576 | tf_op jit(solution)/shard_map/all_to_all | solution.py:490
  86.4 2.3 %collective-permute-start.18 = (f32[6,1024]{1,0:T(8,128)S(1)}, f32[6,1024]{1,0:T(8,128)S(1)}, u32[]{:S(2)}, u32[]{:S(2)}) collective-permute-start(f32[6,1024]{1,0:T(8,128)S(1)} %get-tuple-element.36), channel_id=1, source_target_pairs={{0,128},{64,192},{128,0},{192,64},{1,129},{65,193},{129,1},{193,65... | collective-permute-start | bytes 73736 | tf_op jit(solution)/shard_map/ppermute | solution.py:35
  89.6 1.9 %collective-permute-done.17 = f32[6,1024]{1,0:T(8,128)S(1)} collective-permute-done((f32[6,1024]{1,0:T(8,128)S(1)}, f32[6,1024]{1,0:T(8,128)S(1)}, u32[]{:S(2)}, u32[]{:S(2)}) %collective-permute-start.17) | collective-permute-done | bytes 24608 | tf_op jit(solution)/shard_map/ppermute | solution.py:35
  92.7 12.3 %shard_map.125 = (bf16[16,32,1024]{2,1,0:T(8,128)(2,1)}, bf16[16,32,1024]{2,1,0:T(8,128)(2,1)}) custom-call(s32[1]{0:T(128)} %bitcast.5.core_ref, f32[4,6,1024]{2,1,0:T(8,128)S(1)} %pad_maximum_fusion.2.stat_ref, f32[8,1024]{1,0:T(8,128)S(1)} %get-tuple-element.20.own_ref, bf16[1024,1024]{1,0:T(8,128)(2,1)} %get-tuple-element.21.both_ref, ...), custom_call_target="tpu_custom_call" | custom-call | flops 5368709120 | bytes 14680064 | tf_op jit(solution)/shard_map/pallas_call | solution.py:363
  105.8 1.8 %shard_map.126 = bf16[8,4096]{1,0:T(8,128)(2,1)} custom-call(bf16[8,8,4096]{2,1,0:T(8,128)(2,1)} %copy-done.2, bf16[8,4096]{1,0:T(8,128)(2,1)} %copy-done, bf16[16,32,1024]{2,1,0:T(8,128)(2,1)} %get-tuple-element.25.after_ref.array_ref), custom_call_target="tpu_custom_call" | custom-call | flops 262144 | bytes 524288 | tf_op jit(solution)/shard_map/pallas_call | solution.py:402
  108.5 5.9 %collective-permute-start.20 = (bf16[8,4096]{1,0:T(8,128)(2,1)S(1)}, bf16[8,4096]{1,0:T(8,128)(2,1)S(1)}, u32[]{:S(2)}, u32[]{:S(2)}) collective-permute-start(bf16[8,4096]{1,0:T(8,128)(2,1)S(1)} %copy-done.4), channel_id=1, source_target_pairs={{0,4},{1,5},{2,6},{3,7},{4,0},{5,1},{6,2},{7,3},{8,12},{9,13},{10,... | collective-permute-start | bytes 196616 | tf_op jit(solution)/shard_map/ppermute | solution.py:498
  115.9 6.3 %all-to-all-start.2 = ((bf16[16,32,1024]{2,1,0:T(8,128)(2,1)}), bf16[16,32,1024]{2,1,0:T(8,128)(2,1)S(1)}, u32[]{:S(2)}, u32[]{:S(2)}) async-start(bf16[16,32,1024]{2,1,0:T(8,128)(2,1)} %add_convert_fusion), calls=%async_computation.2 | async-start | bytes 2097152 | tf_op jit(solution)/shard_map/all_to_all | solution.py:507
  123.4 3.3 %collective-permute-start.23 = (bf16[2,8,4096]{2,1,0:T(8,128)(2,1)S(1)}, bf16[2,8,4096]{2,1,0:T(8,128)(2,1)S(1)}, u32[]{:S(2)}, u32[]{:S(2)}) collective-permute-start(bf16[2,8,4096]{2,1,0:T(8,128)(2,1)S(1)} %pad_maximum_fusion.3.v0_ref), channel_id=1, source_target_pairs={{0,3},{1,2},{2,1},{3,0},{4,7},{5,6},{6,5},{7,4},{8,11},{9,10},{10,... | collective-permute-start | bytes 393224 | tf_op jit(solution)/shard_map/ppermute | solution.py:504
  128.1 6.6 %collective-permute-done.22.v2_ref = bf16[2,8,4096]{2,1,0:T(8,128)(2,1)S(1)} collective-permute-done((bf16[2,8,4096]{2,1,0:T(8,128)(2,1)S(1)}, bf16[2,8,4096]{2,1,0:T(8,128)(2,1)S(1)}, u32[]{:S(2)}, u32[]{:S(2)}) %collective-permute-start.22) | collective-permute-done | bytes 131104 | tf_op jit(solution)/shard_map/ppermute | solution.py:504
  135.5 2.2 %all-to-all-done.2 = bf16[16,32,1024]{2,1,0:T(8,128)(2,1)S(1)} async-done(((bf16[16,32,1024]{2,1,0:T(8,128)(2,1)}), bf16[16,32,1024]{2,1,0:T(8,128)(2,1)S(1)}, u32[]{:S(2)}, u32[]{:S(2)}) %all-to-all-start.2) | async-done | bytes 1048608 | tf_op jit(solution)/shard_map/all_to_all | solution.py:507
  (75 shorter events, 21.0 us)
Async XLA Ops:
  0.7 32.4 %collective-permute-start.13 = (bf16[640,1024]{1,0:T(8,128)(2,1)}, bf16[640,1024]{1,0:T(8,128)(2,1)S(1)}, u32[]{:S(2)}, u32[]{:S(2)}) collective-permute-start(bf16[640,1024]{1,0:T(8,128)(2,1)} %own_ref.1), channel_id=1, source_target_pairs={{0,8},{8,0},{1,9},{9,1},{2,10},{10,2},{3,11},{11,3},{4,12},{12,4},... | collective-permute-start | bytes 3932168 | tf_op jit(solution)/shard_map/ppermute | solution.py:461
  6.7 7.2 %collective-permute-start.1 = (bf16[64,512]{1,0:T(8,128)(2,1)S(1)}, bf16[64,512]{1,0:T(8,128)(2,1)S(1)}, u32[]{:S(2)}, u32[]{:S(2)}) collective-permute-start(bf16[64,512]{1,0:T(8,128)(2,1)S(1)} %get-tuple-element.15.after_ref), channel_id=1, source_target_pairs={{0,16},{16,32},{32,48},{48,0},{1,17},{17,33},{33,49},{49,1},{2,18}... | collective-permute-start | bytes 196616 | tf_op jit(solution)/shard_map/ppermute | solution.py:35
  8.3 8.4 %collective-permute-start.2 = (bf16[64,512]{1,0:T(8,128)(2,1)S(1)}, bf16[64,512]{1,0:T(8,128)(2,1)S(1)}, u32[]{:S(2)}, u32[]{:S(2)}) collective-permute-start(bf16[64,512]{1,0:T(8,128)(2,1)S(1)} %get-tuple-element.15.after_ref), channel_id=1, source_target_pairs={{0,32},{16,48},{32,0},{48,16},{1,33},{17,49},{33,1},{49,17},{2,34}... | collective-permute-start | bytes 196616 | tf_op jit(solution)/shard_map/ppermute | solution.py:35
  11.0 7.1 %collective-permute-start.3 = (bf16[64,512]{1,0:T(8,128)(2,1)S(1)}, bf16[64,512]{1,0:T(8,128)(2,1)S(1)}, u32[]{:S(2)}, u32[]{:S(2)}) collective-permute-start(bf16[64,512]{1,0:T(8,128)(2,1)S(1)} %get-tuple-element.15.after_ref), channel_id=1, source_target_pairs={{0,48},{16,0},{32,16},{48,32},{1,49},{17,1},{33,17},{49,33},{2,50}... | collective-permute-start | bytes 196616 | tf_op jit(solution)/shard_map/ppermute | solution.py:35
  11.7 7.3 %collective-permute-start.7 = (bf16[64,512]{1,0:T(8,128)(2,1)S(1)}, bf16[64,512]{1,0:T(8,128)(2,1)S(1)}, u32[]{:S(2)}, u32[]{:S(2)}) collective-permute-start(bf16[64,512]{1,0:T(8,128)(2,1)S(1)} %get-tuple-element.16), channel_id=1, source_target_pairs={{0,64},{64,128},{128,192},{192,0},{1,65},{65,129},{129,193},{193,1... | collective-permute-start | bytes 196616 | tf_op jit(solution)/shard_map/ppermute | solution.py:35
  13.9 6.2 %collective-permute-start.8 = (bf16[64,512]{1,0:T(8,128)(2,1)S(1)}, bf16[64,512]{1,0:T(8,128)(2,1)S(1)}, u32[]{:S(2)}, u32[]{:S(2)}) collective-permute-start(bf16[64,512]{1,0:T(8,128)(2,1)S(1)} %get-tuple-element.16), channel_id=1, source_target_pairs={{0,128},{64,192},{128,0},{192,64},{1,129},{65,193},{129,1},{193,65... | collective-permute-start | bytes 196616 | tf_op jit(solution)/shard_map/ppermute | solution.py:35
  16.7 6.5 %collective-permute-start.9 = (bf16[64,512]{1,0:T(8,128)(2,1)S(1)}, bf16[64,512]{1,0:T(8,128)(2,1)S(1)}, u32[]{:S(2)}, u32[]{:S(2)}) collective-permute-start(bf16[64,512]{1,0:T(8,128)(2,1)S(1)} %get-tuple-element.16), channel_id=1, source_target_pairs={{0,192},{64,0},{128,64},{192,128},{1,193},{65,1},{129,65},{193,129... | collective-permute-start | bytes 196616 | tf_op jit(solution)/shard_map/ppermute | solution.py:35
  18.1 13.9 %collective-permute-start.4 = (bf16[4,64,512]{2,1,0:T(8,128)(2,1)S(1)}, bf16[4,64,512]{2,1,0:T(8,128)(2,1)S(1)}, u32[]{:S(2)}, u32[]{:S(2)}) collective-permute-start(bf16[4,64,512]{2,1,0:T(8,128)(2,1)S(1)} %pad_maximum_fusion.q0_ref), channel_id=1, source_target_pairs={{0,64},{64,128},{128,192},{192,0},{1,65},{65,129},{129,193},{193,1... | collective-permute-start | bytes 786440 | tf_op jit(solution)/shard_map/ppermute | solution.py:35
  20.1 22.0 %collective-permute-start.5 = (bf16[4,64,512]{2,1,0:T(8,128)(2,1)S(1)}, bf16[4,64,512]{2,1,0:T(8,128)(2,1)S(1)}, u32[]{:S(2)}, u32[]{:S(2)}) collective-permute-start(bf16[4,64,512]{2,1,0:T(8,128)(2,1)S(1)} %pad_maximum_fusion.q0_ref), channel_id=1, source_target_pairs={{0,128},{64,192},{128,0},{192,64},{1,129},{65,193},{129,1},{193,65... | collective-permute-start | bytes 786440 | tf_op jit(solution)/shard_map/ppermute | solution.py:35
  23.1 18.9 %collective-permute-start.6 = (bf16[4,64,512]{2,1,0:T(8,128)(2,1)S(1)}, bf16[4,64,512]{2,1,0:T(8,128)(2,1)S(1)}, u32[]{:S(2)}, u32[]{:S(2)}) collective-permute-start(bf16[4,64,512]{2,1,0:T(8,128)(2,1)S(1)} %pad_maximum_fusion.q0_ref), channel_id=1, source_target_pairs={{0,192},{64,0},{128,64},{192,128},{1,193},{65,1},{129,65},{193,129... | collective-permute-start | bytes 786440 | tf_op jit(solution)/shard_map/ppermute | solution.py:35
  24.0 18.0 %collective-permute-start.10 = (bf16[4,64,512]{2,1,0:T(8,128)(2,1)S(1)}, bf16[4,64,512]{2,1,0:T(8,128)(2,1)S(1)}, u32[]{:S(2)}, u32[]{:S(2)}) collective-permute-start(bf16[4,64,512]{2,1,0:T(8,128)(2,1)S(1)} %pad_maximum_fusion.1.b0_ref), channel_id=1, source_target_pairs={{0,16},{16,32},{32,48},{48,0},{1,17},{17,33},{33,49},{49,1},{2,18}... | collective-permute-start | bytes 786440 | tf_op jit(solution)/shard_map/ppermute | solution.py:35
  32.1 10.0 %collective-permute-start.11 = (bf16[4,64,512]{2,1,0:T(8,128)(2,1)S(1)}, bf16[4,64,512]{2,1,0:T(8,128)(2,1)S(1)}, u32[]{:S(2)}, u32[]{:S(2)}) collective-permute-start(bf16[4,64,512]{2,1,0:T(8,128)(2,1)S(1)} %pad_maximum_fusion.1.b0_ref), channel_id=1, source_target_pairs={{0,32},{16,48},{32,0},{48,16},{1,33},{17,49},{33,1},{49,17},{2,34}... | collective-permute-start | bytes 786440 | tf_op jit(solution)/shard_map/ppermute | solution.py:35
  33.0 9.2 %collective-permute-start.12 = (bf16[4,64,512]{2,1,0:T(8,128)(2,1)S(1)}, bf16[4,64,512]{2,1,0:T(8,128)(2,1)S(1)}, u32[]{:S(2)}, u32[]{:S(2)}) collective-permute-start(bf16[4,64,512]{2,1,0:T(8,128)(2,1)S(1)} %pad_maximum_fusion.1.b0_ref), channel_id=1, source_target_pairs={{0,48},{16,0},{32,16},{48,32},{1,49},{17,1},{33,17},{49,33},{2,50}... | collective-permute-start | bytes 786440 | tf_op jit(solution)/shard_map/ppermute | solution.py:35
  51.7 21.4 %all-to-all-start = ((bf16[16,64,640]{2,1,0:T(8,128)(2,1)}), bf16[16,64,640]{2,1,0:T(8,128)(2,1)S(1)}, u32[]{:S(2)}, u32[]{:S(2)}) async-start(bf16[16,64,640]{2,1,0:T(8,128)(2,1)} %bitcast.38), calls=%async_computation | async-start | bytes 2621440 | tf_op jit(solution)/shard_map/all_to_all | solution.py:483
  57.8 13.3 %collective-permute-start.14 = (f32[3,1024]{1,0:T(4,128)S(1)}, f32[3,1024]{1,0:T(4,128)S(1)}, u32[]{:S(2)}, u32[]{:S(2)}) collective-permute-start(f32[3,1024]{1,0:T(4,128)S(1)} %get-tuple-element.34), channel_id=1, source_target_pairs={{0,16},{16,32},{32,48},{48,0},{1,17},{17,33},{33,49},{49,1},{2,18}... | collective-permute-start | bytes 36872 | tf_op jit(solution)/shard_map/ppermute | solution.py:35
  59.3 11.8 %collective-permute-start.15 = (f32[3,1024]{1,0:T(4,128)S(1)}, f32[3,1024]{1,0:T(4,128)S(1)}, u32[]{:S(2)}, u32[]{:S(2)}) collective-permute-start(f32[3,1024]{1,0:T(4,128)S(1)} %get-tuple-element.34), channel_id=1, source_target_pairs={{0,32},{16,48},{32,0},{48,16},{1,33},{17,49},{33,1},{49,17},{2,34}... | collective-permute-start | bytes 36872 | tf_op jit(solution)/shard_map/ppermute | solution.py:35
  60.1 11.0 %collective-permute-start.16 = (f32[3,1024]{1,0:T(4,128)S(1)}, f32[3,1024]{1,0:T(4,128)S(1)}, u32[]{:S(2)}, u32[]{:S(2)}) collective-permute-start(f32[3,1024]{1,0:T(4,128)S(1)} %get-tuple-element.34), channel_id=1, source_target_pairs={{0,48},{16,0},{32,16},{48,32},{1,49},{17,1},{33,17},{49,33},{2,50}... | collective-permute-start | bytes 36872 | tf_op jit(solution)/shard_map/ppermute | solution.py:35
  77.5 27.5 %all-to-all-start.1 = ((bf16[8,8,4096]{2,1,0:T(8,128)(2,1)}), bf16[8,8,4096]{2,1,0:T(8,128)(2,1)S(1)}, u32[]{:S(2)}, u32[]{:S(2)}) async-start(bf16[8,8,4096]{2,1,0:T(8,128)(2,1)} %bitcast.15), calls=%async_computation.1 | async-start | bytes 1048576 | tf_op jit(solution)/shard_map/all_to_all | solution.py:490
  107.6 6.8 %collective-permute-start.24 = (bf16[16,32,1024]{2,1,0:T(8,128)(2,1)}, bf16[16,32,1024]{2,1,0:T(8,128)(2,1)S(1)}, u32[]{:S(2)}, u32[]{:S(2)}) collective-permute-start(bf16[16,32,1024]{2,1,0:T(8,128)(2,1)} %shard_map.128), channel_id=1, source_target_pairs={{0,8},{8,0},{1,9},{9,1},{2,10},{10,2},{3,11},{11,3},{4,12},{12,4},... | collective-permute-start | bytes 3145736 | tf_op jit(solution)/shard_map/ppermute | solution.py:494
  108.5 13.6 %collective-permute-start.20 = (bf16[8,4096]{1,0:T(8,128)(2,1)S(1)}, bf16[8,4096]{1,0:T(8,128)(2,1)S(1)}, u32[]{:S(2)}, u32[]{:S(2)}) collective-permute-start(bf16[8,4096]{1,0:T(8,128)(2,1)S(1)} %copy-done.4), channel_id=1, source_target_pairs={{0,4},{1,5},{2,6},{3,7},{4,0},{5,1},{6,2},{7,3},{8,12},{9,13},{10,... | collective-permute-start | bytes 196616 | tf_op jit(solution)/shard_map/ppermute | solution.py:498
  115.9 21.9 %all-to-all-start.2 = ((bf16[16,32,1024]{2,1,0:T(8,128)(2,1)}), bf16[16,32,1024]{2,1,0:T(8,128)(2,1)S(1)}, u32[]{:S(2)}, u32[]{:S(2)}) async-start(bf16[16,32,1024]{2,1,0:T(8,128)(2,1)} %add_convert_fusion), calls=%async_computation.2 | async-start | bytes 2097152 | tf_op jit(solution)/shard_map/all_to_all | solution.py:507
  122.2 5.9 %collective-permute-start.21 = (bf16[2,8,4096]{2,1,0:T(8,128)(2,1)S(1)}, bf16[2,8,4096]{2,1,0:T(8,128)(2,1)S(1)}, u32[]{:S(2)}, u32[]{:S(2)}) collective-permute-start(bf16[2,8,4096]{2,1,0:T(8,128)(2,1)S(1)} %pad_maximum_fusion.3.v0_ref), channel_id=1, source_target_pairs={{0,1},{1,0},{2,3},{3,2},{4,5},{5,4},{6,7},{7,6},{8,9},{9,8},{10,11... | collective-permute-start | bytes 393224 | tf_op jit(solution)/shard_map/ppermute | solution.py:504
  122.8 11.9 %collective-permute-start.22 = (bf16[2,8,4096]{2,1,0:T(8,128)(2,1)S(1)}, bf16[2,8,4096]{2,1,0:T(8,128)(2,1)S(1)}, u32[]{:S(2)}, u32[]{:S(2)}) collective-permute-start(bf16[2,8,4096]{2,1,0:T(8,128)(2,1)S(1)} %pad_maximum_fusion.3.v0_ref), channel_id=1, source_target_pairs={{0,2},{1,3},{2,0},{3,1},{4,6},{5,7},{6,4},{7,5},{8,10},{9,11},{10,... | collective-permute-start | bytes 393224 | tf_op jit(solution)/shard_map/ppermute | solution.py:504
  123.4 11.3 %collective-permute-start.23 = (bf16[2,8,4096]{2,1,0:T(8,128)(2,1)S(1)}, bf16[2,8,4096]{2,1,0:T(8,128)(2,1)S(1)}, u32[]{:S(2)}, u32[]{:S(2)}) collective-permute-start(bf16[2,8,4096]{2,1,0:T(8,128)(2,1)S(1)} %pad_maximum_fusion.3.v0_ref), channel_id=1, source_target_pairs={{0,3},{1,2},{2,1},{3,0},{4,7},{5,6},{6,5},{7,4},{8,11},{9,10},{10,... | collective-permute-start | bytes 393224 | tf_op jit(solution)/shard_map/ppermute | solution.py:504
  (10 other events, 90.8 us)

commit v5 on v4

--- a/solution.py
+++ b/solution.py
@@ -84,7 +84,7 @@
 def make_latents(latents, w_query, cotangent, w_out):
     rows, depth = latents.shape
     width = w_query.shape[1]
-    steps = 4
+    steps = 2
     out = jax.ShapeDtypeStruct((rows, width), bf16)
     return pl.pallas_call(
         latent_kernel,
@@ -102,7 +102,7 @@
             pltpu.VMEM((rows, width), f32),
             pltpu.VMEM((rows, width), f32),
         ],
-        compiler_params=limits(24 << 20),
+        compiler_params=limits(32 << 20),
         cost_estimate=pl.CostEstimate(
             flops=4 * rows * depth * width,
             bytes_accessed=4 * (rows + width) * depth,
@@ -176,12 +176,6 @@
         out_shape=jax.ShapeDtypeStruct(array.shape, array.dtype),
         input_output_aliases={0: 0},
     )(array, after)
-
-
-def in_three(value):
-    high = value.astype(bf16).astype(f32)
-    middle = (value - high).astype(bf16).astype(f32)
-    return high, middle, value - high - middle
 
 
 def gathered(refs, here, rows):
@@ -229,12 +223,8 @@
     dprob = dot_nt(taken[:, width:], v_ref[...])
     d_ref[...] = dprob
     cross = jnp.sum(weights * dprob, axis=1, keepdims=True)
-    part_ref[:, :width] = dot_nn(rounded, v_ref[...]).astype(bf16)
+    part_ref[...] = dot_nn(rounded, v_ref[...]).astype(bf16)
     lane = lax.broadcasted_iota(jnp.int32, (rows, 128), 1)
-    packed = jnp.zeros((rows, 128), f32)
-    for index, term in enumerate(in_three(top) + in_three(total)):
-        packed = jnp.where(lane == index, term, packed)
-    part_ref[:, width:] = packed.astype(bf16)
     stat_ref[...] = jnp.where(lane == 0, top, jnp.where(lane == 1, total, cross)).T[:8]
 
 
@@ -242,7 +232,7 @@
     side, share, width = query_rings[0].shape
     lat = len(query_rings) * side * share
     slots = keys.shape[0]
-    rows = 256
+    rows = 512
     whole = lambda i: (0, 0)
     chunk = lambda i: (i, 0)
     smem = pl.BlockSpec(memory_space=pltpu.SMEM)
@@ -254,19 +244,19 @@
         out_specs=[
             pl.BlockSpec((rows, slots), chunk),
             pl.BlockSpec((rows, slots), chunk),
-            pl.BlockSpec((rows, width + 128), chunk),
+            pl.BlockSpec((rows, width), chunk),
             pl.BlockSpec((8, rows), lambda i: (0, i)),
             pl.BlockSpec((rows, 2 * width), chunk),
         ],
         out_shape=[
             pltpu.HBM((lat, slots), bf16),
             pltpu.HBM((lat, slots), f32),
-            pltpu.HBM((lat, width + 128), bf16),
+            pltpu.HBM((lat, width), bf16),
             jax.ShapeDtypeStruct((8, lat), f32),
             pltpu.HBM((lat, 2 * width), bf16),
         ],
         scratch_shapes=[pltpu.VMEM((lat, 2 * width), bf16)],
-        compiler_params=limits(40 << 20),
+        compiler_params=limits(48 << 20),
         cost_estimate=pl.CostEstimate(
             flops=6 * lat * slots * width,
             bytes_accessed=6 * lat * slots + 10 * lat * width + 4 * slots * width,
@@ -275,31 +265,53 @@
     )(facts, place, *query_rings, *back_rings, *far(keys, values))
 
 
-def combine_kernel(part_ref, after_ref, attn_ref):
-    width = attn_ref.shape[1]
-    terms = part_ref[:, :, width:].astype(f32)
-    tops = terms[:, :, 0:1] + terms[:, :, 1:2] + terms[:, :, 2:3]
-    totals = terms[:, :, 3:4] + terms[:, :, 4:5] + terms[:, :, 5:6]
-    top = jnp.max(tops, axis=0)
-    factors = jnp.exp(tops - top[None])
-    total = jnp.sum(factors * totals, axis=0)
-    summed = jnp.sum(part_ref[:, :, :width].astype(f32) * factors, axis=0)
+def combine_kernel(place_ref, part_ref, stat_ref, after_ref, attn_ref):
+    rows, width = attn_ref.shape
+    side, lat = stat_ref.shape[0], stat_ref.shape[2]
+    count = stat_ref.shape[1] - 2
+    first = (place_ref[0] * count + place_ref[1]) * rows
+    every = jnp.concatenate([stat_ref[back] for back in range(side)], axis=0)
+    mine = pltpu.roll(every, lax.rem(lat - first, lat), 1)[:, :128]
+    filler = jnp.zeros((128 - mine.shape[0], 128), f32)
+    columns = jnp.concatenate([mine, filler], axis=0).T[:rows]
+    stride = count + 2
+    tops = [
+        [columns[:, stride * x + y : stride * x + y + 1] for y in range(count)] for x in range(side)
+    ]
+    near = [functools.reduce(jnp.maximum, of_x) for of_x in tops]
+    top = functools.reduce(jnp.maximum, near)
+    total = jnp.zeros((rows, 1), f32)
+    for x in range(side):
+        at = stride * x + count
+        total += jnp.exp(near[x] - top) * columns[:, at : at + 1]
+    summed = jnp.zeros((rows, width), f32)
+    for x in range(side):
+        for y in range(count):
+            at_x = lax.rem(place_ref[0] - x + side, side)
+            at_y = lax.rem(place_ref[1] - y + count, count)
+            part = part_ref[at_x * count + at_y].astype(f32)
+            summed += part * jnp.exp(tops[x][y] - top)
     attn_ref[...] = (summed / total).astype(bf16)
 
 
-def combine(partials, after):
-    _, rows, wide = partials.shape
+def combine(place, partials, stats, after):
+    _, rows, width = partials.shape
     vmem = pl.BlockSpec(memory_space=pltpu.VMEM)
     return pl.pallas_call(
         combine_kernel,
-        in_specs=[vmem, pl.BlockSpec(memory_space=pl.ANY)],
+        in_specs=[
+            pl.BlockSpec(memory_space=pltpu.SMEM),
+            vmem,
+            vmem,
+            pl.BlockSpec(memory_space=pl.ANY),
+        ],
         out_specs=vmem,
-        out_shape=jax.ShapeDtypeStruct((rows, wide - 128), bf16),
+        out_shape=jax.ShapeDtypeStruct((rows, width), bf16),
         compiler_params=limits(24 << 20),
         cost_estimate=pl.CostEstimate(
             flops=2 * partials.size, bytes_accessed=2 * partials.size, transcendentals=rows
         ),
-    )(partials, after)
+    )(place, partials, stats, after)
 
 
 def backward_kernel(
@@ -481,11 +493,11 @@
     stats = ring_gather(jnp.concatenate([near_tops, near_sums]), "x")
 
     partials = lax.all_to_all(
-        partial.reshape(chips, rows_here, width + 128), XY, 0, 0, tiled=True
+        pass_on(partial, near_sums).reshape(chips, rows_here, width), XY, 0, 0, tiled=True
     )
     share = rows_here // heads
     lat_share = lax.dynamic_slice_in_dim(latents, lax.axis_index("mp") * share, share, 0)
-    attn_rows = combine(partials, lat_share)
+    attn_rows = combine(place, partials, stats, lat_share)
     projected = jnp.dot(attn_rows, w_out, preferred_element_type=f32).astype(bf16)
     pieces = lax.all_to_all(projected.reshape(heads, share, lat_width), "mp", 0, 0, tiled=True)
     core = lax.axis_index("core")[None].astype(jnp.int32)

time: 139 us -> 135 us (0.971)
  waiting for transfers between devices: 32.1 us -> 29.7 us
  starting transfers between devices: 57.1 us -> 55.4 us
    ppermute x18, starting transfers between devices: 25.5 us -> 28.1 us  [ring_blocks(): lax.ppermute(block, axis, [(i, (i + k) % count) for i in range(count)])]
    ppermute x18, waiting for transfers between devices: 19.9 us -> 17.7 us  [ring_blocks(): lax.ppermute(block, axis, [(i, (i + k) % count) for i in range(count)])]
    all_to_all x1, starting transfers between devices: 6.04 us -> 4.12 us  [on_device(): lax.all_to_all(pass_on(partial, near_sums).reshape(chips, rows_here, widt...]
    all_to_all x1, waiting for transfers between devices: 1.92 us -> 0.44 us  [on_device(): lax.all_to_all(pass_on(partial, near_sums).reshape(chips, rows_here, widt...]
  transfers between devices with their start and end apart: 28 -> 28, of which waited for: 11 -> 12; matrix products, arithmetic and copies ran while one was open for 2% -> 2% of each run, Pallas kernels for 19% -> 19%
where the time goes in v5:
time: 135 us
  starting transfers between devices  55.4 us (41%)
  Pallas kernels  38.5 us (29%)
  waiting for transfers between devices  29.7 us (22%)
  matrix products  3.83 us (3%)
  local copies, waits for them, and re-layouts  3.2 us (2%)
  other arithmetic  2.67 us (2%)
  between operations  1.52 us (1%)
    ppermute x18, starting transfers between devices, ring_blocks(): lax.ppermute(block, axis, [(i, (i + k) % count) for i in range(count)])  28.1 us
    ppermute x18, waiting for transfers between devices, ring_blocks(): lax.ppermute(block, axis, [(i, (i + k) % count) for i in range(count)])  17.7 us
    pallas_call x1, Pallas kernels, backward(): pl.pallas_call(backward_kernel, grid=(slots // block,), in_specs=[pl.Bloc...  12.3 us
    pallas_call x1, Pallas kernels, attend(): pl.pallas_call(scores_kernel, grid=(lat // rows,), in_specs=[smem, smem]...  9.13 us
    all_to_all x1, starting transfers between devices, on_device(): lax.all_to_all(projected.reshape(heads, share, lat_width), 'mp', 0, 0, ti...  8.6 us
    ppermute x3, waiting for transfers between devices, on_device(): lax.ppermute(pair, 'mp', [(i, i ^ move) for i in range(heads)])  8.16 us
    pallas_call x1, Pallas kernels, make_tokens(): pl.pallas_call(token_kernel, grid=(2,), in_specs=[pl.BlockSpec(memory_spa...  7.91 us
    pallas_call x1, Pallas kernels, make_latents(): pl.pallas_call(latent_kernel, grid=(steps,), in_specs=[pl.BlockSpec((rows...  5.14 us
  transfers between devices with their start and end apart: 28, of which 12 were waited for; matrix products, arithmetic and copies ran while one was open for 2% of the time, Pallas kernels for 19%

profile of v5, /device:TPU:8, one launch (start us, length us, event | category | flops | bytes accessed | tf_op | source)
XLA Modules:
  0.0 134.9 jit_solution(10827735461641460855)
XLA Ops:
  0.8 5.1 %shard_map.121 = (bf16[64,512]{1,0:T(8,128)(2,1)S(1)}, bf16[64,512]{1,0:T(8,128)(2,1)S(1)}) custom-call(bf16[64,4096]{1,0:T(8,128)(2,1)} %lat_ref.1, bf16[4096,512]{1,0:T(8,128)(2,1)} %wq_ref.1, bf16[64,4096]{1,0:T(8,128)(2,1)} %cot_ref.1, bf16[512,4096]{1,0:T(8,128)(2,1)} %wo_ref.1), custom_call_target="tpu_custom_call" | custom-call | flops 536870912 | bytes 9437184 | tf_op jit(solution)/shard_map/pallas_call | solution.py:89
  5.9 1.7 %collective-permute-start.1 = (bf16[64,512]{1,0:T(8,128)(2,1)S(1)}, bf16[64,512]{1,0:T(8,128)(2,1)S(1)}, u32[]{:S(2)}, u32[]{:S(2)}) collective-permute-start(bf16[64,512]{1,0:T(8,128)(2,1)S(1)} %get-tuple-element.15.after_ref), channel_id=1, source_target_pairs={{0,16},{16,32},{32,48},{48,0},{1,17},{17,33},{33,49},{49,1},{2,18}... | collective-permute-start | bytes 196616 | tf_op jit(solution)/shard_map/ppermute | solution.py:35
  7.6 2.7 %collective-permute-start.2 = (bf16[64,512]{1,0:T(8,128)(2,1)S(1)}, bf16[64,512]{1,0:T(8,128)(2,1)S(1)}, u32[]{:S(2)}, u32[]{:S(2)}) collective-permute-start(bf16[64,512]{1,0:T(8,128)(2,1)S(1)} %get-tuple-element.15.after_ref), channel_id=1, source_target_pairs={{0,32},{16,48},{32,0},{48,16},{1,33},{17,49},{33,1},{49,17},{2,34}... | collective-permute-start | bytes 196616 | tf_op jit(solution)/shard_map/ppermute | solution.py:35
  13.1 2.8 %collective-permute-start.8 = (bf16[64,512]{1,0:T(8,128)(2,1)S(1)}, bf16[64,512]{1,0:T(8,128)(2,1)S(1)}, u32[]{:S(2)}, u32[]{:S(2)}) collective-permute-start(bf16[64,512]{1,0:T(8,128)(2,1)S(1)} %get-tuple-element.16), channel_id=1, source_target_pairs={{0,128},{64,192},{128,0},{192,64},{1,129},{65,193},{129,1},{193,65... | collective-permute-start | bytes 196616 | tf_op jit(solution)/shard_map/ppermute | solution.py:35
  19.3 3.1 %collective-permute-start.5 = (bf16[4,64,512]{2,1,0:T(8,128)(2,1)S(1)}, bf16[4,64,512]{2,1,0:T(8,128)(2,1)S(1)}, u32[]{:S(2)}, u32[]{:S(2)}) collective-permute-start(bf16[4,64,512]{2,1,0:T(8,128)(2,1)S(1)} %pad_maximum_fusion.q0_ref), channel_id=1, source_target_pairs={{0,128},{64,192},{128,0},{192,64},{1,129},{65,193},{129,1},{193,65... | collective-permute-start | bytes 786440 | tf_op jit(solution)/shard_map/ppermute | solution.py:35
  23.4 7.9 %collective-permute-done.4.q1_ref = bf16[4,64,512]{2,1,0:T(8,128)(2,1)S(1)} collective-permute-done((bf16[4,64,512]{2,1,0:T(8,128)(2,1)S(1)}, bf16[4,64,512]{2,1,0:T(8,128)(2,1)S(1)}, u32[]{:S(2)}, u32[]{:S(2)}) %collective-permute-start.4) | collective-permute-done | bytes 262176 | tf_op jit(solution)/shard_map/ppermute | solution.py:35
  33.4 7.9 %shard_map.122 = (bf16[1280,512]{1,0:T(8,128)(2,1)}, bf16[1280,512]{1,0:T(8,128)(2,1)}, bf16[1280,1024]{1,0:T(8,128)(2,1)}) custom-call(s32[2,6]{1,0:T(2,128)S(1)} %pad_add_fusion.facts_ref, f32[3,1024]{1,0:T(4,128)S(1)} %copy-done.1, bf16[640,1024]{1,0:T(8,128)(2,1)} %own_ref.1, bf16[640,1024]{1,0:T(8,128)(2,1)S(1)} %collective-permute-done.13.other_ref, ...), custom_call_target="tpu_custom_call" | custom-call | flops 2684354560 | bytes 9961472 | tf_op jit(solution)/shard_map/pallas_call | solution.py:141
  41.5 9.1 %shard_map.123 = (bf16[1024,1280]{1,0:T(8,128)(2,1)}, f32[1024,1280]{1,0:T(8,128)}, bf16[1024,512]{1,0:T(8,128)(2,1)}, f32[8,1024]{1,0:T(8,128)S(1)}, bf16[1024,1024]{1,0:T(8,128)(2,1)}) custom-call(s32[2,6]{1,0:T(2,128)S(1)} %pad_add_fusion.facts_ref, s32[3]{0:T(128)S(1)} %pad_add_fusion.1.place_ref, bf16[4,64,512]{2,1,0:T(8,128)(2,1)S(1)} %pad_maximum_fusion.q0_ref, ...), custom_call_target="tpu_custom_call" | custom-call | flops 4026531840 | bytes 15728640 | tf_op jit(solution)/shard_map/pallas_call | solution.py:240
  51.8 3.5 %collective-permute-start.15 = (f32[3,1024]{1,0:T(4,128)S(1)}, f32[3,1024]{1,0:T(4,128)S(1)}, u32[]{:S(2)}, u32[]{:S(2)}) collective-permute-start(f32[3,1024]{1,0:T(4,128)S(1)} %get-tuple-element.34), channel_id=1, source_target_pairs={{0,32},{16,48},{32,0},{48,16},{1,33},{17,49},{33,1},{49,17},{2,34}... | collective-permute-start | bytes 36872 | tf_op jit(solution)/shard_map/ppermute | solution.py:35
  57.1 2.0 %collective-permute-done.16 = f32[3,1024]{1,0:T(4,128)S(1)} collective-permute-done((f32[3,1024]{1,0:T(4,128)S(1)}, f32[3,1024]{1,0:T(4,128)S(1)}, u32[]{:S(2)}, u32[]{:S(2)}) %collective-permute-start.16) | collective-permute-done | bytes 12320 | tf_op jit(solution)/shard_map/ppermute | solution.py:35
  59.8 4.1 %all-to-all-start = ((bf16[16,64,512]{2,1,0:T(8,128)(2,1)}), bf16[16,64,512]{2,1,0:T(8,128)(2,1)S(1)}, u32[]{:S(2)}, u32[]{:S(2)}) async-start(bf16[16,64,512]{2,1,0:T(8,128)(2,1)} %bitcast.38), calls=%async_computation | async-start | bytes 2097152 | tf_op jit(solution)/shard_map/all_to_all | solution.py:495
  65.5 2.7 %collective-permute-start.18 = (f32[6,1024]{1,0:T(8,128)S(1)}, f32[6,1024]{1,0:T(8,128)S(1)}, u32[]{:S(2)}, u32[]{:S(2)}) collective-permute-start(f32[6,1024]{1,0:T(8,128)S(1)} %get-tuple-element.36), channel_id=1, source_target_pairs={{0,128},{64,192},{128,0},{192,64},{1,129},{65,193},{129,1},{193,65... | collective-permute-start | bytes 73736 | tf_op jit(solution)/shard_map/ppermute | solution.py:35
  70.5 3.0 %collective-permute-done.17 = f32[6,1024]{1,0:T(8,128)S(1)} collective-permute-done((f32[6,1024]{1,0:T(8,128)S(1)}, f32[6,1024]{1,0:T(8,128)S(1)}, u32[]{:S(2)}, u32[]{:S(2)}) %collective-permute-start.17) | collective-permute-done | bytes 24608 | tf_op jit(solution)/shard_map/ppermute | solution.py:35
  73.5 2.1 %collective-permute-done.18 = f32[6,1024]{1,0:T(8,128)S(1)} collective-permute-done((f32[6,1024]{1,0:T(8,128)S(1)}, f32[6,1024]{1,0:T(8,128)S(1)}, u32[]{:S(2)}, u32[]{:S(2)}) %collective-permute-start.18) | collective-permute-done | bytes 24608 | tf_op jit(solution)/shard_map/ppermute | solution.py:35
  77.5 3.8 %convolution_convert_fusion.after_ref = bf16[64,4096]{1,0:T(8,128)(2,1)} fusion(bf16[64,512]{1,0:T(8,128)(2,1)S(1)} %shard_map.125, bf16[512,4096]{1,0:T(8,128)(2,1)} %wo_ref.1), kind=kOutput, calls=%fused_computation | convolution fusion | flops 268697600 | bytes 4784128 | tf_op jit(solution)/shard_map/dot_general | solution.py:501
  81.3 8.6 %all-to-all-start.1 = ((bf16[8,8,4096]{2,1,0:T(8,128)(2,1)}), bf16[8,8,4096]{2,1,0:T(8,128)(2,1)S(1)}, u32[]{:S(2)}, u32[]{:S(2)}) async-start(bf16[8,8,4096]{2,1,0:T(8,128)(2,1)} %bitcast.24), calls=%async_computation.1 | async-start | bytes 1048576 | tf_op jit(solution)/shard_map/all_to_all | solution.py:502
  89.9 12.3 %shard_map.126 = (bf16[16,32,1024]{2,1,0:T(8,128)(2,1)}, bf16[16,32,1024]{2,1,0:T(8,128)(2,1)}) custom-call(s32[1]{0:T(128)} %bitcast.3.core_ref, f32[4,6,1024]{2,1,0:T(8,128)S(1)} %pad_maximum_fusion.2.stat_ref, f32[8,1024]{1,0:T(8,128)S(1)} %get-tuple-element.20.own_ref, bf16[1024,1024]{1,0:T(8,128)(2,1)} %get-tuple-element.21.both_ref, ...), custom_call_target="tpu_custom_call" | custom-call | flops 5368709120 | bytes 14680064 | tf_op jit(solution)/shard_map/pallas_call | solution.py:375
  104.0 1.8 %shard_map.127 = bf16[8,4096]{1,0:T(8,128)(2,1)} custom-call(bf16[8,8,4096]{2,1,0:T(8,128)(2,1)} %copy-done.2, bf16[8,4096]{1,0:T(8,128)(2,1)} %copy-done, bf16[16,32,1024]{2,1,0:T(8,128)(2,1)} %get-tuple-element.25.after_ref.array_ref), custom_call_target="tpu_custom_call" | custom-call | flops 262144 | bytes 524288 | tf_op jit(solution)/shard_map/pallas_call | solution.py:414
  106.7 4.9 %collective-permute-start.20 = (bf16[8,4096]{1,0:T(8,128)(2,1)S(1)}, bf16[8,4096]{1,0:T(8,128)(2,1)S(1)}, u32[]{:S(2)}, u32[]{:S(2)}) collective-permute-start(bf16[8,4096]{1,0:T(8,128)(2,1)S(1)} %copy-done.4), channel_id=1, source_target_pairs={{0,4},{1,5},{2,6},{3,7},{4,0},{5,1},{6,2},{7,3},{8,12},{9,13},{10,... | collective-permute-start | bytes 196616 | tf_op jit(solution)/shard_map/ppermute | solution.py:510
  113.0 5.1 %all-to-all-start.2 = ((bf16[16,32,1024]{2,1,0:T(8,128)(2,1)}), bf16[16,32,1024]{2,1,0:T(8,128)(2,1)S(1)}, u32[]{:S(2)}, u32[]{:S(2)}) async-start(bf16[16,32,1024]{2,1,0:T(8,128)(2,1)} %add_convert_fusion), calls=%async_computation.2 | async-start | bytes 2097152 | tf_op jit(solution)/shard_map/all_to_all | solution.py:519
  119.4 3.3 %collective-permute-start.23 = (bf16[2,8,4096]{2,1,0:T(8,128)(2,1)S(1)}, bf16[2,8,4096]{2,1,0:T(8,128)(2,1)S(1)}, u32[]{:S(2)}, u32[]{:S(2)}) collective-permute-start(bf16[2,8,4096]{2,1,0:T(8,128)(2,1)S(1)} %pad_maximum_fusion.3.v0_ref), channel_id=1, source_target_pairs={{0,3},{1,2},{2,1},{3,0},{4,7},{5,6},{6,5},{7,4},{8,11},{9,10},{10,... | collective-permute-start | bytes 393224 | tf_op jit(solution)/shard_map/ppermute | solution.py:516
  122.6 1.6 %collective-permute-done.21.v1_ref = bf16[2,8,4096]{2,1,0:T(8,128)(2,1)S(1)} collective-permute-done((bf16[2,8,4096]{2,1,0:T(8,128)(2,1)S(1)}, bf16[2,8,4096]{2,1,0:T(8,128)(2,1)S(1)}, u32[]{:S(2)}, u32[]{:S(2)}) %collective-permute-start.21) | collective-permute-done | bytes 131104 | tf_op jit(solution)/shard_map/ppermute | solution.py:516
  124.2 6.6 %collective-permute-done.22.v2_ref = bf16[2,8,4096]{2,1,0:T(8,128)(2,1)S(1)} collective-permute-done((bf16[2,8,4096]{2,1,0:T(8,128)(2,1)S(1)}, bf16[2,8,4096]{2,1,0:T(8,128)(2,1)S(1)}, u32[]{:S(2)}, u32[]{:S(2)}) %collective-permute-start.22) | collective-permute-done | bytes 131104 | tf_op jit(solution)/shard_map/ppermute | solution.py:516
  131.6 2.4 %all-to-all-done.2 = bf16[16,32,1024]{2,1,0:T(8,128)(2,1)S(1)} async-done(((bf16[16,32,1024]{2,1,0:T(8,128)(2,1)}), bf16[16,32,1024]{2,1,0:T(8,128)(2,1)S(1)}, u32[]{:S(2)}, u32[]{:S(2)}) %all-to-all-start.2) | async-done | bytes 1048608 | tf_op jit(solution)/shard_map/all_to_all | solution.py:519
  (79 shorter events, 25.3 us)
Async XLA Ops:
  0.7 31.6 %collective-permute-start.13 = (bf16[640,1024]{1,0:T(8,128)(2,1)}, bf16[640,1024]{1,0:T(8,128)(2,1)S(1)}, u32[]{:S(2)}, u32[]{:S(2)}) collective-permute-start(bf16[640,1024]{1,0:T(8,128)(2,1)} %own_ref.1), channel_id=1, source_target_pairs={{0,8},{8,0},{1,9},{9,1},{2,10},{10,2},{3,11},{11,3},{4,12},{12,4},... | collective-permute-start | bytes 3932168 | tf_op jit(solution)/shard_map/ppermute | solution.py:473
  5.9 7.2 %collective-permute-start.1 = (bf16[64,512]{1,0:T(8,128)(2,1)S(1)}, bf16[64,512]{1,0:T(8,128)(2,1)S(1)}, u32[]{:S(2)}, u32[]{:S(2)}) collective-permute-start(bf16[64,512]{1,0:T(8,128)(2,1)S(1)} %get-tuple-element.15.after_ref), channel_id=1, source_target_pairs={{0,16},{16,32},{32,48},{48,0},{1,17},{17,33},{33,49},{49,1},{2,18}... | collective-permute-start | bytes 196616 | tf_op jit(solution)/shard_map/ppermute | solution.py:35
  7.6 8.4 %collective-permute-start.2 = (bf16[64,512]{1,0:T(8,128)(2,1)S(1)}, bf16[64,512]{1,0:T(8,128)(2,1)S(1)}, u32[]{:S(2)}, u32[]{:S(2)}) collective-permute-start(bf16[64,512]{1,0:T(8,128)(2,1)S(1)} %get-tuple-element.15.after_ref), channel_id=1, source_target_pairs={{0,32},{16,48},{32,0},{48,16},{1,33},{17,49},{33,1},{49,17},{2,34}... | collective-permute-start | bytes 196616 | tf_op jit(solution)/shard_map/ppermute | solution.py:35
  10.2 7.1 %collective-permute-start.3 = (bf16[64,512]{1,0:T(8,128)(2,1)S(1)}, bf16[64,512]{1,0:T(8,128)(2,1)S(1)}, u32[]{:S(2)}, u32[]{:S(2)}) collective-permute-start(bf16[64,512]{1,0:T(8,128)(2,1)S(1)} %get-tuple-element.15.after_ref), channel_id=1, source_target_pairs={{0,48},{16,0},{32,16},{48,32},{1,49},{17,1},{33,17},{49,33},{2,50}... | collective-permute-start | bytes 196616 | tf_op jit(solution)/shard_map/ppermute | solution.py:35
  10.9 7.3 %collective-permute-start.7 = (bf16[64,512]{1,0:T(8,128)(2,1)S(1)}, bf16[64,512]{1,0:T(8,128)(2,1)S(1)}, u32[]{:S(2)}, u32[]{:S(2)}) collective-permute-start(bf16[64,512]{1,0:T(8,128)(2,1)S(1)} %get-tuple-element.16), channel_id=1, source_target_pairs={{0,64},{64,128},{128,192},{192,0},{1,65},{65,129},{129,193},{193,1... | collective-permute-start | bytes 196616 | tf_op jit(solution)/shard_map/ppermute | solution.py:35
  13.1 6.2 %collective-permute-start.8 = (bf16[64,512]{1,0:T(8,128)(2,1)S(1)}, bf16[64,512]{1,0:T(8,128)(2,1)S(1)}, u32[]{:S(2)}, u32[]{:S(2)}) collective-permute-start(bf16[64,512]{1,0:T(8,128)(2,1)S(1)} %get-tuple-element.16), channel_id=1, source_target_pairs={{0,128},{64,192},{128,0},{192,64},{1,129},{65,193},{129,1},{193,65... | collective-permute-start | bytes 196616 | tf_op jit(solution)/shard_map/ppermute | solution.py:35
  15.9 6.5 %collective-permute-start.9 = (bf16[64,512]{1,0:T(8,128)(2,1)S(1)}, bf16[64,512]{1,0:T(8,128)(2,1)S(1)}, u32[]{:S(2)}, u32[]{:S(2)}) collective-permute-start(bf16[64,512]{1,0:T(8,128)(2,1)S(1)} %get-tuple-element.16), channel_id=1, source_target_pairs={{0,192},{64,0},{128,64},{192,128},{1,193},{65,1},{129,65},{193,129... | collective-permute-start | bytes 196616 | tf_op jit(solution)/shard_map/ppermute | solution.py:35
  17.4 13.9 %collective-permute-start.4 = (bf16[4,64,512]{2,1,0:T(8,128)(2,1)S(1)}, bf16[4,64,512]{2,1,0:T(8,128)(2,1)S(1)}, u32[]{:S(2)}, u32[]{:S(2)}) collective-permute-start(bf16[4,64,512]{2,1,0:T(8,128)(2,1)S(1)} %pad_maximum_fusion.q0_ref), channel_id=1, source_target_pairs={{0,64},{64,128},{128,192},{192,0},{1,65},{65,129},{129,193},{193,1... | collective-permute-start | bytes 786440 | tf_op jit(solution)/shard_map/ppermute | solution.py:35
  19.3 22.0 %collective-permute-start.5 = (bf16[4,64,512]{2,1,0:T(8,128)(2,1)S(1)}, bf16[4,64,512]{2,1,0:T(8,128)(2,1)S(1)}, u32[]{:S(2)}, u32[]{:S(2)}) collective-permute-start(bf16[4,64,512]{2,1,0:T(8,128)(2,1)S(1)} %pad_maximum_fusion.q0_ref), channel_id=1, source_target_pairs={{0,128},{64,192},{128,0},{192,64},{1,129},{65,193},{129,1},{193,65... | collective-permute-start | bytes 786440 | tf_op jit(solution)/shard_map/ppermute | solution.py:35
  22.4 18.9 %collective-permute-start.6 = (bf16[4,64,512]{2,1,0:T(8,128)(2,1)S(1)}, bf16[4,64,512]{2,1,0:T(8,128)(2,1)S(1)}, u32[]{:S(2)}, u32[]{:S(2)}) collective-permute-start(bf16[4,64,512]{2,1,0:T(8,128)(2,1)S(1)} %pad_maximum_fusion.q0_ref), channel_id=1, source_target_pairs={{0,192},{64,0},{128,64},{192,128},{1,193},{65,1},{129,65},{193,129... | collective-permute-start | bytes 786440 | tf_op jit(solution)/shard_map/ppermute | solution.py:35
  23.3 18.0 %collective-permute-start.10 = (bf16[4,64,512]{2,1,0:T(8,128)(2,1)S(1)}, bf16[4,64,512]{2,1,0:T(8,128)(2,1)S(1)}, u32[]{:S(2)}, u32[]{:S(2)}) collective-permute-start(bf16[4,64,512]{2,1,0:T(8,128)(2,1)S(1)} %pad_maximum_fusion.1.b0_ref), channel_id=1, source_target_pairs={{0,16},{16,32},{32,48},{48,0},{1,17},{17,33},{33,49},{49,1},{2,18}... | collective-permute-start | bytes 786440 | tf_op jit(solution)/shard_map/ppermute | solution.py:35
  31.3 10.0 %collective-permute-start.11 = (bf16[4,64,512]{2,1,0:T(8,128)(2,1)S(1)}, bf16[4,64,512]{2,1,0:T(8,128)(2,1)S(1)}, u32[]{:S(2)}, u32[]{:S(2)}) collective-permute-start(bf16[4,64,512]{2,1,0:T(8,128)(2,1)S(1)} %pad_maximum_fusion.1.b0_ref), channel_id=1, source_target_pairs={{0,32},{16,48},{32,0},{48,16},{1,33},{17,49},{33,1},{49,17},{2,34}... | collective-permute-start | bytes 786440 | tf_op jit(solution)/shard_map/ppermute | solution.py:35
  32.3 9.2 %collective-permute-start.12 = (bf16[4,64,512]{2,1,0:T(8,128)(2,1)S(1)}, bf16[4,64,512]{2,1,0:T(8,128)(2,1)S(1)}, u32[]{:S(2)}, u32[]{:S(2)}) collective-permute-start(bf16[4,64,512]{2,1,0:T(8,128)(2,1)S(1)} %pad_maximum_fusion.1.b0_ref), channel_id=1, source_target_pairs={{0,48},{16,0},{32,16},{48,32},{1,49},{17,1},{33,17},{49,33},{2,50}... | collective-permute-start | bytes 786440 | tf_op jit(solution)/shard_map/ppermute | solution.py:35
  59.8 16.3 %all-to-all-start = ((bf16[16,64,512]{2,1,0:T(8,128)(2,1)}), bf16[16,64,512]{2,1,0:T(8,128)(2,1)S(1)}, u32[]{:S(2)}, u32[]{:S(2)}) async-start(bf16[16,64,512]{2,1,0:T(8,128)(2,1)} %bitcast.38), calls=%async_computation | async-start | bytes 2097152 | tf_op jit(solution)/shard_map/all_to_all | solution.py:495
  64.0 9.6 %collective-permute-start.17 = (f32[6,1024]{1,0:T(8,128)S(1)}, f32[6,1024]{1,0:T(8,128)S(1)}, u32[]{:S(2)}, u32[]{:S(2)}) collective-permute-start(f32[6,1024]{1,0:T(8,128)S(1)} %get-tuple-element.36), channel_id=1, source_target_pairs={{0,64},{64,128},{128,192},{192,0},{1,65},{65,129},{129,193},{193,1... | collective-permute-start | bytes 73736 | tf_op jit(solution)/shard_map/ppermute | solution.py:35
  65.5 10.1 %collective-permute-start.18 = (f32[6,1024]{1,0:T(8,128)S(1)}, f32[6,1024]{1,0:T(8,128)S(1)}, u32[]{:S(2)}, u32[]{:S(2)}) collective-permute-start(f32[6,1024]{1,0:T(8,128)S(1)} %get-tuple-element.36), channel_id=1, source_target_pairs={{0,128},{64,192},{128,0},{192,64},{1,129},{65,193},{129,1},{193,65... | collective-permute-start | bytes 73736 | tf_op jit(solution)/shard_map/ppermute | solution.py:35
  68.2 7.4 %collective-permute-start.19 = (f32[6,1024]{1,0:T(8,128)S(1)}, f32[6,1024]{1,0:T(8,128)S(1)}, u32[]{:S(2)}, u32[]{:S(2)}) collective-permute-start(f32[6,1024]{1,0:T(8,128)S(1)} %get-tuple-element.36), channel_id=1, source_target_pairs={{0,192},{64,0},{128,64},{192,128},{1,193},{65,1},{129,65},{193,129... | collective-permute-start | bytes 73736 | tf_op jit(solution)/shard_map/ppermute | solution.py:35
  81.3 21.9 %all-to-all-start.1 = ((bf16[8,8,4096]{2,1,0:T(8,128)(2,1)}), bf16[8,8,4096]{2,1,0:T(8,128)(2,1)S(1)}, u32[]{:S(2)}, u32[]{:S(2)}) async-start(bf16[8,8,4096]{2,1,0:T(8,128)(2,1)} %bitcast.24), calls=%async_computation.1 | async-start | bytes 1048576 | tf_op jit(solution)/shard_map/all_to_all | solution.py:502
  105.9 5.7 %collective-permute-start.24 = (bf16[16,32,1024]{2,1,0:T(8,128)(2,1)}, bf16[16,32,1024]{2,1,0:T(8,128)(2,1)S(1)}, u32[]{:S(2)}, u32[]{:S(2)}) collective-permute-start(bf16[16,32,1024]{2,1,0:T(8,128)(2,1)} %shard_map.129), channel_id=1, source_target_pairs={{0,8},{8,0},{1,9},{9,1},{2,10},{10,2},{3,11},{11,3},{4,12},{12,4},... | collective-permute-start | bytes 3145736 | tf_op jit(solution)/shard_map/ppermute | solution.py:506
  106.7 11.4 %collective-permute-start.20 = (bf16[8,4096]{1,0:T(8,128)(2,1)S(1)}, bf16[8,4096]{1,0:T(8,128)(2,1)S(1)}, u32[]{:S(2)}, u32[]{:S(2)}) collective-permute-start(bf16[8,4096]{1,0:T(8,128)(2,1)S(1)} %copy-done.4), channel_id=1, source_target_pairs={{0,4},{1,5},{2,6},{3,7},{4,0},{5,1},{6,2},{7,3},{8,12},{9,13},{10,... | collective-permute-start | bytes 196616 | tf_op jit(solution)/shard_map/ppermute | solution.py:510
  113.0 21.0 %all-to-all-start.2 = ((bf16[16,32,1024]{2,1,0:T(8,128)(2,1)}), bf16[16,32,1024]{2,1,0:T(8,128)(2,1)S(1)}, u32[]{:S(2)}, u32[]{:S(2)}) async-start(bf16[16,32,1024]{2,1,0:T(8,128)(2,1)} %add_convert_fusion), calls=%async_computation.2 | async-start | bytes 2097152 | tf_op jit(solution)/shard_map/all_to_all | solution.py:519
  118.1 6.0 %collective-permute-start.21 = (bf16[2,8,4096]{2,1,0:T(8,128)(2,1)S(1)}, bf16[2,8,4096]{2,1,0:T(8,128)(2,1)S(1)}, u32[]{:S(2)}, u32[]{:S(2)}) collective-permute-start(bf16[2,8,4096]{2,1,0:T(8,128)(2,1)S(1)} %pad_maximum_fusion.3.v0_ref), channel_id=1, source_target_pairs={{0,1},{1,0},{2,3},{3,2},{4,5},{5,4},{6,7},{7,6},{8,9},{9,8},{10,11... | collective-permute-start | bytes 393224 | tf_op jit(solution)/shard_map/ppermute | solution.py:516
  118.8 12.0 %collective-permute-start.22 = (bf16[2,8,4096]{2,1,0:T(8,128)(2,1)S(1)}, bf16[2,8,4096]{2,1,0:T(8,128)(2,1)S(1)}, u32[]{:S(2)}, u32[]{:S(2)}) collective-permute-start(bf16[2,8,4096]{2,1,0:T(8,128)(2,1)S(1)} %pad_maximum_fusion.3.v0_ref), channel_id=1, source_target_pairs={{0,2},{1,3},{2,0},{3,1},{4,6},{5,7},{6,4},{7,5},{8,10},{9,11},{10,... | collective-permute-start | bytes 393224 | tf_op jit(solution)/shard_map/ppermute | solution.py:516
  119.4 11.4 %collective-permute-start.23 = (bf16[2,8,4096]{2,1,0:T(8,128)(2,1)S(1)}, bf16[2,8,4096]{2,1,0:T(8,128)(2,1)S(1)}, u32[]{:S(2)}, u32[]{:S(2)}) collective-permute-start(bf16[2,8,4096]{2,1,0:T(8,128)(2,1)S(1)} %pad_maximum_fusion.3.v0_ref), channel_id=1, source_target_pairs={{0,3},{1,2},{2,1},{3,0},{4,7},{5,6},{6,5},{7,4},{8,11},{9,10},{10,... | collective-permute-start | bytes 393224 | tf_op jit(solution)/shard_map/ppermute | solution.py:516
  (11 other events, 88.4 us)

commit v6 on v5

--- a/solution.py
+++ b/solution.py
@@ -265,7 +265,7 @@
     )(facts, place, *query_rings, *back_rings, *far(keys, values))
 
 
-def combine_kernel(place_ref, part_ref, stat_ref, after_ref, attn_ref):
+def combine_rows(place_ref, part_ref, stat_ref, attn_ref):
     rows, width = attn_ref.shape
     side, lat = stat_ref.shape[0], stat_ref.shape[2]
     count = stat_ref.shape[1] - 2
@@ -294,24 +294,38 @@
     attn_ref[...] = (summed / total).astype(bf16)
 
 
-def combine(place, partials, stats, after):
+def combine_kernel(place_ref, part_ref, stat_ref, w_ref, after_ref, out_ref, attn_ref):
+    @pl.when(pl.program_id(0) == 0)
+    def _():
+        combine_rows(place_ref, part_ref, stat_ref, attn_ref)
+
+    out_ref[...] = dot_nn(attn_ref[...], w_ref[...]).astype(bf16)
+
+
+def combine(place, partials, stats, w_out, after):
     _, rows, width = partials.shape
-    vmem = pl.BlockSpec(memory_space=pltpu.VMEM)
+    depth = w_out.shape[1]
+    steps = 2
     return pl.pallas_call(
         combine_kernel,
+        grid=(steps,),
         in_specs=[
             pl.BlockSpec(memory_space=pltpu.SMEM),
-            vmem,
-            vmem,
+            pl.BlockSpec(partials.shape, lambda i: (0, 0, 0)),
+            pl.BlockSpec(stats.shape, lambda i: (0, 0, 0)),
+            pl.BlockSpec((width, depth // steps), lambda i: (0, i)),
             pl.BlockSpec(memory_space=pl.ANY),
         ],
-        out_specs=vmem,
-        out_shape=jax.ShapeDtypeStruct((rows, width), bf16),
+        out_specs=pl.BlockSpec((rows, depth // steps), lambda i: (0, i)),
+        out_shape=jax.ShapeDtypeStruct((rows, depth), bf16),
+        scratch_shapes=[pltpu.VMEM((rows, width), bf16)],
         compiler_params=limits(24 << 20),
         cost_estimate=pl.CostEstimate(
-            flops=2 * partials.size, bytes_accessed=2 * partials.size, transcendentals=rows
-        ),
-    )(place, partials, stats, after)
+            flops=2 * partials.size + 2 * rows * width * depth,
+            bytes_accessed=2 * partials.size + 2 * depth * (rows + width),
+            transcendentals=rows,
+        ),
+    )(place, partials, stats, *far(w_out), after)
 
 
 def backward_kernel(
@@ -497,8 +511,7 @@
     )
     share = rows_here // heads
     lat_share = lax.dynamic_slice_in_dim(latents, lax.axis_index("mp") * share, share, 0)
-    attn_rows = combine(place, partials, stats, lat_share)
-    projected = jnp.dot(attn_rows, w_out, preferred_element_type=f32).astype(bf16)
+    projected = combine(place, partials, stats, w_out, lat_share)
     pieces = lax.all_to_all(projected.reshape(heads, share, lat_width), "mp", 0, 0, tiled=True)
     core = lax.axis_index("core")[None].astype(jnp.int32)
     keep, give = backward(core, stats, own, both, weights, dprob, normed, projected, chips)

time: 135 us -> 134 us (level)
  matrix products: 3.83 us -> 0 us
  Pallas kernels: 38.5 us -> 41.3 us
    dot_general x1 -> x0, matrix products: 3.83 us -> none  [on_device(): jnp.dot(attn_rows, w_out, preferred_element_type=f32).astype(bf16)]
    pallas_call x1, Pallas kernels: 1.41 us -> 4.18 us  [combine(): pl.pallas_call(combine_kernel, grid=(steps,), in_specs=[pl.BlockSpec(memo...]
  transfers between devices with their start and end apart: 28 -> 28, of which waited for: 12 -> 12; matrix products, arithmetic and copies ran while one was open for 2% -> 2% of each run, Pallas kernels for 19% -> 20%
where the time goes in v6:
time: 134 us
  starting transfers between devices  55.4 us (41%)
  Pallas kernels  41.3 us (31%)
  waiting for transfers between devices  29.7 us (22%)
  local copies, waits for them, and re-layouts  3.2 us (2%)
  other arithmetic  2.67 us (2%)
  between operations  1.51 us (1%)
    ppermute x18, starting transfers between devices, ring_blocks(): lax.ppermute(block, axis, [(i, (i + k) % count) for i in range(count)])  28.1 us
    ppermute x18, waiting for transfers between devices, ring_blocks(): lax.ppermute(block, axis, [(i, (i + k) % count) for i in range(count)])  17.7 us
    pallas_call x1, Pallas kernels, backward(): pl.pallas_call(backward_kernel, grid=(slots // block,), in_specs=[pl.Bloc...  12.3 us
    pallas_call x1, Pallas kernels, attend(): pl.pallas_call(scores_kernel, grid=(lat // rows,), in_specs=[smem, smem]...  9.13 us
    all_to_all x1, starting transfers between devices, on_device(): lax.all_to_all(projected.reshape(heads, share, lat_width), 'mp', 0, 0, ti...  8.59 us
    ppermute x3, waiting for transfers between devices, on_device(): lax.ppermute(pair, 'mp', [(i, i ^ move) for i in range(heads)])  8.15 us
    pallas_call x1, Pallas kernels, make_tokens(): pl.pallas_call(token_kernel, grid=(2,), in_specs=[pl.BlockSpec(memory_spa...  7.91 us
    pallas_call x1, Pallas kernels, make_latents(): pl.pallas_call(latent_kernel, grid=(steps,), in_specs=[pl.BlockSpec((rows...  5.14 us
  transfers between devices with their start and end apart: 28, of which 12 were waited for; matrix products, arithmetic and copies ran while one was open for 2% of the time, Pallas kernels for 20%

profile of v6, /device:TPU:8, one launch (start us, length us, event | category | flops | bytes accessed | tf_op | source)
XLA Modules:
  0.0 133.8 jit_solution(16438484759497013189)
XLA Ops:
  0.8 5.1 %shard_map.121 = (bf16[64,512]{1,0:T(8,128)(2,1)S(1)}, bf16[64,512]{1,0:T(8,128)(2,1)S(1)}) custom-call(bf16[64,4096]{1,0:T(8,128)(2,1)} %lat_ref.1, bf16[4096,512]{1,0:T(8,128)(2,1)} %wq_ref.1, bf16[64,4096]{1,0:T(8,128)(2,1)} %cot_ref.1, bf16[512,4096]{1,0:T(8,128)(2,1)} %w_ref.1), custom_call_target="tpu_custom_call" | custom-call | flops 536870912 | bytes 9437184 | tf_op jit(solution)/shard_map/pallas_call | solution.py:89
  5.9 1.7 %collective-permute-start.1 = (bf16[64,512]{1,0:T(8,128)(2,1)S(1)}, bf16[64,512]{1,0:T(8,128)(2,1)S(1)}, u32[]{:S(2)}, u32[]{:S(2)}) collective-permute-start(bf16[64,512]{1,0:T(8,128)(2,1)S(1)} %get-tuple-element.15.after_ref), channel_id=1, source_target_pairs={{0,16},{16,32},{32,48},{48,0},{1,17},{17,33},{33,49},{49,1},{2,18}... | collective-permute-start | bytes 196616 | tf_op jit(solution)/shard_map/ppermute | solution.py:35
  7.6 2.7 %collective-permute-start.2 = (bf16[64,512]{1,0:T(8,128)(2,1)S(1)}, bf16[64,512]{1,0:T(8,128)(2,1)S(1)}, u32[]{:S(2)}, u32[]{:S(2)}) collective-permute-start(bf16[64,512]{1,0:T(8,128)(2,1)S(1)} %get-tuple-element.15.after_ref), channel_id=1, source_target_pairs={{0,32},{16,48},{32,0},{48,16},{1,33},{17,49},{33,1},{49,17},{2,34}... | collective-permute-start | bytes 196616 | tf_op jit(solution)/shard_map/ppermute | solution.py:35
  13.1 2.8 %collective-permute-start.8 = (bf16[64,512]{1,0:T(8,128)(2,1)S(1)}, bf16[64,512]{1,0:T(8,128)(2,1)S(1)}, u32[]{:S(2)}, u32[]{:S(2)}) collective-permute-start(bf16[64,512]{1,0:T(8,128)(2,1)S(1)} %get-tuple-element.16), channel_id=1, source_target_pairs={{0,128},{64,192},{128,0},{192,64},{1,129},{65,193},{129,1},{193,65... | collective-permute-start | bytes 196616 | tf_op jit(solution)/shard_map/ppermute | solution.py:35
  19.3 3.1 %collective-permute-start.5 = (bf16[4,64,512]{2,1,0:T(8,128)(2,1)S(1)}, bf16[4,64,512]{2,1,0:T(8,128)(2,1)S(1)}, u32[]{:S(2)}, u32[]{:S(2)}) collective-permute-start(bf16[4,64,512]{2,1,0:T(8,128)(2,1)S(1)} %pad_maximum_fusion.q0_ref), channel_id=1, source_target_pairs={{0,128},{64,192},{128,0},{192,64},{1,129},{65,193},{129,1},{193,65... | collective-permute-start | bytes 786440 | tf_op jit(solution)/shard_map/ppermute | solution.py:35
  23.4 7.9 %collective-permute-done.4.q1_ref = bf16[4,64,512]{2,1,0:T(8,128)(2,1)S(1)} collective-permute-done((bf16[4,64,512]{2,1,0:T(8,128)(2,1)S(1)}, bf16[4,64,512]{2,1,0:T(8,128)(2,1)S(1)}, u32[]{:S(2)}, u32[]{:S(2)}) %collective-permute-start.4) | collective-permute-done | bytes 262176 | tf_op jit(solution)/shard_map/ppermute | solution.py:35
  33.4 7.9 %shard_map.122 = (bf16[1280,512]{1,0:T(8,128)(2,1)}, bf16[1280,512]{1,0:T(8,128)(2,1)}, bf16[1280,1024]{1,0:T(8,128)(2,1)}) custom-call(s32[2,6]{1,0:T(2,128)S(1)} %pad_add_fusion.facts_ref, f32[3,1024]{1,0:T(4,128)S(1)} %copy-done.1, bf16[640,1024]{1,0:T(8,128)(2,1)} %own_ref.1, bf16[640,1024]{1,0:T(8,128)(2,1)S(1)} %collective-permute-done.13.other_ref, ...), custom_call_target="tpu_custom_call" | custom-call | flops 2684354560 | bytes 9961472 | tf_op jit(solution)/shard_map/pallas_call | solution.py:141
  41.5 9.1 %shard_map.123 = (bf16[1024,1280]{1,0:T(8,128)(2,1)}, f32[1024,1280]{1,0:T(8,128)}, bf16[1024,512]{1,0:T(8,128)(2,1)}, f32[8,1024]{1,0:T(8,128)S(1)}, bf16[1024,1024]{1,0:T(8,128)(2,1)}) custom-call(s32[2,6]{1,0:T(2,128)S(1)} %pad_add_fusion.facts_ref, s32[3]{0:T(128)S(1)} %pad_add_fusion.1.place_ref, bf16[4,64,512]{2,1,0:T(8,128)(2,1)S(1)} %pad_maximum_fusion.q0_ref, ...), custom_call_target="tpu_custom_call" | custom-call | flops 4026531840 | bytes 15728640 | tf_op jit(solution)/shard_map/pallas_call | solution.py:240
  51.8 3.5 %collective-permute-start.15 = (f32[3,1024]{1,0:T(4,128)S(1)}, f32[3,1024]{1,0:T(4,128)S(1)}, u32[]{:S(2)}, u32[]{:S(2)}) collective-permute-start(f32[3,1024]{1,0:T(4,128)S(1)} %get-tuple-element.34), channel_id=1, source_target_pairs={{0,32},{16,48},{32,0},{48,16},{1,33},{17,49},{33,1},{49,17},{2,34}... | collective-permute-start | bytes 36872 | tf_op jit(solution)/shard_map/ppermute | solution.py:35
  57.1 2.0 %collective-permute-done.16 = f32[3,1024]{1,0:T(4,128)S(1)} collective-permute-done((f32[3,1024]{1,0:T(4,128)S(1)}, f32[3,1024]{1,0:T(4,128)S(1)}, u32[]{:S(2)}, u32[]{:S(2)}) %collective-permute-start.16) | collective-permute-done | bytes 12320 | tf_op jit(solution)/shard_map/ppermute | solution.py:35
  59.8 4.1 %all-to-all-start = ((bf16[16,64,512]{2,1,0:T(8,128)(2,1)}), bf16[16,64,512]{2,1,0:T(8,128)(2,1)S(1)}, u32[]{:S(2)}, u32[]{:S(2)}) async-start(bf16[16,64,512]{2,1,0:T(8,128)(2,1)} %bitcast.36), calls=%async_computation | async-start | bytes 2097152 | tf_op jit(solution)/shard_map/all_to_all | solution.py:509
  64.0 1.5 %collective-permute-start.17 = (f32[6,1024]{1,0:T(8,128)S(1)}, f32[6,1024]{1,0:T(8,128)S(1)}, u32[]{:S(2)}, u32[]{:S(2)}) collective-permute-start(f32[6,1024]{1,0:T(8,128)S(1)} %get-tuple-element.36), channel_id=1, source_target_pairs={{0,64},{64,128},{128,192},{192,0},{1,65},{65,129},{129,193},{193,1... | collective-permute-start | bytes 73736 | tf_op jit(solution)/shard_map/ppermute | solution.py:35
  65.5 2.7 %collective-permute-start.18 = (f32[6,1024]{1,0:T(8,128)S(1)}, f32[6,1024]{1,0:T(8,128)S(1)}, u32[]{:S(2)}, u32[]{:S(2)}) collective-permute-start(f32[6,1024]{1,0:T(8,128)S(1)} %get-tuple-element.36), channel_id=1, source_target_pairs={{0,128},{64,192},{128,0},{192,64},{1,129},{65,193},{129,1},{193,65... | collective-permute-start | bytes 73736 | tf_op jit(solution)/shard_map/ppermute | solution.py:35
  70.5 3.1 %collective-permute-done.17 = f32[6,1024]{1,0:T(8,128)S(1)} collective-permute-done((f32[6,1024]{1,0:T(8,128)S(1)}, f32[6,1024]{1,0:T(8,128)S(1)}, u32[]{:S(2)}, u32[]{:S(2)}) %collective-permute-start.17) | collective-permute-done | bytes 24608 | tf_op jit(solution)/shard_map/ppermute | solution.py:35
  73.6 2.1 %collective-permute-done.18 = f32[6,1024]{1,0:T(8,128)S(1)} collective-permute-done((f32[6,1024]{1,0:T(8,128)S(1)}, f32[6,1024]{1,0:T(8,128)S(1)}, u32[]{:S(2)}, u32[]{:S(2)}) %collective-permute-start.18) | collective-permute-done | bytes 24608 | tf_op jit(solution)/shard_map/ppermute | solution.py:35
  76.1 4.2 %shard_map.125.after_ref = bf16[64,4096]{1,0:T(8,128)(2,1)} custom-call(s32[3]{0:T(128)S(1)} %pad_add_fusion.1.place_ref, bf16[16,64,512]{2,1,0:T(8,128)(2,1)S(1)} %all-to-all-done.part_ref, f32[4,6,1024]{2,1,0:T(8,128)S(1)} %pad_maximum_fusion.2.stat_ref, bf16[512,4096]{1,0:T(8,128)(2,1)} %w_ref.1, ...), custom_call_target="tpu_custom_call" | custom-call | flops 269484032 | bytes 5767168 | tf_op jit(solution)/shard_map/pallas_call | solution.py:309
  80.3 8.6 %all-to-all-start.1 = ((bf16[8,8,4096]{2,1,0:T(8,128)(2,1)}), bf16[8,8,4096]{2,1,0:T(8,128)(2,1)S(1)}, u32[]{:S(2)}, u32[]{:S(2)}) async-start(bf16[8,8,4096]{2,1,0:T(8,128)(2,1)} %bitcast.24), calls=%async_computation.1 | async-start | bytes 1048576 | tf_op jit(solution)/shard_map/all_to_all | solution.py:515
  88.9 12.3 %shard_map.126 = (bf16[16,32,1024]{2,1,0:T(8,128)(2,1)}, bf16[16,32,1024]{2,1,0:T(8,128)(2,1)}) custom-call(s32[1]{0:T(128)} %bitcast.3.core_ref, f32[4,6,1024]{2,1,0:T(8,128)S(1)} %pad_maximum_fusion.2.stat_ref, f32[8,1024]{1,0:T(8,128)S(1)} %get-tuple-element.20.own_ref, bf16[1024,1024]{1,0:T(8,128)(2,1)} %get-tuple-element.21.both_ref, ...), custom_call_target="tpu_custom_call" | custom-call | flops 5368709120 | bytes 14680064 | tf_op jit(solution)/shard_map/pallas_call | solution.py:389
  103.0 1.8 %shard_map.127 = bf16[8,4096]{1,0:T(8,128)(2,1)} custom-call(bf16[8,8,4096]{2,1,0:T(8,128)(2,1)} %copy-done.2, bf16[8,4096]{1,0:T(8,128)(2,1)} %copy-done, bf16[16,32,1024]{2,1,0:T(8,128)(2,1)} %get-tuple-element.25.after_ref.array_ref), custom_call_target="tpu_custom_call" | custom-call | flops 262144 | bytes 524288 | tf_op jit(solution)/shard_map/pallas_call | solution.py:428
  105.6 4.9 %collective-permute-start.20 = (bf16[8,4096]{1,0:T(8,128)(2,1)S(1)}, bf16[8,4096]{1,0:T(8,128)(2,1)S(1)}, u32[]{:S(2)}, u32[]{:S(2)}) collective-permute-start(bf16[8,4096]{1,0:T(8,128)(2,1)S(1)} %copy-done.4), channel_id=1, source_target_pairs={{0,4},{1,5},{2,6},{3,7},{4,0},{5,1},{6,2},{7,3},{8,12},{9,13},{10,... | collective-permute-start | bytes 196616 | tf_op jit(solution)/shard_map/ppermute | solution.py:523
  111.9 5.1 %all-to-all-start.2 = ((bf16[16,32,1024]{2,1,0:T(8,128)(2,1)}), bf16[16,32,1024]{2,1,0:T(8,128)(2,1)S(1)}, u32[]{:S(2)}, u32[]{:S(2)}) async-start(bf16[16,32,1024]{2,1,0:T(8,128)(2,1)} %add_convert_fusion), calls=%async_computation.2 | async-start | bytes 2097152 | tf_op jit(solution)/shard_map/all_to_all | solution.py:532
  118.3 3.3 %collective-permute-start.23 = (bf16[2,8,4096]{2,1,0:T(8,128)(2,1)S(1)}, bf16[2,8,4096]{2,1,0:T(8,128)(2,1)S(1)}, u32[]{:S(2)}, u32[]{:S(2)}) collective-permute-start(bf16[2,8,4096]{2,1,0:T(8,128)(2,1)S(1)} %pad_maximum_fusion.3.v0_ref), channel_id=1, source_target_pairs={{0,3},{1,2},{2,1},{3,0},{4,7},{5,6},{6,5},{7,4},{8,11},{9,10},{10,... | collective-permute-start | bytes 393224 | tf_op jit(solution)/shard_map/ppermute | solution.py:529
  123.1 6.6 %collective-permute-done.22.v2_ref = bf16[2,8,4096]{2,1,0:T(8,128)(2,1)S(1)} collective-permute-done((bf16[2,8,4096]{2,1,0:T(8,128)(2,1)S(1)}, bf16[2,8,4096]{2,1,0:T(8,128)(2,1)S(1)}, u32[]{:S(2)}, u32[]{:S(2)}) %collective-permute-start.22) | collective-permute-done | bytes 131104 | tf_op jit(solution)/shard_map/ppermute | solution.py:529
  130.6 2.4 %all-to-all-done.2 = bf16[16,32,1024]{2,1,0:T(8,128)(2,1)S(1)} async-done(((bf16[16,32,1024]{2,1,0:T(8,128)(2,1)}), bf16[16,32,1024]{2,1,0:T(8,128)(2,1)S(1)}, u32[]{:S(2)}, u32[]{:S(2)}) %all-to-all-start.2) | async-done | bytes 1048608 | tf_op jit(solution)/shard_map/all_to_all | solution.py:532
  (78 shorter events, 23.9 us)
Async XLA Ops:
  0.7 31.6 %collective-permute-start.13 = (bf16[640,1024]{1,0:T(8,128)(2,1)}, bf16[640,1024]{1,0:T(8,128)(2,1)S(1)}, u32[]{:S(2)}, u32[]{:S(2)}) collective-permute-start(bf16[640,1024]{1,0:T(8,128)(2,1)} %own_ref.1), channel_id=1, source_target_pairs={{0,8},{8,0},{1,9},{9,1},{2,10},{10,2},{3,11},{11,3},{4,12},{12,4},... | collective-permute-start | bytes 3932168 | tf_op jit(solution)/shard_map/ppermute | solution.py:487
  5.9 7.2 %collective-permute-start.1 = (bf16[64,512]{1,0:T(8,128)(2,1)S(1)}, bf16[64,512]{1,0:T(8,128)(2,1)S(1)}, u32[]{:S(2)}, u32[]{:S(2)}) collective-permute-start(bf16[64,512]{1,0:T(8,128)(2,1)S(1)} %get-tuple-element.15.after_ref), channel_id=1, source_target_pairs={{0,16},{16,32},{32,48},{48,0},{1,17},{17,33},{33,49},{49,1},{2,18}... | collective-permute-start | bytes 196616 | tf_op jit(solution)/shard_map/ppermute | solution.py:35
  7.6 8.4 %collective-permute-start.2 = (bf16[64,512]{1,0:T(8,128)(2,1)S(1)}, bf16[64,512]{1,0:T(8,128)(2,1)S(1)}, u32[]{:S(2)}, u32[]{:S(2)}) collective-permute-start(bf16[64,512]{1,0:T(8,128)(2,1)S(1)} %get-tuple-element.15.after_ref), channel_id=1, source_target_pairs={{0,32},{16,48},{32,0},{48,16},{1,33},{17,49},{33,1},{49,17},{2,34}... | collective-permute-start | bytes 196616 | tf_op jit(solution)/shard_map/ppermute | solution.py:35
  10.2 7.1 %collective-permute-start.3 = (bf16[64,512]{1,0:T(8,128)(2,1)S(1)}, bf16[64,512]{1,0:T(8,128)(2,1)S(1)}, u32[]{:S(2)}, u32[]{:S(2)}) collective-permute-start(bf16[64,512]{1,0:T(8,128)(2,1)S(1)} %get-tuple-element.15.after_ref), channel_id=1, source_target_pairs={{0,48},{16,0},{32,16},{48,32},{1,49},{17,1},{33,17},{49,33},{2,50}... | collective-permute-start | bytes 196616 | tf_op jit(solution)/shard_map/ppermute | solution.py:35
  10.9 7.3 %collective-permute-start.7 = (bf16[64,512]{1,0:T(8,128)(2,1)S(1)}, bf16[64,512]{1,0:T(8,128)(2,1)S(1)}, u32[]{:S(2)}, u32[]{:S(2)}) collective-permute-start(bf16[64,512]{1,0:T(8,128)(2,1)S(1)} %get-tuple-element.16), channel_id=1, source_target_pairs={{0,64},{64,128},{128,192},{192,0},{1,65},{65,129},{129,193},{193,1... | collective-permute-start | bytes 196616 | tf_op jit(solution)/shard_map/ppermute | solution.py:35
  13.1 6.2 %collective-permute-start.8 = (bf16[64,512]{1,0:T(8,128)(2,1)S(1)}, bf16[64,512]{1,0:T(8,128)(2,1)S(1)}, u32[]{:S(2)}, u32[]{:S(2)}) collective-permute-start(bf16[64,512]{1,0:T(8,128)(2,1)S(1)} %get-tuple-element.16), channel_id=1, source_target_pairs={{0,128},{64,192},{128,0},{192,64},{1,129},{65,193},{129,1},{193,65... | collective-permute-start | bytes 196616 | tf_op jit(solution)/shard_map/ppermute | solution.py:35
  15.9 6.5 %collective-permute-start.9 = (bf16[64,512]{1,0:T(8,128)(2,1)S(1)}, bf16[64,512]{1,0:T(8,128)(2,1)S(1)}, u32[]{:S(2)}, u32[]{:S(2)}) collective-permute-start(bf16[64,512]{1,0:T(8,128)(2,1)S(1)} %get-tuple-element.16), channel_id=1, source_target_pairs={{0,192},{64,0},{128,64},{192,128},{1,193},{65,1},{129,65},{193,129... | collective-permute-start | bytes 196616 | tf_op jit(solution)/shard_map/ppermute | solution.py:35
  17.4 13.9 %collective-permute-start.4 = (bf16[4,64,512]{2,1,0:T(8,128)(2,1)S(1)}, bf16[4,64,512]{2,1,0:T(8,128)(2,1)S(1)}, u32[]{:S(2)}, u32[]{:S(2)}) collective-permute-start(bf16[4,64,512]{2,1,0:T(8,128)(2,1)S(1)} %pad_maximum_fusion.q0_ref), channel_id=1, source_target_pairs={{0,64},{64,128},{128,192},{192,0},{1,65},{65,129},{129,193},{193,1... | collective-permute-start | bytes 786440 | tf_op jit(solution)/shard_map/ppermute | solution.py:35
  19.3 22.0 %collective-permute-start.5 = (bf16[4,64,512]{2,1,0:T(8,128)(2,1)S(1)}, bf16[4,64,512]{2,1,0:T(8,128)(2,1)S(1)}, u32[]{:S(2)}, u32[]{:S(2)}) collective-permute-start(bf16[4,64,512]{2,1,0:T(8,128)(2,1)S(1)} %pad_maximum_fusion.q0_ref), channel_id=1, source_target_pairs={{0,128},{64,192},{128,0},{192,64},{1,129},{65,193},{129,1},{193,65... | collective-permute-start | bytes 786440 | tf_op jit(solution)/shard_map/ppermute | solution.py:35
  22.4 18.9 %collective-permute-start.6 = (bf16[4,64,512]{2,1,0:T(8,128)(2,1)S(1)}, bf16[4,64,512]{2,1,0:T(8,128)(2,1)S(1)}, u32[]{:S(2)}, u32[]{:S(2)}) collective-permute-start(bf16[4,64,512]{2,1,0:T(8,128)(2,1)S(1)} %pad_maximum_fusion.q0_ref), channel_id=1, source_target_pairs={{0,192},{64,0},{128,64},{192,128},{1,193},{65,1},{129,65},{193,129... | collective-permute-start | bytes 786440 | tf_op jit(solution)/shard_map/ppermute | solution.py:35
  23.3 18.0 %collective-permute-start.10 = (bf16[4,64,512]{2,1,0:T(8,128)(2,1)S(1)}, bf16[4,64,512]{2,1,0:T(8,128)(2,1)S(1)}, u32[]{:S(2)}, u32[]{:S(2)}) collective-permute-start(bf16[4,64,512]{2,1,0:T(8,128)(2,1)S(1)} %pad_maximum_fusion.1.b0_ref), channel_id=1, source_target_pairs={{0,16},{16,32},{32,48},{48,0},{1,17},{17,33},{33,49},{49,1},{2,18}... | collective-permute-start | bytes 786440 | tf_op jit(solution)/shard_map/ppermute | solution.py:35
  31.3 10.0 %collective-permute-start.11 = (bf16[4,64,512]{2,1,0:T(8,128)(2,1)S(1)}, bf16[4,64,512]{2,1,0:T(8,128)(2,1)S(1)}, u32[]{:S(2)}, u32[]{:S(2)}) collective-permute-start(bf16[4,64,512]{2,1,0:T(8,128)(2,1)S(1)} %pad_maximum_fusion.1.b0_ref), channel_id=1, source_target_pairs={{0,32},{16,48},{32,0},{48,16},{1,33},{17,49},{33,1},{49,17},{2,34}... | collective-permute-start | bytes 786440 | tf_op jit(solution)/shard_map/ppermute | solution.py:35
  32.3 9.2 %collective-permute-start.12 = (bf16[4,64,512]{2,1,0:T(8,128)(2,1)S(1)}, bf16[4,64,512]{2,1,0:T(8,128)(2,1)S(1)}, u32[]{:S(2)}, u32[]{:S(2)}) collective-permute-start(bf16[4,64,512]{2,1,0:T(8,128)(2,1)S(1)} %pad_maximum_fusion.1.b0_ref), channel_id=1, source_target_pairs={{0,48},{16,0},{32,16},{48,32},{1,49},{17,1},{33,17},{49,33},{2,50}... | collective-permute-start | bytes 786440 | tf_op jit(solution)/shard_map/ppermute | solution.py:35
  59.8 16.3 %all-to-all-start = ((bf16[16,64,512]{2,1,0:T(8,128)(2,1)}), bf16[16,64,512]{2,1,0:T(8,128)(2,1)S(1)}, u32[]{:S(2)}, u32[]{:S(2)}) async-start(bf16[16,64,512]{2,1,0:T(8,128)(2,1)} %bitcast.36), calls=%async_computation | async-start | bytes 2097152 | tf_op jit(solution)/shard_map/all_to_all | solution.py:509
  64.0 9.6 %collective-permute-start.17 = (f32[6,1024]{1,0:T(8,128)S(1)}, f32[6,1024]{1,0:T(8,128)S(1)}, u32[]{:S(2)}, u32[]{:S(2)}) collective-permute-start(f32[6,1024]{1,0:T(8,128)S(1)} %get-tuple-element.36), channel_id=1, source_target_pairs={{0,64},{64,128},{128,192},{192,0},{1,65},{65,129},{129,193},{193,1... | collective-permute-start | bytes 73736 | tf_op jit(solution)/shard_map/ppermute | solution.py:35
  65.5 10.1 %collective-permute-start.18 = (f32[6,1024]{1,0:T(8,128)S(1)}, f32[6,1024]{1,0:T(8,128)S(1)}, u32[]{:S(2)}, u32[]{:S(2)}) collective-permute-start(f32[6,1024]{1,0:T(8,128)S(1)} %get-tuple-element.36), channel_id=1, source_target_pairs={{0,128},{64,192},{128,0},{192,64},{1,129},{65,193},{129,1},{193,65... | collective-permute-start | bytes 73736 | tf_op jit(solution)/shard_map/ppermute | solution.py:35
  68.2 7.5 %collective-permute-start.19 = (f32[6,1024]{1,0:T(8,128)S(1)}, f32[6,1024]{1,0:T(8,128)S(1)}, u32[]{:S(2)}, u32[]{:S(2)}) collective-permute-start(f32[6,1024]{1,0:T(8,128)S(1)} %get-tuple-element.36), channel_id=1, source_target_pairs={{0,192},{64,0},{128,64},{192,128},{1,193},{65,1},{129,65},{193,129... | collective-permute-start | bytes 73736 | tf_op jit(solution)/shard_map/ppermute | solution.py:35
  80.3 21.9 %all-to-all-start.1 = ((bf16[8,8,4096]{2,1,0:T(8,128)(2,1)}), bf16[8,8,4096]{2,1,0:T(8,128)(2,1)S(1)}, u32[]{:S(2)}, u32[]{:S(2)}) async-start(bf16[8,8,4096]{2,1,0:T(8,128)(2,1)} %bitcast.24), calls=%async_computation.1 | async-start | bytes 1048576 | tf_op jit(solution)/shard_map/all_to_all | solution.py:515
  104.8 5.7 %collective-permute-start.24 = (bf16[16,32,1024]{2,1,0:T(8,128)(2,1)}, bf16[16,32,1024]{2,1,0:T(8,128)(2,1)S(1)}, u32[]{:S(2)}, u32[]{:S(2)}) collective-permute-start(bf16[16,32,1024]{2,1,0:T(8,128)(2,1)} %shard_map.129), channel_id=1, source_target_pairs={{0,8},{8,0},{1,9},{9,1},{2,10},{10,2},{3,11},{11,3},{4,12},{12,4},... | collective-permute-start | bytes 3145736 | tf_op jit(solution)/shard_map/ppermute | solution.py:519
  105.6 11.4 %collective-permute-start.20 = (bf16[8,4096]{1,0:T(8,128)(2,1)S(1)}, bf16[8,4096]{1,0:T(8,128)(2,1)S(1)}, u32[]{:S(2)}, u32[]{:S(2)}) collective-permute-start(bf16[8,4096]{1,0:T(8,128)(2,1)S(1)} %copy-done.4), channel_id=1, source_target_pairs={{0,4},{1,5},{2,6},{3,7},{4,0},{5,1},{6,2},{7,3},{8,12},{9,13},{10,... | collective-permute-start | bytes 196616 | tf_op jit(solution)/shard_map/ppermute | solution.py:523
  111.9 21.0 %all-to-all-start.2 = ((bf16[16,32,1024]{2,1,0:T(8,128)(2,1)}), bf16[16,32,1024]{2,1,0:T(8,128)(2,1)S(1)}, u32[]{:S(2)}, u32[]{:S(2)}) async-start(bf16[16,32,1024]{2,1,0:T(8,128)(2,1)} %add_convert_fusion), calls=%async_computation.2 | async-start | bytes 2097152 | tf_op jit(solution)/shard_map/all_to_all | solution.py:532
  117.1 6.0 %collective-permute-start.21 = (bf16[2,8,4096]{2,1,0:T(8,128)(2,1)S(1)}, bf16[2,8,4096]{2,1,0:T(8,128)(2,1)S(1)}, u32[]{:S(2)}, u32[]{:S(2)}) collective-permute-start(bf16[2,8,4096]{2,1,0:T(8,128)(2,1)S(1)} %pad_maximum_fusion.3.v0_ref), channel_id=1, source_target_pairs={{0,1},{1,0},{2,3},{3,2},{4,5},{5,4},{6,7},{7,6},{8,9},{9,8},{10,11... | collective-permute-start | bytes 393224 | tf_op jit(solution)/shard_map/ppermute | solution.py:529
  117.7 12.0 %collective-permute-start.22 = (bf16[2,8,4096]{2,1,0:T(8,128)(2,1)S(1)}, bf16[2,8,4096]{2,1,0:T(8,128)(2,1)S(1)}, u32[]{:S(2)}, u32[]{:S(2)}) collective-permute-start(bf16[2,8,4096]{2,1,0:T(8,128)(2,1)S(1)} %pad_maximum_fusion.3.v0_ref), channel_id=1, source_target_pairs={{0,2},{1,3},{2,0},{3,1},{4,6},{5,7},{6,4},{7,5},{8,10},{9,11},{10,... | collective-permute-start | bytes 393224 | tf_op jit(solution)/shard_map/ppermute | solution.py:529
  118.3 11.4 %collective-permute-start.23 = (bf16[2,8,4096]{2,1,0:T(8,128)(2,1)S(1)}, bf16[2,8,4096]{2,1,0:T(8,128)(2,1)S(1)}, u32[]{:S(2)}, u32[]{:S(2)}) collective-permute-start(bf16[2,8,4096]{2,1,0:T(8,128)(2,1)S(1)} %pad_maximum_fusion.3.v0_ref), channel_id=1, source_target_pairs={{0,3},{1,2},{2,1},{3,0},{4,7},{5,6},{6,5},{7,4},{8,11},{9,10},{10,... | collective-permute-start | bytes 393224 | tf_op jit(solution)/shard_map/ppermute | solution.py:529
  (11 other events, 87.3 us)
